TPU v7x, 512 devices: a whole 4x8x8 slice. The times are simulated.
512 devices in a mesh: tiles: 128 (over z, y, core), sub: 4 (over x).
Axes of the slice: x: 4, y: 8, z: 8, core: 2. Of those that a mesh axis runs over, the one named last changes fastest.
Arguments:
- state: float32 [80, 3, 8, 512, 128], P(None, None, 'sub', 'tiles'), may hold values from -6 to 6
- eastward_current: float32 [8, 128], P('sub'), may hold values from -0.3 to 0.3
- northward_current: float32 [8, 128], P('sub'), may hold values from -0.3 to 0.3
- obs_col: int32 [12, 128], replicated, may hold values from 0 to 511, as said below
- obs_row: int32 [12, 128], replicated, may hold values from 0 to 127
- obs_field: int32 [12, 128], replicated, may hold values from 0 to 2
- obs_class: int32 [12, 128], replicated, may hold values from 0 to 3
- obs_value: float32 [12, 128], replicated, may hold values from -6 to 6
- obs_error: float32 [12, 128], replicated, may hold values from 0.02 to 0.3
- vertical_table: float32 [4, 8], P(None, 'sub'), may hold values from 0.1 to 1
Outputs:
- analysis: float32 [80, 3, 8, 512, 128], P(None, None, 'sub', 'tiles')
Inputs may be any that keep to these rules, and one draw needn't show every extreme that they name: `obs_col`: the observations of one batch lie in 4 consecutive column tiles of 4 columns each, counted cyclically from a tile drawn for the batch.
All inputs are finite; a program needn't handle non-finite values.
Results may differ from a plain program's by a relative error of at most 0.00014.
Values sent between devices are 32-bit elements; how exact they have to be, the bound alone decides.
No kernel may reach another device: no remote copies, remote signals or barrier semaphores. Data moves between devices by JAX's collectives and lax.ppermute only.
A program may use at most 64 MiB of HBM per device.

v0:
```python
import jax
import jax.numpy as jnp
from jax import lax
from jax.sharding import PartitionSpec as P

RADY = 40


KAPPA_COEF = 0.2
EPSILON = 1e-05


def extended(x, sides, width):
    for axis, dim in sides:
        peers, length = (lax.axis_size(axis), x.shape[dim])
        up = [(i, (i + 1) % peers) for i in range(peers - 1)]
        down = [(j, i) for i, j in up]
        last = lax.slice_in_dim(x, length - width, length, axis=dim)
        leading = lax.slice_in_dim(x, 0, width, axis=dim)
        before = lax.ppermute(last, axis, up)
        after = lax.ppermute(leading, axis, down)
        x = jnp.concatenate([before, x, after], axis=dim)
    return x


def march_forward(widened_grid, eastward_current, northward_current):
    center = widened_grid[:, :, :, 1:-1, :]
    eastern = widened_grid[:, :, :, 2:, :]
    western = widened_grid[:, :, :, :-2, :]
    padded = jnp.pad(center, ((0, 0), (0, 0), (0, 0), (0, 0), (1, 1)))
    northern = padded[:, :, :, :, 2:]
    southern = padded[:, :, :, :, :-2]
    zonal = eastward_current[:, None, :]
    meridional = northward_current[:, None, :]
    tendency = (
        -0.5 * zonal * (eastern - western)
        - 0.5 * meridional * (northern - southern)
        + KAPPA_COEF * (eastern + western + northern + southern - 4.0 * center)
    )
    return center + tendency


def taper_weight(first_col, first_row, second_col, second_row, radius_col, radius_row):
    offset_col = (second_col - first_col).astype(jnp.float32) / radius_col
    offset_row = (second_row - first_row).astype(jnp.float32) / radius_row
    radial = 1.0 - offset_col * offset_col - offset_row * offset_row
    clipped = jnp.maximum(radial, 0.0)
    return clipped * clipped


def analysis_rows(priors, obs_value, obs_error):
    members = priors.shape[1]
    average = jnp.mean(priors, axis=1, keepdims=True)
    spread = priors - average
    variance = jnp.sum(spread * spread, axis=1, keepdims=True) / (members - 1) + EPSILON
    error_var = obs_error[:, None]
    shrink = variance / (variance + error_var)
    factor = jnp.sqrt(error_var / (variance + error_var))
    increments = shrink * (obs_value[:, None] - average) + (factor - 1.0) * spread
    regress = spread / ((members - 1) * variance)
    return (increments, regress)


def shards(
    state,
    eastward_current,
    northward_current,
    obs_col,
    obs_row,
    obs_field,
    obs_class,
    obs_value,
    obs_error,
    vertical_table,
):
    count_of_members, count_of_fields, level_count, column_count, row_count = state.shape
    batch_count, obs_count = obs_col.shape
    tile_count = lax.axis_size("tiles")
    level_parts = lax.axis_size("sub")
    first_col = lax.axis_index("tiles") * column_count
    total_cols = column_count * tile_count
    total_levels = level_count * level_parts
    radius_col = float(total_cols)
    radius_row = float(RADY)
    predicted_state = state
    for sweep_index in range(2):
        widened_grid = extended(predicted_state, (("tiles", 3),), 1)
        predicted_state = march_forward(widened_grid, eastward_current, northward_current)
    local_cols = first_col + jnp.arange(column_count, dtype=jnp.int32)
    grid_rows = jnp.arange(row_count, dtype=jnp.int32)
    position = jnp.arange(column_count * row_count, dtype=jnp.int32)
    field_axis = jnp.arange(count_of_fields, dtype=jnp.int32)
    class_axis = jnp.arange(vertical_table.shape[0], dtype=jnp.int32)
    level_surface = level_count * column_count * row_count

    def observed(flattened_state, column_ids, row_ids, field_ids):
        cubes = flattened_state.reshape(
            count_of_members, count_of_fields, level_count, column_count * row_count
        )
        target = (column_ids - first_col) * row_count + row_ids
        pick_cells = (target[:, None] == position[None, :]).astype(jnp.float32)
        choose = (field_ids[:, None] == field_axis[None, :]).astype(jnp.float32)
        all_fields = jnp.einsum("kp,mflp->kmfl", pick_cells, cubes, precision=lax.Precision.HIGHEST)
        return jnp.einsum("kmfl,kf->kml", all_fields, choose, precision=lax.Precision.HIGHEST)

    def prior_total(partial_value):
        return lax.psum(partial_value, ("tiles", "sub")) / total_levels

    def vertical_weights(class_ids):
        selector = (class_ids[:, None] == class_axis[None, :]).astype(jnp.float32)
        return jnp.dot(
            selector,
            vertical_table,
            precision=lax.Precision.HIGHEST,
            preferred_element_type=jnp.float32,
        )

    def regression(flattened_state, increments, regress, column_ids, row_ids, vertical):
        horizontal = taper_weight(
            column_ids[:, None, None],
            row_ids[:, None, None],
            local_cols[None, :, None],
            grid_rows[None, None, :],
            radius_col,
            radius_row,
        )
        weights = (vertical[:, :, None, None] * horizontal[:, None, :, :]).reshape(
            obs_count, 1, level_surface
        )
        anomaly = flattened_state - jnp.mean(flattened_state, axis=0, keepdims=True)
        covariance = jnp.dot(
            regress, anomaly, precision=lax.Precision.HIGHEST, preferred_element_type=jnp.float32
        )
        weighted = (
            covariance.reshape(obs_count, count_of_fields, level_surface) * weights
        ).reshape(obs_count, count_of_fields * level_surface)
        increment_field = lax.dot_general(
            increments,
            weighted,
            (((0,), (0,)), ((), ())),
            precision=lax.Precision.HIGHEST,
            preferred_element_type=jnp.float32,
        )
        return flattened_state + increment_field

    flattened_state = predicted_state.reshape(count_of_members, count_of_fields * level_surface)

    def step_after(which_batch, current):
        column_ids = obs_col[which_batch]
        row_ids = obs_row[which_batch]
        gathered = observed(current, column_ids, row_ids, obs_field[which_batch])
        priors_now = prior_total(jnp.sum(gathered, axis=2))
        increments, regress = analysis_rows(
            priors_now, obs_value[which_batch], obs_error[which_batch]
        )
        vertical = vertical_weights(obs_class[which_batch])
        return regression(current, increments, regress, column_ids, row_ids, vertical)

    flattened_state = lax.fori_loop(0, batch_count, step_after, flattened_state)
    return flattened_state.reshape(state.shape)


def solution(mesh):
    placed = (
        P(None, None, "sub", "tiles", None),
        P("sub", None),
        P("sub", None),
        P(),
        P(),
        P(),
        P(),
        P(),
        P(),
        P(None, "sub"),
    )
    return jax.shard_map(
        shards,
        mesh=mesh,
        in_specs=placed,
        out_specs=P(None, None, "sub", "tiles", None),
        check_vma=False,
    )
```

profile of v0, /device:TPU:1, one launch (start us, length us, event | category | flops | bytes accessed | tf_op | source)
XLA Modules:
  0.0 1336.0 jit_solution(14813947143549925154)
XLA Ops:
  0.0 1.4 copy.39
  1.4 8.8 collective-permute-start
  10.2 1.9 collective-permute-start.1
  12.2 3.1 collective-permute-done.1
  16.0 1.9 collective-permute-start.2
  17.9 4.4 collective-permute-start.3
  22.3 1.9 collective-permute-done.2
  26.8 1307.7 %while.17 = (s32[]{:T(128)}, f32[80,3072]{1,0:T(8,128)S(1)}, s32[12,128]{1,0:T(8,128)}, s32[]{:T(128)}, s32[12,128]{1,0:T(8,128)}, /*index=5*/s32[12,128]{1,0:T(...) while((s32[]{:T(128)}, f32[80,3072]{1,0:T(8,128)S(1)}, ...), condition=%wide.region_6.7_spmd.clone.clone, body=%wide.region_0.6_spmd.clone.clone.sunk | while | flops 1134324992 | bytes 24842136 | solution.py:159
  29.4 1.6 copy.56
  33.5 2.0 fusion.74
  36.4 106.0 %psum.17 = f32[128,80]{0,1:T(8,128)S(1)} all-reduce(f32[128,80]{0,1:T(8,128)S(1)} %reduce_sum.81), channel_id=1, replica_groups=mesh['tiles'=128,'sub'=4] {'tiles','sub'}, use_global_device_ids=true, to_apply=%region_2.2 | all-reduce | flops 10240 | bytes 81920 | tf_op jit(solution)/shard_map/while/body/eval_jaxpr/psum | solution.py:107
  143.2 1.4 convolution_multiply_fusion.2
  144.7 1.3 convolution_add_fusion.2
  148.6 1.6 copy.56
  152.7 2.0 fusion.74
  155.6 93.5 %psum.17 = f32[128,80]{0,1:T(8,128)S(1)} all-reduce(f32[128,80]{0,1:T(8,128)S(1)} %reduce_sum.81), channel_id=1, replica_groups=mesh['tiles'=128,'sub'=4] {'tiles','sub'}, use_global_device_ids=true, to_apply=%region_2.2 | all-reduce | flops 10240 | bytes 81920 | tf_op jit(solution)/shard_map/while/body/eval_jaxpr/psum | solution.py:107
  249.9 1.4 convolution_multiply_fusion.2
  255.3 1.6 copy.56
  259.5 2.0 fusion.74
  262.4 95.1 %psum.17 = f32[128,80]{0,1:T(8,128)S(1)} all-reduce(f32[128,80]{0,1:T(8,128)S(1)} %reduce_sum.81), channel_id=1, replica_groups=mesh['tiles'=128,'sub'=4] {'tiles','sub'}, use_global_device_ids=true, to_apply=%region_2.2 | all-reduce | flops 10240 | bytes 81920 | tf_op jit(solution)/shard_map/while/body/eval_jaxpr/psum | solution.py:107
  358.3 1.4 convolution_multiply_fusion.2
  359.8 1.4 convolution_add_fusion.2
  363.7 1.6 copy.56
  367.8 2.0 fusion.74
  370.7 94.5 %psum.17 = f32[128,80]{0,1:T(8,128)S(1)} all-reduce(f32[128,80]{0,1:T(8,128)S(1)} %reduce_sum.81), channel_id=1, replica_groups=mesh['tiles'=128,'sub'=4] {'tiles','sub'}, use_global_device_ids=true, to_apply=%region_2.2 | all-reduce | flops 10240 | bytes 81920 | tf_op jit(solution)/shard_map/while/body/eval_jaxpr/psum | solution.py:107
  466.0 1.4 convolution_multiply_fusion.2
  471.4 1.6 copy.56
  475.5 2.0 fusion.74
  478.4 95.4 %psum.17 = f32[128,80]{0,1:T(8,128)S(1)} all-reduce(f32[128,80]{0,1:T(8,128)S(1)} %reduce_sum.81), channel_id=1, replica_groups=mesh['tiles'=128,'sub'=4] {'tiles','sub'}, use_global_device_ids=true, to_apply=%region_2.2 | all-reduce | flops 10240 | bytes 81920 | tf_op jit(solution)/shard_map/while/body/eval_jaxpr/psum | solution.py:107
  574.6 1.4 convolution_multiply_fusion.2
  576.1 1.3 convolution_add_fusion.2
  580.0 1.6 copy.56
  584.1 2.0 fusion.74
  587.0 94.5 %psum.17 = f32[128,80]{0,1:T(8,128)S(1)} all-reduce(f32[128,80]{0,1:T(8,128)S(1)} %reduce_sum.81), channel_id=1, replica_groups=mesh['tiles'=128,'sub'=4] {'tiles','sub'}, use_global_device_ids=true, to_apply=%region_2.2 | all-reduce | flops 10240 | bytes 81920 | tf_op jit(solution)/shard_map/while/body/eval_jaxpr/psum | solution.py:107
  682.3 1.4 convolution_multiply_fusion.2
  683.8 1.4 convolution_add_fusion.2
  687.7 1.6 copy.56
  691.9 2.0 fusion.74
  694.8 95.4 %psum.17 = f32[128,80]{0,1:T(8,128)S(1)} all-reduce(f32[128,80]{0,1:T(8,128)S(1)} %reduce_sum.81), channel_id=1, replica_groups=mesh['tiles'=128,'sub'=4] {'tiles','sub'}, use_global_device_ids=true, to_apply=%region_2.2 | all-reduce | flops 10240 | bytes 81920 | tf_op jit(solution)/shard_map/while/body/eval_jaxpr/psum | solution.py:107
  790.9 1.4 convolution_multiply_fusion.2
  792.4 1.4 convolution_add_fusion.2
  796.3 1.6 copy.56
  800.5 2.0 fusion.74
  803.4 94.5 %psum.17 = f32[128,80]{0,1:T(8,128)S(1)} all-reduce(f32[128,80]{0,1:T(8,128)S(1)} %reduce_sum.81), channel_id=1, replica_groups=mesh['tiles'=128,'sub'=4] {'tiles','sub'}, use_global_device_ids=true, to_apply=%region_2.2 | all-reduce | flops 10240 | bytes 81920 | tf_op jit(solution)/shard_map/while/body/eval_jaxpr/psum | solution.py:107
  898.7 1.4 convolution_multiply_fusion.2
  904.1 1.6 copy.56
  908.2 2.0 fusion.74
  911.1 95.4 %psum.17 = f32[128,80]{0,1:T(8,128)S(1)} all-reduce(f32[128,80]{0,1:T(8,128)S(1)} %reduce_sum.81), channel_id=1, replica_groups=mesh['tiles'=128,'sub'=4] {'tiles','sub'}, use_global_device_ids=true, to_apply=%region_2.2 | all-reduce | flops 10240 | bytes 81920 | tf_op jit(solution)/shard_map/while/body/eval_jaxpr/psum | solution.py:107
  1007.3 1.4 convolution_multiply_fusion.2
  1008.8 1.3 convolution_add_fusion.2
  1012.7 1.6 copy.56
  1016.9 2.0 fusion.74
  1019.8 94.6 %psum.17 = f32[128,80]{0,1:T(8,128)S(1)} all-reduce(f32[128,80]{0,1:T(8,128)S(1)} %reduce_sum.81), channel_id=1, replica_groups=mesh['tiles'=128,'sub'=4] {'tiles','sub'}, use_global_device_ids=true, to_apply=%region_2.2 | all-reduce | flops 10240 | bytes 81920 | tf_op jit(solution)/shard_map/while/body/eval_jaxpr/psum | solution.py:107
  1115.2 1.4 convolution_multiply_fusion.2
  1116.7 1.4 convolution_add_fusion.2
  1120.6 1.6 copy.56
  1124.7 2.0 fusion.74
  1127.7 95.4 %psum.17 = f32[128,80]{0,1:T(8,128)S(1)} all-reduce(f32[128,80]{0,1:T(8,128)S(1)} %reduce_sum.81), channel_id=1, replica_groups=mesh['tiles'=128,'sub'=4] {'tiles','sub'}, use_global_device_ids=true, to_apply=%region_2.2 | all-reduce | flops 10240 | bytes 81920 | tf_op jit(solution)/shard_map/while/body/eval_jaxpr/psum | solution.py:107
  1223.9 1.4 convolution_multiply_fusion.2
  1229.2 1.6 copy.56
  1233.4 2.0 fusion.74
  1236.3 94.6 %psum.17 = f32[128,80]{0,1:T(8,128)S(1)} all-reduce(f32[128,80]{0,1:T(8,128)S(1)} %reduce_sum.81), channel_id=1, replica_groups=mesh['tiles'=128,'sub'=4] {'tiles','sub'}, use_global_device_ids=true, to_apply=%region_2.2 | all-reduce | flops 10240 | bytes 81920 | tf_op jit(solution)/shard_map/while/body/eval_jaxpr/psum | solution.py:107
  1331.7 1.4 convolution_multiply_fusion.2
  1334.6 1.4 reshape.274
  (296 shorter events, 90.3 us)
Async XLA Ops:
  0.0 12.2 copy-start.1
  0.0 12.2 copy-start.2
  1.4 10.8 collective-permute-start
  10.2 5.0 collective-permute-start.1
  16.0 8.3 collective-permute-start.2
  17.9 7.5 collective-permute-start.3
  26.0 0.8 copy-start.3
  31.1 112.1 %copy-start = (f32[128,3072]{1,0:T(8,128)S(1)}, f32[128,3072]{1,0:T(8,128)}, u32[]{:S(2)}) copy-start(f32[128,3072]{1,0:T(8,128)} %copy.56) | copy-start | bytes 4718596 | tf_op jit(solution)/shard_map/while
  144.7 1.4 copy-start.4
  150.3 99.7 %copy-start = (f32[128,3072]{1,0:T(8,128)S(1)}, f32[128,3072]{1,0:T(8,128)}, u32[]{:S(2)}) copy-start(f32[128,3072]{1,0:T(8,128)} %copy.56) | copy-start | bytes 4718596 | tf_op jit(solution)/shard_map/while
  251.4 1.4 copy-start.4
  257.0 101.3 %copy-start = (f32[128,3072]{1,0:T(8,128)S(1)}, f32[128,3072]{1,0:T(8,128)}, u32[]{:S(2)}) copy-start(f32[128,3072]{1,0:T(8,128)} %copy.56) | copy-start | bytes 4718596 | tf_op jit(solution)/shard_map/while
  359.7 1.4 copy-start.4
  365.4 100.6 %copy-start = (f32[128,3072]{1,0:T(8,128)S(1)}, f32[128,3072]{1,0:T(8,128)}, u32[]{:S(2)}) copy-start(f32[128,3072]{1,0:T(8,128)} %copy.56) | copy-start | bytes 4718596 | tf_op jit(solution)/shard_map/while
  467.5 1.4 copy-start.4
  473.1 101.5 %copy-start = (f32[128,3072]{1,0:T(8,128)S(1)}, f32[128,3072]{1,0:T(8,128)}, u32[]{:S(2)}) copy-start(f32[128,3072]{1,0:T(8,128)} %copy.56) | copy-start | bytes 4718596 | tf_op jit(solution)/shard_map/while
  576.1 1.4 copy-start.4
  581.7 100.6 %copy-start = (f32[128,3072]{1,0:T(8,128)S(1)}, f32[128,3072]{1,0:T(8,128)}, u32[]{:S(2)}) copy-start(f32[128,3072]{1,0:T(8,128)} %copy.56) | copy-start | bytes 4718596 | tf_op jit(solution)/shard_map/while
  683.8 1.4 copy-start.4
  689.4 101.5 %copy-start = (f32[128,3072]{1,0:T(8,128)S(1)}, f32[128,3072]{1,0:T(8,128)}, u32[]{:S(2)}) copy-start(f32[128,3072]{1,0:T(8,128)} %copy.56) | copy-start | bytes 4718596 | tf_op jit(solution)/shard_map/while
  792.4 1.4 copy-start.4
  798.0 100.7 %copy-start = (f32[128,3072]{1,0:T(8,128)S(1)}, f32[128,3072]{1,0:T(8,128)}, u32[]{:S(2)}) copy-start(f32[128,3072]{1,0:T(8,128)} %copy.56) | copy-start | bytes 4718596 | tf_op jit(solution)/shard_map/while
  900.1 1.4 copy-start.4
  905.8 101.6 %copy-start = (f32[128,3072]{1,0:T(8,128)S(1)}, f32[128,3072]{1,0:T(8,128)}, u32[]{:S(2)}) copy-start(f32[128,3072]{1,0:T(8,128)} %copy.56) | copy-start | bytes 4718596 | tf_op jit(solution)/shard_map/while
  1008.8 1.4 copy-start.4
  1014.4 100.8 %copy-start = (f32[128,3072]{1,0:T(8,128)S(1)}, f32[128,3072]{1,0:T(8,128)}, u32[]{:S(2)}) copy-start(f32[128,3072]{1,0:T(8,128)} %copy.56) | copy-start | bytes 4718596 | tf_op jit(solution)/shard_map/while
  1116.7 1.4 copy-start.4
  1122.3 101.6 %copy-start = (f32[128,3072]{1,0:T(8,128)S(1)}, f32[128,3072]{1,0:T(8,128)}, u32[]{:S(2)}) copy-start(f32[128,3072]{1,0:T(8,128)} %copy.56) | copy-start | bytes 4718596 | tf_op jit(solution)/shard_map/while
  1225.3 1.4 copy-start.4
  1230.9 100.8 %copy-start = (f32[128,3072]{1,0:T(8,128)S(1)}, f32[128,3072]{1,0:T(8,128)}, u32[]{:S(2)}) copy-start(f32[128,3072]{1,0:T(8,128)} %copy.56) | copy-start | bytes 4718596 | tf_op jit(solution)/shard_map/while
  1333.2 1.4 copy-start.4
where the time goes:
time: 1340 us
  blocking collectives  1150 us (86%)
  matrix products  60 us (4%)
  local copies, waits for them, and re-layouts  53.9 us (4%)
  other arithmetic  48.5 us (4%)
  starting transfers between devices  17 us (1%)
    psum x12, blocking collectives, prior_total(): return lax.psum(partial_value, ('tiles', 'sub')) / total_levels  1150 us
  transfers between devices with their start and end apart: 4, of which 3 were waited for; matrix products, arithmetic and copies ran while one was open for 0% of the time, Pallas kernels for 0%

commit v1 on v0

v1 whole, which is shorter than its diff:
```python
import jax
import jax.numpy as jnp
from jax import lax
from jax.experimental import pallas as pl
from jax.experimental.pallas import tpu as pltpu
from jax.sharding import Mesh, PartitionSpec as P

RADY = 40
KAPPA_COEF = 0.2
EPSILON = 1e-05
LANES = 128
TILES = ("z", "y", "core")


def forecast_kernel(
    place, present, state, left, right, east, north, meta, table, grid, mine, other, wide, sems
):
    members, fields, levels, columns, rows = state.shape
    halo = left.shape[3]
    batches = meta.shape[0]
    span = columns + 2 * halo
    groups = fields * levels
    first, core, origin = place[0], place[1], place[2]
    copies = []
    for f in range(fields):
        for l in range(levels):
            for k in range(span):
                if k < halo:
                    source = left.at[:, f, l, k, :]
                elif k < halo + columns:
                    source = state.at[:, f, l, k - halo, :]
                else:
                    source = right.at[:, f, l, k - halo - columns, :]
                slot = (f * levels + l) * span + k
                copies.append(pltpu.make_async_copy(source, wide.at[slot], sems.at[slot]))
    for copy in copies:
        copy.start()
    lane = lax.broadcasted_iota(jnp.int32, (1, rows), 1)
    for g in range(groups):
        for k in range(span):
            copies[g * span + k].wait()
        l = g % levels
        zonal = 0.5 * east[l : l + 1, :]
        meridional = 0.5 * north[l : l + 1, :]
        to_east = KAPPA_COEF - zonal
        to_west = KAPPA_COEF + zonal
        to_north = jnp.where(lane == rows - 1, 0.0, KAPPA_COEF - meridional)
        to_south = jnp.where(lane == 0, 0.0, KAPPA_COEF + meridional)

        def step(west, here, east_):
            north_ = pltpu.roll(here, rows - 1, 1)
            south_ = pltpu.roll(here, 1, 1)
            return (
                (1.0 - 4.0 * KAPPA_COEF) * here
                + to_east * east_
                + to_west * west
                + to_north * north_
                + to_south * south_
            )

        base = g * span
        once = []
        for k in range(1, span - 1):
            value = step(wide[base + k - 1], wide[base + k], wide[base + k + 1])
            if k < halo or k >= halo + columns:
                col = first + (k - halo)
                inside = jnp.logical_and(col >= 0, col < place[3])
                value = jnp.where(inside, value, 0.0)
            once.append(value)
        for k in range(columns):
            at = k + halo - 1
            grid[g * columns + k] = step(once[at - 1], once[at], once[at + 1])
    for out in (mine, other):
        out[batches * members :, :] = jnp.zeros(
            (out.shape[0] - batches * members, LANES), jnp.float32
        )
    vt = jnp.zeros((8, LANES), jnp.float32)
    spot = lax.broadcasted_iota(jnp.int32, (8, LANES), 1)
    for k in range(table.shape[0]):
        own_weight = jnp.where(core == 0, table[k, 0], table[k, 1])
        vt = jnp.where(spot == k, own_weight, vt)
    mine[batches * members : batches * members + 8, :] = jnp.where(origin == 1, vt, 0.0)

    def pick(b, carry):
        rows_of = pl.ds(pl.multiple_of(b * members, 8), members)

        @pl.when(present[b] == 0)
        def _():
            mine[rows_of, :] = jnp.zeros((members, LANES), jnp.float32)
            other[rows_of, :] = jnp.zeros((members, LANES), jnp.float32)

        @pl.when(present[b] != 0)
        def _():
            info = meta[b]
            target = info[2:3] * columns + (info[0:1] - first)
            inside = jnp.logical_and(info[0:1] >= first, info[0:1] < first + columns)
            target = jnp.where(inside, target, -1)
            target = jnp.broadcast_to(target, (members, LANES))
            index = jnp.broadcast_to(info[1:2], (members, LANES))
            for out, level in ((mine, core), (other, 1 - core)):
                total = jnp.zeros((members, LANES), jnp.float32)
                for f in range(fields):
                    for k in range(columns):
                        slab = grid[(f * levels + level) * columns + k]
                        picked = jnp.take_along_axis(slab, index, axis=1)
                        total = jnp.where(target == f * columns + k, picked, total)
                out[rows_of, :] = total

        return carry

    lax.fori_loop(0, batches, pick, 0)


def halves(x):
    high = x.astype(jnp.bfloat16)
    low = (x - high.astype(jnp.float32)).astype(jnp.bfloat16)
    return high, low


def analysis_kernel(
    place, table, info, near, far, grid, out, local, remote, spread_rows, spread_cols, vertical, profile, sems
):
    parts, length, _ = near.shape
    slabs, members, rows = grid.shape
    fields, levels, columns = out.shape[1], out.shape[2], out.shape[3]
    batches = info.shape[0]
    all_levels = 2 * parts
    total_cols = place[1].astype(jnp.float32)
    classes = table.shape[0]
    first = place[0].astype(jnp.float32)
    incoming = [
        pltpu.make_async_copy(near, remote.at[0:parts], sems.at[0]),
        pltpu.make_async_copy(far, remote.at[parts:all_levels], sems.at[1]),
        pltpu.make_async_copy(grid, local, sems.at[2]),
    ]
    for copy in incoming:
        copy.start()
    for copy in incoming:
        copy.wait()
    inverse = 1.0 / total_cols

    def update(x, weight):
        high, low = halves(x)
        covariance = jnp.dot(
            spread_cols[...],
            jnp.concatenate([high, high, low], axis=0),
            preferred_element_type=jnp.float32,
        )
        high, low = halves(covariance * weight)
        return x + jnp.dot(
            spread_rows[...],
            jnp.concatenate([high, high, low], axis=0),
            preferred_element_type=jnp.float32,
        )

    def batch(b, carry):
        mine = pl.ds(pl.multiple_of(b * members, 8), members)
        facts = info[b]
        priors = remote[0, mine, :]
        for level in range(1, all_levels):
            priors = priors + remote[level, mine, :]
        priors = priors * (1.0 / all_levels)
        average = jnp.sum(priors, axis=0, keepdims=True) * (1.0 / members)
        spread = priors - average
        variance = jnp.sum(spread * spread, axis=0, keepdims=True) / (members - 1) + EPSILON
        error = facts[4:5]
        ratio = 1.0 / (variance + error)
        shrink = variance * ratio
        factor = jnp.sqrt(error * ratio)
        increments = shrink * (facts[3:4] - average) + (factor - 1.0) * spread
        regress = spread / ((members - 1) * variance)
        high, low = halves(increments)
        spread_rows[...] = jnp.concatenate([high, low, high], axis=1)
        high = regress.astype(jnp.bfloat16).astype(jnp.float32)
        low = regress - high
        stacked = jnp.concatenate(
            [high, low, high, jnp.zeros((256 - 3 * members, LANES), jnp.float32)], axis=0
        )
        spread_cols[...] = jnp.transpose(stacked)[:, : 3 * members].astype(jnp.bfloat16)

        def column_of(k):
            return jnp.transpose(jnp.broadcast_to(facts[k : k + 1], (LANES, LANES)))

        obs_col, obs_row, obs_class = column_of(0), column_of(1), column_of(2)
        for level in range(all_levels + levels):
            if level < all_levels:
                row = remote[level, batches * members : batches * members + 8, :]
                weights = [
                    jnp.broadcast_to(row[0:1, k : k + 1], (LANES, LANES)) for k in range(classes)
                ]
            else:
                weights = [table[k, level - all_levels] for k in range(classes)]
            chosen = jnp.zeros((LANES, LANES), jnp.float32) + weights[classes - 1]
            for k in range(classes - 1):
                chosen = jnp.where(obs_class == float(k), weights[k], chosen)
            vertical[level] = chosen

        def later(c, carry):
            theirs = pl.ds(pl.multiple_of(c * members, 8), members)
            there = info[c]
            d_col = (there[0:1] - obs_col) * inverse
            d_row = (there[1:2] - obs_row) * (1.0 / RADY)
            radial = jnp.maximum(1.0 - d_col * d_col - d_row * d_row, 0.0)
            taper = radial * radial
            for level in range(0, all_levels, 2):
                x = jnp.concatenate([remote[level, theirs, :], remote[level + 1, theirs, :]], axis=1)
                weight = jnp.concatenate(
                    [taper * vertical[level], taper * vertical[level + 1]], axis=1
                )
                x = update(x, weight)
                remote[level, theirs, :] = x[:, :LANES]
                remote[level + 1, theirs, :] = x[:, LANES:]
            return carry

        lax.fori_loop(b + 1, batches, later, 0)
        lane = lax.broadcasted_iota(jnp.int32, (1, LANES), 1).astype(jnp.float32)
        d_row = (lane - obs_row) * (1.0 / RADY)
        profile[0] = 1.0 - d_row * d_row
        profile[1] = (first - obs_col) * inverse

        def cells(pair, carry):
            tapers = []
            for k in range(2):
                col = (2 * pair + k).astype(jnp.float32)
                d_col = profile[1] + col * inverse
                radial = jnp.maximum(profile[0] - d_col * d_col, 0.0)
                tapers.append(radial * radial)
            for level in range(levels):
                v = vertical[all_levels + level]
                weight = jnp.concatenate([tapers[0] * v, tapers[1] * v], axis=1)
                for f in range(fields):
                    at = (f * levels + level) * columns + 2 * pair
                    x = jnp.concatenate([local[at], local[at + 1]], axis=1)
                    x = update(x, weight)
                    local[at] = x[:, :LANES]
                    local[at + 1] = x[:, LANES:]
            return carry

        lax.fori_loop(0, columns // 2, cells, 0)
        return carry

    lax.fori_loop(0, batches, batch, 0)
    outgoing = []
    for f in range(fields):
        for level in range(levels):
            for k in range(columns):
                at = (f * levels + level) * columns + k
                outgoing.append(
                    pltpu.make_async_copy(
                        local.at[at], out.at[:, f, level, k, :], sems.at[3 + at]
                    )
                )
    for copy in outgoing:
        copy.start()
    for copy in outgoing:
        copy.wait()


def forecast(place, present, state, left, right, east, north, meta, table, length):
    members, fields, levels, columns, rows = state.shape
    halo = left.shape[3]
    slots = fields * levels * (columns + 2 * halo)
    smem = pl.BlockSpec(memory_space=pltpu.SMEM)
    vmem = pl.BlockSpec(memory_space=pltpu.VMEM)
    anywhere = pl.BlockSpec(memory_space=pl.ANY)
    picks = jax.ShapeDtypeStruct((length, LANES), jnp.float32)
    return pl.pallas_call(
        forecast_kernel,
        out_shape=(
            jax.ShapeDtypeStruct((fields * levels * columns, members, rows), jnp.float32),
            picks,
            picks,
        ),
        in_specs=[smem, smem, anywhere, anywhere, anywhere, vmem, vmem, vmem, smem],
        out_specs=(vmem, vmem, vmem),
        scratch_shapes=[
            pltpu.VMEM((slots, members, rows), jnp.float32),
            pltpu.SemaphoreType.DMA((slots,)),
        ],
        compiler_params=pltpu.CompilerParams(vmem_limit_bytes=40 * 2**20),
    )(place, present, state, left, right, east, north, meta, table)


def assimilate(place, table, info, near, far, grid, shape):
    members, fields, levels, columns, rows = shape
    smem = pl.BlockSpec(memory_space=pltpu.SMEM)
    vmem = pl.BlockSpec(memory_space=pltpu.VMEM)
    anywhere = pl.BlockSpec(memory_space=pl.ANY)
    parts, length, _ = near.shape
    return pl.pallas_call(
        analysis_kernel,
        out_shape=jax.ShapeDtypeStruct(shape, jnp.float32),
        in_specs=[smem, smem, vmem, anywhere, anywhere, anywhere],
        out_specs=anywhere,
        scratch_shapes=[
            pltpu.VMEM(grid.shape, jnp.float32),
            pltpu.VMEM((2 * parts, length, LANES), jnp.float32),
            pltpu.VMEM((members, 3 * LANES), jnp.bfloat16),
            pltpu.VMEM((LANES, 3 * members), jnp.bfloat16),
            pltpu.VMEM((2 * parts + levels, LANES, LANES), jnp.float32),
            pltpu.VMEM((2, LANES, LANES), jnp.float32),
            pltpu.SemaphoreType.DMA((3 + grid.shape[0],)),
        ],
        compiler_params=pltpu.CompilerParams(vmem_limit_bytes=40 * 2**20),
    )(place, table, info, near, far, grid)


def shards(
    state,
    eastward_current,
    northward_current,
    obs_col,
    obs_row,
    obs_field,
    obs_class,
    obs_value,
    obs_error,
    vertical_table,
):
    members, fields, levels, columns, rows = state.shape
    batches, obs = obs_col.shape
    homes = lax.axis_size("z") * lax.axis_size("y")
    tiles = homes * lax.axis_size("core")
    tile = lax.axis_index(TILES)
    core = lax.axis_index("core")
    first = tile * columns
    chunk = -(-(batches * members + 8) // (8 * homes)) * 8
    length = chunk * homes

    up = [(i, i + 1) for i in range(tiles - 1)]
    down = [(j, i) for i, j in up]
    left = lax.ppermute(state[:, :, :, columns - 2 :, :], TILES, up)
    right = lax.ppermute(state[:, :, :, :2, :], TILES, down)

    zero = jnp.zeros_like(obs_col)
    meta = jnp.stack([obs_col, obs_row, obs_field, zero, zero, zero, zero, zero], axis=1)
    inside = jnp.logical_and(obs_col >= first, obs_col < first + columns)
    present = jnp.any(inside, axis=1).astype(jnp.int32)
    origin = (tile // 2 == 0).astype(jnp.int32)
    place = jnp.stack([first, core, origin, jnp.int32(tiles * columns)]).astype(jnp.int32)
    grid, mine, other = forecast(
        place, present, state, left, right, eastward_current, northward_current, meta,
        vertical_table, length,
    )

    swap = [(0, 1), (1, 0)]
    mine = mine + lax.ppermute(other, "core", swap)
    mine = lax.all_to_all(mine.reshape(homes, chunk, LANES), ("z", "y"), 0, 0, tiled=True)
    mine = jnp.sum(mine, axis=0)
    mine = lax.all_to_all(
        jnp.broadcast_to(mine[None], (homes, chunk, LANES)), ("z", "y"), 0, 0, tiled=True
    )
    mine = mine.reshape(length, LANES)
    near = lax.all_gather(mine, "x")
    far = lax.ppermute(near, "core", swap)

    as_float = [v.astype(jnp.float32) for v in (obs_col, obs_row, obs_class)]
    blank = jnp.zeros_like(obs_value)
    info = jnp.stack([*as_float, obs_value, obs_error, blank, blank, blank], axis=1)
    where = jnp.stack([first, jnp.int32(tiles * columns)]).astype(jnp.int32)
    return assimilate(where, vertical_table, info, near, far, grid, state.shape)


def solution(mesh):
    fine = Mesh(mesh.devices.reshape(8, 8, 2, 4), ("z", "y", "core", "x"))
    state = P(None, None, "x", TILES, None)
    placed = (
        state,
        P("x", None),
        P("x", None),
        P(),
        P(),
        P(),
        P(),
        P(),
        P(),
        P(None, "x"),
    )
    return jax.shard_map(shards, mesh=fine, in_specs=placed, out_specs=state, check_vma=False)
```

time: 1340 us -> 207 us (0.15)
  blocking collectives: 1150 us -> 54.7 us
  Pallas kernels: 0 us -> 73.3 us
  matrix products: 60 us -> 0 us
  other arithmetic: 48.5 us -> 1.11 us
  local copies, waits for them, and re-layouts: 53.9 us -> 7.68 us
  waiting for transfers between devices: 6.19 us -> 40.4 us
  between operations: 0.14 us -> 13.7 us
    psum x12 -> x0, blocking collectives: 1150 us -> none  [prior_total(): return lax.psum(partial_value, ('tiles', 'sub')) / total_levels]
    pallas_call x0 -> x2, Pallas kernels: none -> 73.3 us  [the longest x1 68.5 us: assimilate(): pl.pallas_call(analysis_kernel, out_shape=jax.ShapeDtypeStruct(shape, jnp...]
    dot_general x48 -> x0, matrix products: 60 us -> none  [the longest x12 24.1 us: observed(): jnp.einsum('kp,mflp->kmfl', pick_cells, cubes, precision=lax.Precision.HI...]
    all_to_all x0 -> x2, blocking collectives: none -> 54.7 us  [the longest x1 31.8 us: shards(): lax.all_to_all(mine.reshape(homes, chunk, LANES), ('z', 'y'), 0, 0, tiled...]
    all_gather x0 -> x1, waiting for transfers between devices: none -> 33 us  [shards(): near = lax.all_gather(mine, 'x')]
    mul x24 -> x0, local copies, waits for them, and re-layouts: 20.7 us -> none  [regression(): covariance.reshape(obs_count, count_of_fields, level_surface) * weights]
    add x26 -> x1, other arithmetic: 16.2 us -> 0.05 us  [shards(): mine = mine + lax.ppermute(other, 'core', swap)]
  transfers between devices with their start and end apart: 4 -> 5, of which waited for: 3 -> 4; matrix products, arithmetic and copies ran while one was open for 0% -> 2% of each run, Pallas kernels for 0% -> 0%
where the time goes in v1:
time: 207 us; the launch traced here: 206 us
  Pallas kernels  73.3 us (35%)
  blocking collectives  54.7 us (26%)
  waiting for transfers between devices  40.4 us (20%)
  starting transfers between devices  15.2 us (7%)
  between operations  13.7 us (7%)
  local copies, waits for them, and re-layouts  7.68 us (4%)
    pallas_call x1, Pallas kernels, assimilate(): pl.pallas_call(analysis_kernel, out_shape=jax.ShapeDtypeStruct(shape, jnp...  68.5 us
    all_gather x1, waiting for transfers between devices, shards(): near = lax.all_gather(mine, 'x')  33 us
    all_to_all x1, blocking collectives, shards(): lax.all_to_all(mine.reshape(homes, chunk, LANES), ('z', 'y'), 0, 0, tiled...  31.8 us
    all_to_all x1, blocking collectives, shards(): lax.all_to_all(jnp.broadcast_to(mine[None], (homes, chunk, LANES)), ('z',...  22.9 us
    ppermute x1, starting transfers between devices, shards(): right = lax.ppermute(state[:, :, :, :2, :], TILES, down)  8.79 us
    pallas_call x1, Pallas kernels, forecast(): pl.pallas_call(forecast_kernel, out_shape=(jax.ShapeDtypeStruct((fields *...  4.72 us
  transfers between devices with their start and end apart: 5, of which 4 were waited for; matrix products, arithmetic and copies ran while one was open for 2% of the time, Pallas kernels for 0%

profile of v1, /device:TPU:1, one launch (start us, length us, event | category | flops | bytes accessed | tf_op | source)
XLA Modules:
  0.0 206.0 jit_solution(1870609686143060848)
XLA Ops:
  6.5 0.0 copy-start
  6.5 0.0 copy-start.5
  6.5 0.0 copy-start.4
  6.5 0.0 all-gather.2.cloned.1.call-start
  6.5 2.0 fusion
  8.6 8.8 %collective-permute-start.1 = (f32[80,3,2,2,128]{4,3,2,1,0:T(2,128)S(1)}, f32[80,3,2,2,128]{4,3,2,1,0:T(2,128)S(1)}, u32[]{:S(2)}, u32[]{:S(2)}) collective-permute-start(f32[80,3,2,2,128]{4,3,2,1,0:T(2,128)S(1)} %get-tuple-element.11), channel_id=1, source_target_pairs={{4,0},{8,4},{12,8},{16,12},{20,16},{24,20},{28,24},{32,28},{36,32}... | collective-permute-start | bytes 1474568 | tf_op jit(solution)/shard_map/ppermute | solution.py:333
  17.3 1.9 collective-permute-start
  19.3 0.7 stack.68
  20.0 0.8 and_reduce_fusion
  20.8 0.8 copy.14.table
  21.6 0.7 stack.70
  22.3 0.7 stack.69
  23.0 0.1 stack.72.meta
  23.1 0.1 pad_add_fusion.1.place
  23.2 0.0 collective-permute-done.1.right
  23.2 1.9 collective-permute-done.left
  25.0 0.0 copy-done
  25.0 0.0 copy-done.5
  25.0 0.0 copy-done.4
  25.0 4.7 %shard_map.100 = (f32[24,80,128]{2,1,0:T(8,128)S(1)}, f32[1024,128]{1,0:T(8,128)S(1)}, f32[1024,128]{1,0:T(8,128)S(1)}) custom-call(s32[4]{0:T(128)S(1)} %pad_add_fusion.1.place, s32[12]{0:T(128)S(1)} %convert_element_type.16.present, f32[80,3,2,4,128]{4,3,2,1,0:T(4,128)S(1)} %copy-done, f32[80,3,2,2,128]{4,3,2,1,0:T(2,128)S(1)} %collective-permute-done.left, ...), custom_call_target="tpu_custom_call" | custom-call | tf_op jit(solution)/shard_map/pallas_call | solution.py:267
  29.8 0.0 copy-start.2
  29.8 0.9 copy-done.2
  30.7 1.9 collective-permute-start.2
  32.6 1.9 collective-permute-done.2
  34.5 0.1 add.16
  34.6 0.0 copy-start.7
  34.6 0.0 copy-start.6
  34.6 0.0 copy-start.8
  34.6 0.0 copy-start.9
  34.6 0.0 copy-start.10
  34.6 0.0 copy-start.3
  34.6 31.8 %all_to_all.10 = f32[64,16,128]{2,1,0:T(8,128)S(1)} all-to-all(f32[64,16,128]{2,1,0:T(8,128)S(1)} %bitcast.5), channel_id=1, replica_groups=mesh['z'=8,'y'=8,'core'=2,'x'=4] {'z','y'}, dimensions={0} | all-to-all | bytes 1048576 | tf_op jit(solution)/shard_map/all_to_all | solution.py:348
  66.4 0.1 reduce_sum.9
  66.5 22.9 %all_to_all.11 = f32[64,16,128]{2,1,0:T(8,128)} all-to-all(f32[64,16,128]{2,1,0:T(8,128)S(1)} %broadcast_in_dim.2), channel_id=1, replica_groups=mesh['z'=8,'y'=8,'core'=2,'x'=4] {'z','y'}, dimensions={0} | all-to-all | bytes 1048576 | tf_op jit(solution)/shard_map/all_to_all | solution.py:350
  89.5 0.0 all-gather.2.cloned.1.call-update
  89.5 33.0 %all-gather.2.cloned.1.call-done.near = f32[4,1024,128]{2,1,0:T(8,128)} async-done(((f32[1,1024,128]{2,1,0:T(8,128)}), f32[4,1024,128]{2,1,0:T(8,128)}) %all-gather.2.cloned.1.call-update) | async-done | bytes 2097168 | tf_op jit(solution)/shard_map/all_gather | solution.py:354
  122.5 2.6 %collective-permute-start.3 = (f32[4,1024,128]{2,1,0:T(8,128)}, f32[4,1024,128]{2,1,0:T(8,128)S(1)}, u32[]{:S(2)}, u32[]{:S(2)}) collective-permute-start(f32[4,1024,128]{2,1,0:T(8,128)} %all-gather.2.cloned.1.call-done.near), channel_id=1, source_target_pairs={{0,4},{4,0},{1,5},{5,1},{2,6},{6,2},{3,7},{7,3},{8,12},{12,8},{9,1... | collective-permute-start | bytes 6291464 | tf_op jit(solution)/shard_map/ppermute | solution.py:355
  125.0 0.0 copy-done.7
  125.1 0.0 copy-done.6
  125.1 0.0 copy-done.8
  125.1 0.0 copy-done.9
  125.1 0.0 copy-done.10
  125.2 0.1 stack.63.info
  125.3 0.1 pad_add_fusion.place
  125.4 3.6 %collective-permute-done.3.far = f32[4,1024,128]{2,1,0:T(8,128)S(1)} collective-permute-done((f32[4,1024,128]{2,1,0:T(8,128)}, f32[4,1024,128]{2,1,0:T(8,128)S(1)}, u32[]{:S(2)}, u32[]{:S(2)}) %collective-permute-start.3) | collective-permute-done | bytes 2097184 | tf_op jit(solution)/shard_map/ppermute | solution.py:355
  129.0 0.0 copy-done.3
  129.0 0.0 copy-start.1
  129.0 1.6 copy-done.1
  130.6 68.5 %shard_map.101 = f32[80,3,2,4,128]{4,3,2,1,0:T(4,128)} custom-call(s32[2]{0:T(128)S(1)} %pad_add_fusion.place, f32[4,2]{1,0:T(4,128)S(1)} %copy.14.table, f32[12,8,128]{2,1,0:T(8,128)S(1)} %stack.63.info, f32[4,1024,128]{2,1,0:T(8,128)S(1)} %copy-done.1, f32[4,1024,128]{2,1,0:T(8,128)S(1)} %collective-permute-done.3.far, f32[24,80,128]{2,1,0:T(8,128)S(1)} %copy-done.3), custom_call_target="tpu_custom_call" | custom-call | tf_op jit(solution)/shard_map/pallas_call | solution.py:290
  (14 shorter events, 0.1 us)
Async XLA Ops:
  6.5 18.5 %copy-start = (f32[80,3,2,4,128]{4,3,2,1,0:T(4,128)S(1)}, f32[80,3,2,4,128]{4,3,2,1,0:T(4,128)}, u32[]{:S(2)}) copy-start(f32[80,3,2,4,128]{4,3,2,1,0:T(4,128)} %state.1) | copy-start | bytes 2949124
  6.5 18.5 %copy-start.5 = (f32[2,128]{1,0:T(2,128)S(1)}, f32[2,128]{1,0:T(2,128)}, u32[]{:S(2)}) copy-start(f32[2,128]{1,0:T(2,128)} %north.1) | copy-start | bytes 3076
  6.5 18.5 %copy-start.4 = (f32[2,128]{1,0:T(2,128)S(1)}, f32[2,128]{1,0:T(2,128)}, u32[]{:S(2)}) copy-start(f32[2,128]{1,0:T(2,128)} %east.1) | copy-start | bytes 3076
  6.5 115.9 %all-gather.2.cloned.1.call-start = ((), (), s32[]{:S(2)}) async-start(), calls=%async_computation.2 | async-start | bytes 2621440 | tf_op jit(solution)/shard_map/all_gather | solution.py:354
  8.6 14.6 %collective-permute-start.1 = (f32[80,3,2,2,128]{4,3,2,1,0:T(2,128)S(1)}, f32[80,3,2,2,128]{4,3,2,1,0:T(2,128)S(1)}, u32[]{:S(2)}, u32[]{:S(2)}) collective-permute-start(f32[80,3,2,2,128]{4,3,2,1,0:T(2,128)S(1)} %get-tuple-element.11), channel_id=1, source_target_pairs={{4,0},{8,4},{12,8},{16,12},{20,16},{24,20},{28,24},{32,28},{36,32}... | collective-permute-start | bytes 1474568 | tf_op jit(solution)/shard_map/ppermute | solution.py:333
  17.3 7.7 %collective-permute-start = (f32[80,3,2,2,128]{4,3,2,1,0:T(2,128)S(1)}, f32[80,3,2,2,128]{4,3,2,1,0:T(2,128)S(1)}, u32[]{:S(2)}, u32[]{:S(2)}) collective-permute-start(f32[80,3,2,2,128]{4,3,2,1,0:T(2,128)S(1)} %get-tuple-element.12), channel_id=1, source_target_pairs={{0,4},{4,8},{8,12},{12,16},{16,20},{20,24},{24,28},{28,32},{32,36}... | collective-permute-start | bytes 1474568 | tf_op jit(solution)/shard_map/ppermute | solution.py:332
  29.8 0.9 copy-start.2
  30.7 3.8 %collective-permute-start.2 = (f32[1024,128]{1,0:T(8,128)S(1)}, f32[1024,128]{1,0:T(8,128)S(1)}, u32[]{:S(2)}, u32[]{:S(2)}) collective-permute-start(f32[1024,128]{1,0:T(8,128)S(1)} %get-tuple-element.9), channel_id=1, source_target_pairs={{0,4},{4,0},{1,5},{5,1},{2,6},{6,2},{3,7},{7,3},{8,12},{12,8},{9,1... | collective-permute-start | bytes 1572872 | tf_op jit(solution)/shard_map/ppermute | solution.py:347
  34.6 90.5 %copy-start.7 = (s32[12,128]{1,0:T(8,128)S(1)}, s32[12,128]{1,0:T(8,128)}, u32[]{:S(2)}) copy-start(s32[12,128]{1,0:T(8,128)} %param.14) | copy-start | bytes 18436
  34.6 90.5 %copy-start.6 = (s32[12,128]{1,0:T(8,128)S(1)}, s32[12,128]{1,0:T(8,128)}, u32[]{:S(2)}) copy-start(s32[12,128]{1,0:T(8,128)} %param.13) | copy-start | bytes 18436
  34.6 90.5 %copy-start.8 = (f32[12,128]{1,0:T(8,128)S(1)}, f32[12,128]{1,0:T(8,128)}, u32[]{:S(2)}) copy-start(f32[12,128]{1,0:T(8,128)} %param.17) | copy-start | bytes 18436
  34.6 90.5 %copy-start.9 = (f32[12,128]{1,0:T(8,128)S(1)}, f32[12,128]{1,0:T(8,128)}, u32[]{:S(2)}) copy-start(f32[12,128]{1,0:T(8,128)} %param.18) | copy-start | bytes 18436
  34.6 90.5 %copy-start.10 = (s32[12,128]{1,0:T(8,128)S(1)}, s32[12,128]{1,0:T(8,128)}, u32[]{:S(2)}) copy-start(s32[12,128]{1,0:T(8,128)} %param.16) | copy-start | bytes 18436
  34.6 94.4 %copy-start.3 = (f32[24,80,128]{2,1,0:T(8,128)S(1)}, f32[24,80,128]{2,1,0:T(8,128)}, u32[]{:S(2)}) copy-start(f32[24,80,128]{2,1,0:T(8,128)} %copy-done.2) | copy-start | bytes 2949124
  122.5 6.6 %collective-permute-start.3 = (f32[4,1024,128]{2,1,0:T(8,128)}, f32[4,1024,128]{2,1,0:T(8,128)S(1)}, u32[]{:S(2)}, u32[]{:S(2)}) collective-permute-start(f32[4,1024,128]{2,1,0:T(8,128)} %all-gather.2.cloned.1.call-done.near), channel_id=1, source_target_pairs={{0,4},{4,0},{1,5},{5,1},{2,6},{6,2},{3,7},{7,3},{8,12},{12,8},{9,1... | collective-permute-start | bytes 6291464 | tf_op jit(solution)/shard_map/ppermute | solution.py:355
  129.0 1.6 copy-start.1
Sparse Core Ops, SparseCore 0:
  89.6 32.8 all-gather.1

commit v2 on v1

v2 whole, which is shorter than its diff:
```python
import functools

import jax
import jax.numpy as jnp
from jax import lax
from jax.experimental import pallas as pl
from jax.experimental.pallas import tpu as pltpu
from jax.sharding import Mesh, PartitionSpec as P

RADY = 40
KAPPA_COEF = 0.2
EPSILON = 1e-05
LANES = 128
TILES = ("z", "y", "core")


def forecast_kernel(
    place, table, state, east, north, cols, rws, flds, grid, to_left, to_right, mine, other,
    plain, ahead, seen, sems
):
    members, fields, levels, columns, rows = state.shape
    reach = 2
    batches = cols.shape[0]
    span = columns + 2 * reach
    groups = fields * levels
    first, core, origin, total_cols = place[0], place[1], place[2], place[3]
    copies = []
    for g in range(groups):
        for k in range(columns):
            slot = g * columns + k
            copies.append(
                pltpu.make_async_copy(
                    state.at[:, g // levels, g % levels, k, :], plain.at[slot], sems.at[slot]
                )
            )
    for copy in copies:
        copy.start()
    slot = cols[...] - (first - reach)
    near = jnp.where(jnp.logical_and(slot >= 0, slot < span), 1.0, 0.0)
    near = jnp.max(near, axis=1, keepdims=True)
    for b in range(batches):
        seen[b] = near[b, 0].astype(jnp.int32)
    lane = lax.broadcasted_iota(jnp.int32, (1, rows), 1)
    for g in range(groups):
        for k in range(columns):
            copies[g * columns + k].wait()
        l = g % levels
        zonal = 0.5 * east[l : l + 1, :]
        meridional = 0.5 * north[l : l + 1, :]
        to_east = KAPPA_COEF - zonal
        to_west = KAPPA_COEF + zonal
        to_north = jnp.where(lane == rows - 1, 0.0, KAPPA_COEF - meridional)
        to_south = jnp.where(lane == 0, 0.0, KAPPA_COEF + meridional)

        def step(west, here, east_):
            total = None
            if here is not None:
                total = (
                    (1.0 - 4.0 * KAPPA_COEF) * here
                    + to_north * pltpu.roll(here, rows - 1, 1)
                    + to_south * pltpu.roll(here, 1, 1)
                )
            if east_ is not None:
                total = to_east * east_ if total is None else total + to_east * east_
            if west is not None:
                total = to_west * west if total is None else total + to_west * west
            return total

        none = [None] * reach
        start = none + [plain[g * columns + k] for k in range(columns)] + none
        once = [None] * span
        for k in range(1, span - 1):
            value = step(start[k - 1], start[k], start[k + 1])
            if k < reach or k >= reach + columns:
                col = first + (k - reach)
                inside = jnp.logical_and(col >= 0, col < total_cols)
                value = jnp.where(inside, value, 0.0)
            once[k] = value
        for k in range(span):
            west = once[k - 1] if k > 0 else None
            east_ = once[k + 1] if k < span - 1 else None
            value = step(west, once[k], east_)
            ahead[g * span + k] = value
            if k < reach:
                to_left[g * reach + k] = value
            elif k < reach + columns:
                grid[g * columns + k - reach] = value
            else:
                to_right[g * reach + k - reach - columns] = value
    for out in (mine, other):
        out[batches * members :, :] = jnp.zeros(
            (out.shape[0] - batches * members, LANES), jnp.float32
        )
    vt = jnp.zeros((8, LANES), jnp.float32)
    spot = lax.broadcasted_iota(jnp.int32, (8, LANES), 1)
    for k in range(table.shape[0]):
        own_weight = jnp.where(core == 0, table[k, 0], table[k, 1])
        vt = jnp.where(spot == k, own_weight, vt)
    mine[batches * members : batches * members + 8, :] = jnp.where(origin == 1, vt, 0.0)

    def pick(b, carry):
        rows_of = pl.ds(pl.multiple_of(b * members, 8), members)
        slot = cols[pl.ds(b, 1), :] - (first - reach)
        inside = jnp.logical_and(slot >= 0, slot < span)
        target = jnp.where(inside, flds[pl.ds(b, 1), :] * span + slot, -1)
        present = seen[b] > 0

        @pl.when(jnp.logical_not(present))
        def _():
            mine[rows_of, :] = jnp.zeros((members, LANES), jnp.float32)
            other[rows_of, :] = jnp.zeros((members, LANES), jnp.float32)

        @pl.when(present)
        def _():
            wanted = jnp.broadcast_to(target, (members, LANES))
            index = jnp.broadcast_to(rws[pl.ds(b, 1), :], (members, LANES))
            for out, level in ((mine, core), (other, 1 - core)):
                total = jnp.zeros((members, LANES), jnp.float32)
                for f in range(fields):
                    for k in range(span):
                        slab = ahead[(f * levels + level) * span + k]
                        picked = jnp.take_along_axis(slab, index, axis=1)
                        total = jnp.where(wanted == f * span + k, picked, total)
                out[rows_of, :] = total

        return carry

    lax.fori_loop(0, batches, pick, 0)


def halves(x):
    high = x.astype(jnp.bfloat16)
    low = (x - high.astype(jnp.float32)).astype(jnp.bfloat16)
    return high, low


def analysis_kernel(count, place, table, info, *refs):
    arrived, rest = refs[:count], refs[count:]
    grid, from_left, from_right, out = rest[:4]
    local, remote, edges, spread_rows, spread_cols, vertical, sems = rest[4:]
    all_levels, length, _ = remote.shape
    slabs, members, rows = grid.shape
    fields, levels, columns = out.shape[1], out.shape[2], out.shape[3]
    groups = fields * levels
    batches = info.shape[0]
    total_cols = place[1].astype(jnp.float32)
    classes = table.shape[0]
    first = place[0].astype(jnp.float32)
    incoming = []
    level, at = 0, 0
    for ref in arrived:
        size = ref.shape[0]
        incoming.append((ref, remote.at[level, at : at + size]))
        at += size
        if at == length:
            level, at = level + 1, 0
    incoming += [(grid, local), (from_left, edges.at[0]), (from_right, edges.at[1])]
    incoming = [
        pltpu.make_async_copy(ref, target, sems.at[slabs + n])
        for n, (ref, target) in enumerate(incoming)
    ]
    for copy in incoming:
        copy.start()
    for copy in incoming:
        copy.wait()
    for g in range(groups):
        for k in range(2):
            west, east = g * columns + k, g * columns + columns - 2 + k
            local[west] = local[west] + edges[0, g * 2 + k]
            local[east] = local[east] + edges[1, g * 2 + k]
    inverse = 1.0 / total_cols

    def update(x, weight):
        high, low = halves(x)
        covariance = jnp.dot(
            spread_cols[...],
            jnp.concatenate([high, high, low], axis=0),
            preferred_element_type=jnp.float32,
        )
        change = jnp.dot(
            spread_rows[...],
            jnp.concatenate(halves(covariance * weight), axis=0),
            preferred_element_type=jnp.float32,
        )
        return x + (change[:members] + change[members:])

    def batch(b, carry):
        mine = pl.ds(pl.multiple_of(b * members, 8), members)
        facts = info[b]
        priors = remote[0, mine, :]
        for level in range(1, all_levels):
            priors = priors + remote[level, mine, :]
        priors = priors * (1.0 / all_levels)
        average = jnp.sum(priors, axis=0, keepdims=True) * (1.0 / members)
        spread = priors - average
        variance = jnp.sum(spread * spread, axis=0, keepdims=True) / (members - 1) + EPSILON
        error = facts[4:5]
        ratio = 1.0 / (variance + error)
        shrink = variance * ratio
        factor = jnp.sqrt(error * ratio)
        increments = shrink * (facts[3:4] - average) + (factor - 1.0) * spread
        regress = spread / ((members - 1) * variance)
        high, low = halves(increments)
        spread_rows[:members, :LANES] = high
        spread_rows[:members, LANES:] = high
        spread_rows[members:, :LANES] = low
        spread_rows[members:, LANES:] = jnp.zeros_like(low)
        high = regress.astype(jnp.bfloat16).astype(jnp.float32)
        low = regress - high
        stacked = jnp.concatenate(
            [high, low, high, jnp.zeros((256 - 3 * members, LANES), jnp.float32)], axis=0
        )
        spread_cols[...] = jnp.transpose(stacked)[:, : 3 * members].astype(jnp.bfloat16)

        def column_of(k):
            return jnp.transpose(jnp.broadcast_to(facts[k : k + 1], (LANES, LANES)))

        obs_col, obs_row, obs_class = column_of(0), column_of(1), column_of(2)
        for level in range(all_levels + levels):
            if level < all_levels:
                row = remote[level, batches * members : batches * members + 8, :]
                weights = [
                    jnp.broadcast_to(row[0:1, k : k + 1], (LANES, LANES)) for k in range(classes)
                ]
            else:
                weights = [table[k, level - all_levels] for k in range(classes)]
            chosen = jnp.zeros((LANES, LANES), jnp.float32) + weights[classes - 1]
            for k in range(classes - 1):
                chosen = jnp.where(obs_class == float(k), weights[k], chosen)
            vertical[level] = chosen

        def later_many(c0, many):
            xs, ws, keep = [], [], []
            for k in range(many):
                c = c0 + k
                theirs = pl.ds(pl.multiple_of(c * members, 8), members)
                there = info[c]
                d_col = (there[0:1] - obs_col) * inverse
                d_row = (there[1:2] - obs_row) * (1.0 / RADY)
                radial = jnp.maximum(1.0 - d_col * d_col - d_row * d_row, 0.0)
                taper = radial * radial
                for g in range(all_levels):
                    xs.append(remote[g, theirs, :])
                    ws.append(taper * vertical[g])
                    keep.append((g, theirs))
            x = update(jnp.concatenate(xs, axis=1), jnp.concatenate(ws, axis=1))
            for n, (g, theirs) in enumerate(keep):
                remote[g, theirs, :] = x[:, n * LANES : (n + 1) * LANES]

        count = batches - 1 - b

        for size in (1, 2):

            @pl.when((count // size) % 2 == 1)
            def _():
                later_many(b + 1 + (count % size), size)

        start = b + 1 + count % 4

        def four(i, carry):
            later_many(start + 4 * i, 4)
            return carry

        lax.fori_loop(0, count // 4, four, 0)
        lane = lax.broadcasted_iota(jnp.int32, (1, LANES), 1).astype(jnp.float32)
        d_row = (lane - obs_row) * (1.0 / RADY)
        across = 1.0 - d_row * d_row
        along = (first - obs_col) * inverse
        xs, ws = [], []
        for k in range(columns):
            d_col = along + k * inverse
            radial = jnp.maximum(across - d_col * d_col, 0.0)
            taper = radial * radial
            for level in range(levels):
                weight = taper * vertical[all_levels + level]
                for f in range(fields):
                    xs.append((f * levels + level) * columns + k)
                    ws.append(weight)
        step = 24
        for n in range(0, len(xs), step):
            x = update(
                jnp.concatenate([local[at] for at in xs[n : n + step]], axis=1),
                jnp.concatenate(ws[n : n + step], axis=1),
            )
            for i, at in enumerate(xs[n : n + step]):
                local[at] = x[:, i * LANES : (i + 1) * LANES]
        return carry

    lax.fori_loop(0, batches, batch, 0)
    outgoing = []
    for f in range(fields):
        for level in range(levels):
            for k in range(columns):
                at = (f * levels + level) * columns + k
                outgoing.append(
                    pltpu.make_async_copy(
                        local.at[at], out.at[:, f, level, k, :], sems.at[at]
                    )
                )
    for copy in outgoing:
        copy.start()
    for copy in outgoing:
        copy.wait()


def forecast(place, table, state, east, north, cols, rws, flds, length):
    members, fields, levels, columns, rows = state.shape
    groups = fields * levels
    smem = pl.BlockSpec(memory_space=pltpu.SMEM)
    vmem = pl.BlockSpec(memory_space=pltpu.VMEM)
    anywhere = pl.BlockSpec(memory_space=pl.ANY)
    picks = jax.ShapeDtypeStruct((length, LANES), jnp.float32)
    edge = jax.ShapeDtypeStruct((groups * 2, members, rows), jnp.float32)
    return pl.pallas_call(
        forecast_kernel,
        out_shape=(
            jax.ShapeDtypeStruct((groups * columns, members, rows), jnp.float32),
            edge,
            edge,
            picks,
            picks,
        ),
        in_specs=[smem, smem, anywhere] + [vmem] * 5,
        out_specs=(vmem,) * 5,
        scratch_shapes=[
            pltpu.VMEM((groups * columns, members, rows), jnp.float32),
            pltpu.VMEM((groups * (columns + 4), members, rows), jnp.float32),
            pltpu.SMEM((cols.shape[0],), jnp.int32),
            pltpu.SemaphoreType.DMA((groups * columns,)),
        ],
        compiler_params=pltpu.CompilerParams(vmem_limit_bytes=40 * 2**20),
    )(place, table, state, east, north, cols, rws, flds)


def assimilate(place, table, info, arrived, grid, from_left, from_right, shape, length):
    members, fields, levels, columns, rows = shape
    smem = pl.BlockSpec(memory_space=pltpu.SMEM)
    vmem = pl.BlockSpec(memory_space=pltpu.VMEM)
    anywhere = pl.BlockSpec(memory_space=pl.ANY)
    all_levels = sum(part.shape[0] for part in arrived) // length
    return pl.pallas_call(
        functools.partial(analysis_kernel, len(arrived)),
        out_shape=jax.ShapeDtypeStruct(shape, jnp.float32),
        in_specs=[smem, smem, vmem] + [anywhere] * (len(arrived) + 3),
        out_specs=anywhere,
        scratch_shapes=[
            pltpu.VMEM(grid.shape, jnp.float32),
            pltpu.VMEM((all_levels, length, LANES), jnp.float32),
            pltpu.VMEM((2,) + from_left.shape, jnp.float32),
            pltpu.VMEM((2 * members, 2 * LANES), jnp.bfloat16),
            pltpu.VMEM((LANES, 3 * members), jnp.bfloat16),
            pltpu.VMEM((all_levels + levels, LANES, LANES), jnp.float32),
            pltpu.SemaphoreType.DMA((grid.shape[0] + len(arrived) + 3,)),
        ],
        compiler_params=pltpu.CompilerParams(vmem_limit_bytes=48 * 2**20),
    )(place, table, info, *arrived, grid, from_left, from_right)


def shards(
    state,
    eastward_current,
    northward_current,
    obs_col,
    obs_row,
    obs_field,
    obs_class,
    obs_value,
    obs_error,
    vertical_table,
):
    members, fields, levels, columns, rows = state.shape
    batches, obs = obs_col.shape
    homes = lax.axis_size("z") * lax.axis_size("y")
    tiles = homes * lax.axis_size("core")
    tile = lax.axis_index(TILES)
    core = lax.axis_index("core")
    first = tile * columns
    chunk = -(-(batches * members + 8) // (8 * homes)) * 8
    length = chunk * homes

    origin = (tile // 2 == 0).astype(jnp.int32)
    place = jnp.stack([first, core, origin, jnp.int32(tiles * columns)]).astype(jnp.int32)
    grid, to_left, to_right, mine, other = forecast(
        place, vertical_table, state, eastward_current, northward_current, obs_col, obs_row,
        obs_field, length,
    )

    swap = [(0, 1), (1, 0)]
    mine = mine + lax.ppermute(other, "core", swap)
    mine = lax.all_to_all(mine.reshape(homes, chunk, LANES), ("z", "y"), 0, 0, tiled=True)
    mine = jnp.sum(mine, axis=0)
    mine = lax.all_to_all(
        jnp.broadcast_to(mine[None], (homes, chunk, LANES)), ("z", "y"), 0, 0, tiled=True
    )
    mine = mine.reshape(length, LANES)

    mine, to_left, to_right = lax.optimization_barrier((mine, to_left, to_right))
    ring = lax.axis_size("x")
    right = [(i, (i + 1) % ring) for i in range(ring)]
    left = [(j, i) for i, j in right]
    before = lax.ppermute(mine, "x", right)
    after = lax.ppermute(mine, "x", left)
    across_a = lax.ppermute(after[: length // 2], "x", left)
    across_b = lax.ppermute(before[length // 2 :], "x", right)
    parts = [mine, before, after, across_a, across_b]
    arrived = parts + [lax.ppermute(part, "core", swap) for part in parts]
    up = [(i, i + 1) for i in range(tiles - 1)]
    down = [(j, i) for i, j in up]
    from_left = lax.ppermute(to_right, TILES, up)
    from_right = lax.ppermute(to_left, TILES, down)

    as_float = [v.astype(jnp.float32) for v in (obs_col, obs_row, obs_class)]
    blank = jnp.zeros_like(obs_value)
    info = jnp.stack([*as_float, obs_value, obs_error, blank, blank, blank], axis=1)
    where = jnp.stack([first, jnp.int32(tiles * columns)]).astype(jnp.int32)
    return assimilate(
        where, vertical_table, info, arrived, grid, from_left, from_right, state.shape, length
    )


def solution(mesh):
    fine = Mesh(mesh.devices.reshape(8, 8, 2, 4), ("z", "y", "core", "x"))
    state = P(None, None, "x", TILES, None)
    placed = (
        state,
        P("x", None),
        P("x", None),
        P(),
        P(),
        P(),
        P(),
        P(),
        P(),
        P(None, "x"),
    )
    return jax.shard_map(shards, mesh=fine, in_specs=placed, out_specs=state, check_vma=False)
```

time: 207 us -> 148 us (0.71)
  waiting for transfers between devices: 40.4 us -> 1.54 us
  Pallas kernels: 73.3 us -> 41.8 us
  starting transfers between devices: 15.2 us -> 43.2 us
  between operations: 13.7 us -> 0.42 us
  blocking collectives: 54.7 us -> 51.7 us
    all_gather x1 -> x0, waiting for transfers between devices: 33 us -> none  [shards(): near = lax.all_gather(mine, 'x')]
    pallas_call x2, Pallas kernels: 73.3 us -> 41.8 us  [the longest x1 37.6 us: assimilate(): pl.pallas_call(functools.partial(analysis_kernel, len(arrived)), out_shap...]
    ppermute x3 -> x11, starting transfers between devices: 13.3 us -> 34.4 us  [the longest x5 12.2 us: shards(): arrived = parts + [lax.ppermute(part, 'core', swap) for part in parts]]
    ppermute x1, starting transfers between devices: 1.91 us -> 8.79 us  [shards(): mine = mine + lax.ppermute(other, 'core', swap)]
    ppermute x3 -> x11, waiting for transfers between devices: 5.51 us -> 0.03 us  [the longest x5 0.01 us: shards(): arrived = parts + [lax.ppermute(part, 'core', swap) for part in parts]]
    unnamed x23 -> x37, local copies, waits for them, and re-layouts: 3.35 us -> 7.64 us
    all_to_all x1, blocking collectives: 31.8 us -> 28.8 us  [shards(): lax.all_to_all(mine.reshape(homes, chunk, LANES), ('z', 'y'), 0, 0, tiled...]
    another operation x6 -> x0, local copies, waits for them, and re-layouts: 2.18 us -> none  [shards(): jnp.stack([obs_col, obs_row, obs_field, zero, zero, zero, zero, zero], ax...]
  transfers between devices with their start and end apart: 5 -> 12, of which waited for: 4 -> 1; matrix products, arithmetic and copies ran while one was open for 2% -> 0% of each run, Pallas kernels for 0% -> 0%
where the time goes in v2:
time: 148 us; the launch traced here: 147 us
  blocking collectives  51.7 us (35%)
  starting transfers between devices  43.2 us (29%)
  Pallas kernels  41.8 us (28%)
  local copies, waits for them, and re-layouts  7.83 us (5%)
  waiting for transfers between devices  1.54 us (1%)
    pallas_call x1, Pallas kernels, assimilate(): pl.pallas_call(functools.partial(analysis_kernel, len(arrived)), out_shap...  37.6 us
    all_to_all x1, blocking collectives, shards(): lax.all_to_all(mine.reshape(homes, chunk, LANES), ('z', 'y'), 0, 0, tiled...  28.8 us
    all_to_all x1, blocking collectives, shards(): lax.all_to_all(jnp.broadcast_to(mine[None], (homes, chunk, LANES)), ('z',...  22.9 us
    ppermute x5, starting transfers between devices, shards(): arrived = parts + [lax.ppermute(part, 'core', swap) for part in parts]  12.2 us
    ppermute x1, starting transfers between devices, shards(): mine = mine + lax.ppermute(other, 'core', swap)  8.79 us
    unnamed x37, local copies, waits for them, and re-layouts  7.64 us
    ppermute x1, starting transfers between devices, shards(): from_left = lax.ppermute(to_right, TILES, up)  7.2 us
    ppermute x1, starting transfers between devices, shards(): across_a = lax.ppermute(after[:length // 2], 'x', left)  4.85 us
  transfers between devices with their start and end apart: 12, of which 1 were waited for; matrix products, arithmetic and copies ran while one was open for 0% of the time, Pallas kernels for 0%

profile of v2, /device:TPU:1, one launch (start us, length us, event | category | flops | bytes accessed | tf_op | source)
XLA Modules:
  0.0 146.7 jit_solution(17148582880204763477)
XLA Ops:
  0.0 0.0 copy-start.7
  0.0 0.0 copy-start.5
  0.0 0.0 copy-start.6
  0.0 0.6 copy-done.17
  0.7 0.1 copy.12.table
  0.8 0.1 pad_add_fusion.1.place
  0.8 0.0 copy-done.8
  0.9 0.0 copy-done.9
  0.9 0.0 copy-done.7
  0.9 0.0 copy-done.5
  0.9 0.0 copy-done.6
  0.9 0.0 copy-start
  0.9 1.2 copy-done
  2.1 4.1 %shard_map.100 = (f32[24,80,128]{2,1,0:T(8,128)S(1)}, f32[12,80,128]{2,1,0:T(8,128)S(1)}, f32[12,80,128]{2,1,0:T(8,128)S(1)}, f32[1024,128]{1,0:T(8,128)S(1)}, f32[1024,128]{1,0:T(8,128)S(1)}) custom-call(s32[4]{0:T(128)S(1)} %pad_add_fusion.1.place, f32[4,2]{1,0:T(4,128)S(1)} %copy.12.table, f32[80,3,2,4,128]{4,3,2,1,0:T(4,128)S(1)} %copy-done, ...), custom_call_target="tpu_custom_call" | custom-call | tf_op jit(solution)/shard_map/pallas_call | solution.py:314
  6.2 0.0 copy-start.10
  6.2 0.0 copy-start.12
  6.3 8.8 %collective-permute-start = (f32[1024,128]{1,0:T(8,128)S(1)}, f32[1024,128]{1,0:T(8,128)S(1)}, u32[]{:S(2)}, u32[]{:S(2)}) collective-permute-start(f32[1024,128]{1,0:T(8,128)S(1)} %get-tuple-element.14), channel_id=1, source_target_pairs={{0,4},{4,0},{1,5},{5,1},{2,6},{6,2},{3,7},{7,3},{8,12},{12,8},{9,1... | collective-permute-start | bytes 1572872 | tf_op jit(solution)/shard_map/ppermute | solution.py:389
  15.0 1.5 %collective-permute-done = f32[1024,128]{1,0:T(8,128)S(1)} collective-permute-done((f32[1024,128]{1,0:T(8,128)S(1)}, f32[1024,128]{1,0:T(8,128)S(1)}, u32[]{:S(2)}, u32[]{:S(2)}) %collective-permute-start) | collective-permute-done | bytes 524320 | tf_op jit(solution)/shard_map/ppermute | solution.py:389
  16.6 0.1 add.12
  16.6 0.0 copy-done.10
  16.6 0.0 copy-done.12
  16.6 28.8 %all_to_all.10 = f32[64,16,128]{2,1,0:T(8,128)S(1)} all-to-all(f32[64,16,128]{2,1,0:T(8,128)S(1)} %bitcast.9), channel_id=1, replica_groups=mesh['z'=8,'y'=8,'core'=2,'x'=4] {'z','y'}, dimensions={0} | all-to-all | bytes 1048576 | tf_op jit(solution)/shard_map/all_to_all | solution.py:390
  45.5 0.1 reduce_sum.9
  45.6 0.0 copy-start.13
  45.6 0.0 copy-start.11
  45.6 22.9 %all_to_all.11 = f32[64,16,128]{2,1,0:T(8,128)S(1)} all-to-all(f32[64,16,128]{2,1,0:T(8,128)S(1)} %broadcast_in_dim.2), channel_id=1, replica_groups=mesh['z'=8,'y'=8,'core'=2,'x'=4] {'z','y'}, dimensions={0} | all-to-all | bytes 1048576 | tf_op jit(solution)/shard_map/all_to_all | solution.py:392
  68.5 4.4 %collective-permute-start.2 = (f32[1024,128]{1,0:T(8,128)S(1)}, f32[1024,128]{1,0:T(8,128)S(1)}, u32[]{:S(2)}, u32[]{:S(2)}) collective-permute-start(f32[1024,128]{1,0:T(8,128)S(1)} %bitcast.5), channel_id=1, source_target_pairs={{1,0},{2,1},{3,2},{0,3},{5,4},{6,5},{7,6},{4,7},{9,8},{10,9},{11,1... | collective-permute-start | bytes 1572872 | tf_op jit(solution)/shard_map/ppermute | solution.py:402
  72.9 1.9 %collective-permute-start.1 = (f32[1024,128]{1,0:T(8,128)S(1)}, f32[1024,128]{1,0:T(8,128)S(1)}, u32[]{:S(2)}, u32[]{:S(2)}) collective-permute-start(f32[1024,128]{1,0:T(8,128)S(1)} %bitcast.6), channel_id=1, source_target_pairs={{0,1},{1,2},{2,3},{3,0},{4,5},{5,6},{6,7},{7,4},{8,9},{9,10},{10,1... | collective-permute-start | bytes 1572872 | tf_op jit(solution)/shard_map/ppermute | solution.py:401
  74.8 0.0 copy-done.13
  74.8 7.2 %collective-permute-start.10 = (f32[12,80,128]{2,1,0:T(8,128)S(1)}, f32[12,80,128]{2,1,0:T(8,128)S(1)}, u32[]{:S(2)}, u32[]{:S(2)}) collective-permute-start(f32[12,80,128]{2,1,0:T(8,128)S(1)} %copy-done.13), channel_id=1, source_target_pairs={{0,4},{4,8},{8,12},{12,16},{16,20},{20,24},{24,28},{28,32},{32,36}... | collective-permute-start | bytes 1474568 | tf_op jit(solution)/shard_map/ppermute | solution.py:409
  82.0 0.0 copy-done.11
  82.0 1.9 %collective-permute-start.11 = (f32[12,80,128]{2,1,0:T(8,128)S(1)}, f32[12,80,128]{2,1,0:T(8,128)S(1)}, u32[]{:S(2)}, u32[]{:S(2)}) collective-permute-start(f32[12,80,128]{2,1,0:T(8,128)S(1)} %copy-done.11), channel_id=1, source_target_pairs={{4,0},{8,4},{12,8},{16,12},{20,16},{24,20},{28,24},{32,28},{36,32}... | collective-permute-start | bytes 1474568 | tf_op jit(solution)/shard_map/ppermute | solution.py:410
  84.0 1.9 %collective-permute-start.5 = (f32[1024,128]{1,0:T(8,128)S(1)}, f32[1024,128]{1,0:T(8,128)S(1)}, u32[]{:S(2)}, u32[]{:S(2)}) collective-permute-start(f32[1024,128]{1,0:T(8,128)S(1)} %bitcast.7), channel_id=1, source_target_pairs={{0,4},{4,0},{1,5},{5,1},{2,6},{6,2},{3,7},{7,3},{8,12},{12,8},{9,1... | collective-permute-start | bytes 1572872 | tf_op jit(solution)/shard_map/ppermute | solution.py:406
  85.9 0.0 collective-permute-done.2.refs_2_
  85.9 4.9 %collective-permute-start.3 = (f32[512,128]{1,0:T(8,128)S(1)}, f32[512,128]{1,0:T(8,128)S(1)}, u32[]{:S(2)}, u32[]{:S(2)}) collective-permute-start(f32[512,128]{1,0:T(8,128)S(1)} %slice.8), channel_id=1, source_target_pairs={{1,0},{2,1},{3,2},{0,3},{5,4},{6,5},{7,6},{4,7},{9,8},{10,9},{11,1... | collective-permute-start | bytes 786440 | tf_op jit(solution)/shard_map/ppermute | solution.py:403
  90.8 0.0 collective-permute-done.1.refs_1_
  90.8 1.9 %collective-permute-start.4 = (f32[512,128]{1,0:T(8,128)S(1)}, f32[512,128]{1,0:T(8,128)}, u32[]{:S(2)}, u32[]{:S(2)}) collective-permute-start(f32[512,128]{1,0:T(8,128)S(1)} %slice.9), channel_id=1, source_target_pairs={{0,1},{1,2},{2,3},{3,0},{4,5},{5,6},{6,7},{7,4},{8,9},{9,10},{10,1... | collective-permute-start | bytes 786440 | tf_op jit(solution)/shard_map/ppermute | solution.py:404
  92.8 0.0 collective-permute-done.10.refs_11_
  92.8 0.0 copy-start.1
  92.8 0.8 copy-done.1
  93.6 2.7 %collective-permute-start.7 = (f32[1024,128]{1,0:T(8,128)S(1)}, f32[1024,128]{1,0:T(8,128)}, u32[]{:S(2)}, u32[]{:S(2)}) collective-permute-start(f32[1024,128]{1,0:T(8,128)S(1)} %collective-permute-done.2.refs_2_), channel_id=1, source_target_pairs={{0,4},{4,0},{1,5},{5,1},{2,6},{6,2},{3,7},{7,3},{8,12},{12,8},{9,1... | collective-permute-start | bytes 1572872 | tf_op jit(solution)/shard_map/ppermute | solution.py:406
  96.2 0.0 collective-permute-done.11.refs_12_
  96.3 0.0 copy-start.3
  96.3 0.8 copy-done.3
  97.0 1.9 %collective-permute-start.6 = (f32[1024,128]{1,0:T(8,128)S(1)}, f32[1024,128]{1,0:T(8,128)}, u32[]{:S(2)}, u32[]{:S(2)}) collective-permute-start(f32[1024,128]{1,0:T(8,128)S(1)} %collective-permute-done.1.refs_1_), channel_id=1, source_target_pairs={{0,4},{4,0},{1,5},{5,1},{2,6},{6,2},{3,7},{7,3},{8,12},{12,8},{9,1... | collective-permute-start | bytes 1572872 | tf_op jit(solution)/shard_map/ppermute | solution.py:406
  99.0 0.0 collective-permute-done.3.refs_3_
  99.0 2.4 %collective-permute-start.8 = (f32[512,128]{1,0:T(8,128)S(1)}, f32[512,128]{1,0:T(8,128)}, u32[]{:S(2)}, u32[]{:S(2)}) collective-permute-start(f32[512,128]{1,0:T(8,128)S(1)} %collective-permute-done.3.refs_3_), channel_id=1, source_target_pairs={{0,4},{4,0},{1,5},{5,1},{2,6},{6,2},{3,7},{7,3},{8,12},{12,8},{9,1... | collective-permute-start | bytes 786440 | tf_op jit(solution)/shard_map/ppermute | solution.py:406
  101.4 0.0 collective-permute-done.4.refs_4_
  101.4 3.3 %collective-permute-start.9 = (f32[512,128]{1,0:T(8,128)}, f32[512,128]{1,0:T(8,128)}, u32[]{:S(2)}, u32[]{:S(2)}) collective-permute-start(f32[512,128]{1,0:T(8,128)} %collective-permute-done.4.refs_4_), channel_id=1, source_target_pairs={{0,4},{4,0},{1,5},{5,1},{2,6},{6,2},{3,7},{7,3},{8,12},{12,8},{9,1... | collective-permute-start | bytes 786440 | tf_op jit(solution)/shard_map/ppermute | solution.py:406
  104.7 0.0 copy-start.14
  104.7 0.7 copy-done.14
  105.4 0.7 copy-done.15
  106.1 0.7 copy-done.16
  106.9 0.1 stack.48.info
  106.9 0.1 pad_add_fusion.place
  107.0 0.0 collective-permute-done.5.refs_5_
  107.0 0.0 collective-permute-done.8.refs_8_
  107.0 0.0 collective-permute-done.7.refs_7_
  107.0 0.0 collective-permute-done.9.refs_9_
  107.0 0.0 collective-permute-done.6.refs_6_
  107.0 0.0 copy-start.2
  107.1 1.0 copy-done.2
  108.1 1.0 copy-done.4
  109.1 37.6 %shard_map.101 = f32[80,3,2,4,128]{4,3,2,1,0:T(4,128)} custom-call(s32[2]{0:T(128)S(1)} %pad_add_fusion.place, f32[4,2]{1,0:T(4,128)S(1)} %copy.12.table, f32[12,8,128]{2,1,0:T(8,128)S(1)} %stack.48.info, f32[1024,128]{1,0:T(8,128)S(1)} %bitcast.8, f32[1024,128]{1,0:T(8,128)S(1)} %collective-permute-done.1.refs_1_, ...), custom_call_target="tpu_custom_call" | custom-call | tf_op jit(solution)/shard_map/pallas_call | solution.py:341
  (19 shorter events, 0.1 us)
Async XLA Ops:
  0.0 0.7 copy-start.17
  0.0 0.8 copy-start.8
  0.0 0.8 copy-start.9
  0.0 0.8 copy-start.7
  0.0 0.8 copy-start.5
  0.0 0.8 copy-start.6
  0.9 1.2 copy-start
  6.2 10.4 %copy-start.10 = (f32[12,80,128]{2,1,0:T(8,128)}, f32[12,80,128]{2,1,0:T(8,128)S(1)}, u32[]{:S(2)}) copy-start(f32[12,80,128]{2,1,0:T(8,128)S(1)} %get-tuple-element.20) | copy-start | bytes 1474564
  6.2 10.4 %copy-start.12 = (f32[12,80,128]{2,1,0:T(8,128)}, f32[12,80,128]{2,1,0:T(8,128)S(1)}, u32[]{:S(2)}) copy-start(f32[12,80,128]{2,1,0:T(8,128)S(1)} %get-tuple-element.19) | copy-start | bytes 1474564
  6.3 10.3 %collective-permute-start = (f32[1024,128]{1,0:T(8,128)S(1)}, f32[1024,128]{1,0:T(8,128)S(1)}, u32[]{:S(2)}, u32[]{:S(2)}) collective-permute-start(f32[1024,128]{1,0:T(8,128)S(1)} %get-tuple-element.14), channel_id=1, source_target_pairs={{0,4},{4,0},{1,5},{5,1},{2,6},{6,2},{3,7},{7,3},{8,12},{12,8},{9,1... | collective-permute-start | bytes 1572872 | tf_op jit(solution)/shard_map/ppermute | solution.py:389
  45.6 29.2 %copy-start.13 = (f32[12,80,128]{2,1,0:T(8,128)S(1)}, f32[12,80,128]{2,1,0:T(8,128)}, u32[]{:S(2)}) copy-start(f32[12,80,128]{2,1,0:T(8,128)} %copy-done.12) | copy-start | bytes 1474564
  45.6 36.4 %copy-start.11 = (f32[12,80,128]{2,1,0:T(8,128)S(1)}, f32[12,80,128]{2,1,0:T(8,128)}, u32[]{:S(2)}) copy-start(f32[12,80,128]{2,1,0:T(8,128)} %copy-done.10) | copy-start | bytes 1474564
  68.5 17.4 %collective-permute-start.2 = (f32[1024,128]{1,0:T(8,128)S(1)}, f32[1024,128]{1,0:T(8,128)S(1)}, u32[]{:S(2)}, u32[]{:S(2)}) collective-permute-start(f32[1024,128]{1,0:T(8,128)S(1)} %bitcast.5), channel_id=1, source_target_pairs={{1,0},{2,1},{3,2},{0,3},{5,4},{6,5},{7,6},{4,7},{9,8},{10,9},{11,1... | collective-permute-start | bytes 1572872 | tf_op jit(solution)/shard_map/ppermute | solution.py:402
  72.9 17.9 %collective-permute-start.1 = (f32[1024,128]{1,0:T(8,128)S(1)}, f32[1024,128]{1,0:T(8,128)S(1)}, u32[]{:S(2)}, u32[]{:S(2)}) collective-permute-start(f32[1024,128]{1,0:T(8,128)S(1)} %bitcast.6), channel_id=1, source_target_pairs={{0,1},{1,2},{2,3},{3,0},{4,5},{5,6},{6,7},{7,4},{8,9},{9,10},{10,1... | collective-permute-start | bytes 1572872 | tf_op jit(solution)/shard_map/ppermute | solution.py:401
  74.8 17.9 %collective-permute-start.10 = (f32[12,80,128]{2,1,0:T(8,128)S(1)}, f32[12,80,128]{2,1,0:T(8,128)S(1)}, u32[]{:S(2)}, u32[]{:S(2)}) collective-permute-start(f32[12,80,128]{2,1,0:T(8,128)S(1)} %copy-done.13), channel_id=1, source_target_pairs={{0,4},{4,8},{8,12},{12,16},{16,20},{20,24},{24,28},{28,32},{32,36}... | collective-permute-start | bytes 1474568 | tf_op jit(solution)/shard_map/ppermute | solution.py:409
  82.0 14.2 %collective-permute-start.11 = (f32[12,80,128]{2,1,0:T(8,128)S(1)}, f32[12,80,128]{2,1,0:T(8,128)S(1)}, u32[]{:S(2)}, u32[]{:S(2)}) collective-permute-start(f32[12,80,128]{2,1,0:T(8,128)S(1)} %copy-done.11), channel_id=1, source_target_pairs={{4,0},{8,4},{12,8},{16,12},{20,16},{24,20},{28,24},{32,28},{36,32}... | collective-permute-start | bytes 1474568 | tf_op jit(solution)/shard_map/ppermute | solution.py:410
  84.0 23.0 %collective-permute-start.5 = (f32[1024,128]{1,0:T(8,128)S(1)}, f32[1024,128]{1,0:T(8,128)S(1)}, u32[]{:S(2)}, u32[]{:S(2)}) collective-permute-start(f32[1024,128]{1,0:T(8,128)S(1)} %bitcast.7), channel_id=1, source_target_pairs={{0,4},{4,0},{1,5},{5,1},{2,6},{6,2},{3,7},{7,3},{8,12},{12,8},{9,1... | collective-permute-start | bytes 1572872 | tf_op jit(solution)/shard_map/ppermute | solution.py:406
  85.9 13.0 %collective-permute-start.3 = (f32[512,128]{1,0:T(8,128)S(1)}, f32[512,128]{1,0:T(8,128)S(1)}, u32[]{:S(2)}, u32[]{:S(2)}) collective-permute-start(f32[512,128]{1,0:T(8,128)S(1)} %slice.8), channel_id=1, source_target_pairs={{1,0},{2,1},{3,2},{0,3},{5,4},{6,5},{7,6},{4,7},{9,8},{10,9},{11,1... | collective-permute-start | bytes 786440 | tf_op jit(solution)/shard_map/ppermute | solution.py:403
  90.8 10.6 %collective-permute-start.4 = (f32[512,128]{1,0:T(8,128)S(1)}, f32[512,128]{1,0:T(8,128)}, u32[]{:S(2)}, u32[]{:S(2)}) collective-permute-start(f32[512,128]{1,0:T(8,128)S(1)} %slice.9), channel_id=1, source_target_pairs={{0,1},{1,2},{2,3},{3,0},{4,5},{5,6},{6,7},{7,4},{8,9},{9,10},{10,1... | collective-permute-start | bytes 786440 | tf_op jit(solution)/shard_map/ppermute | solution.py:404
  92.8 0.8 copy-start.1
  93.6 13.5 %collective-permute-start.7 = (f32[1024,128]{1,0:T(8,128)S(1)}, f32[1024,128]{1,0:T(8,128)}, u32[]{:S(2)}, u32[]{:S(2)}) collective-permute-start(f32[1024,128]{1,0:T(8,128)S(1)} %collective-permute-done.2.refs_2_), channel_id=1, source_target_pairs={{0,4},{4,0},{1,5},{5,1},{2,6},{6,2},{3,7},{7,3},{8,12},{12,8},{9,1... | collective-permute-start | bytes 1572872 | tf_op jit(solution)/shard_map/ppermute | solution.py:406
  96.3 0.8 copy-start.3
  97.0 10.0 %collective-permute-start.6 = (f32[1024,128]{1,0:T(8,128)S(1)}, f32[1024,128]{1,0:T(8,128)}, u32[]{:S(2)}, u32[]{:S(2)}) collective-permute-start(f32[1024,128]{1,0:T(8,128)S(1)} %collective-permute-done.1.refs_1_), channel_id=1, source_target_pairs={{0,4},{4,0},{1,5},{5,1},{2,6},{6,2},{3,7},{7,3},{8,12},{12,8},{9,1... | collective-permute-start | bytes 1572872 | tf_op jit(solution)/shard_map/ppermute | solution.py:406
  99.0 8.0 %collective-permute-start.8 = (f32[512,128]{1,0:T(8,128)S(1)}, f32[512,128]{1,0:T(8,128)}, u32[]{:S(2)}, u32[]{:S(2)}) collective-permute-start(f32[512,128]{1,0:T(8,128)S(1)} %collective-permute-done.3.refs_3_), channel_id=1, source_target_pairs={{0,4},{4,0},{1,5},{5,1},{2,6},{6,2},{3,7},{7,3},{8,12},{12,8},{9,1... | collective-permute-start | bytes 786440 | tf_op jit(solution)/shard_map/ppermute | solution.py:406
  101.4 5.6 %collective-permute-start.9 = (f32[512,128]{1,0:T(8,128)}, f32[512,128]{1,0:T(8,128)}, u32[]{:S(2)}, u32[]{:S(2)}) collective-permute-start(f32[512,128]{1,0:T(8,128)} %collective-permute-done.4.refs_4_), channel_id=1, source_target_pairs={{0,4},{4,0},{1,5},{5,1},{2,6},{6,2},{3,7},{7,3},{8,12},{12,8},{9,1... | collective-permute-start | bytes 786440 | tf_op jit(solution)/shard_map/ppermute | solution.py:406
  104.7 0.7 copy-start.14
  105.4 0.7 copy-start.15
  106.1 0.7 copy-start.16
  107.0 1.0 copy-start.2
  108.1 1.0 copy-start.4

commit v3 on v2

--- a/solution.py
+++ b/solution.py
@@ -328,7 +328,7 @@
             pltpu.SMEM((cols.shape[0],), jnp.int32),
             pltpu.SemaphoreType.DMA((groups * columns,)),
         ],
-        compiler_params=pltpu.CompilerParams(vmem_limit_bytes=40 * 2**20),
+        compiler_params=pltpu.CompilerParams(vmem_limit_bytes=16 * 2**20),
     )(place, table, state, east, north, cols, rws, flds)
 
 
@@ -352,7 +352,7 @@
             pltpu.VMEM((all_levels + levels, LANES, LANES), jnp.float32),
             pltpu.SemaphoreType.DMA((grid.shape[0] + len(arrived) + 3,)),
         ],
-        compiler_params=pltpu.CompilerParams(vmem_limit_bytes=48 * 2**20),
+        compiler_params=pltpu.CompilerParams(vmem_limit_bytes=28 * 2**20),
     )(place, table, info, *arrived, grid, from_left, from_right)
 
 
@@ -394,16 +394,23 @@
     )
     mine = mine.reshape(length, LANES)
 
-    mine, to_left, to_right = lax.optimization_barrier((mine, to_left, to_right))
     ring = lax.axis_size("x")
-    right = [(i, (i + 1) % ring) for i in range(ring)]
-    left = [(j, i) for i, j in right]
-    before = lax.ppermute(mine, "x", right)
-    after = lax.ppermute(mine, "x", left)
-    across_a = lax.ppermute(after[: length // 2], "x", left)
-    across_b = lax.ppermute(before[length // 2 :], "x", right)
-    parts = [mine, before, after, across_a, across_b]
-    arrived = parts + [lax.ppermute(part, "core", swap) for part in parts]
+    both_ways = [(i, (i + 1) % ring) for i in range(ring)]
+    both_ways += [(ring + (i + 1) % ring, ring + i) for i in range(ring)]
+
+    def ship(part):
+        return lax.ppermute(part, ("core", "x"), both_ways)
+
+    def other_core(part):
+        return lax.ppermute(part, "core", swap)
+
+    beside = ship(mine)
+    mate = other_core(mine)
+    mated = ship(mate)
+    opposite = ship(beside)
+    mated, to_left, to_right = lax.optimization_barrier((mated, to_left, to_right))
+    arrived = [mine, mate, beside, mated, opposite]
+    arrived += [other_core(part) for part in (beside, mated, opposite)]
     up = [(i, i + 1) for i in range(tiles - 1)]
     down = [(j, i) for i, j in up]
     from_left = lax.ppermute(to_right, TILES, up)

time: 148 us -> 156 us (1.054)
  waiting for transfers between devices: 1.54 us -> 15.6 us
  local copies, waits for them, and re-layouts: 7.83 us -> 4.16 us
  starting transfers between devices: 43.2 us -> 40.7 us
    ppermute x9 -> x7, waiting for transfers between devices: 0.02 us -> 7.91 us  [the longest x3 7.9 us: ship(): return lax.ppermute(part, ('core', 'x'), both_ways)]
    ppermute x1, waiting for transfers between devices: 0.01 us -> 4.4 us  [shards(): from_right = lax.ppermute(to_left, TILES, down)]
    ppermute x1, starting transfers between devices: 7.2 us -> 3.43 us  [shards(): from_left = lax.ppermute(to_right, TILES, up)]
    unnamed x37 -> x21, local copies, waits for them, and re-layouts: 7.64 us -> 4 us
    ppermute x1, waiting for transfers between devices: 0.01 us -> 1.81 us  [shards(): from_left = lax.ppermute(to_right, TILES, up)]
    ppermute x9 -> x7, starting transfers between devices: 25.3 us -> 26.6 us  [the longest x4 14.7 us: other_core(): return lax.ppermute(part, 'core', swap)]
  transfers between devices with their start and end apart: 12 -> 10, of which waited for: 1 -> 5; matrix products, arithmetic and copies ran while one was open for 0% -> 0% of each run, Pallas kernels for 0% -> 0%
where the time goes in v3:
time: 156 us; the launch traced here: 155 us
  blocking collectives  51.2 us (33%)
  Pallas kernels  43.2 us (28%)
  starting transfers between devices  40.7 us (26%)
  waiting for transfers between devices  15.6 us (10%)
  local copies, waits for them, and re-layouts  4.16 us (3%)
    pallas_call x1, Pallas kernels, assimilate(): pl.pallas_call(functools.partial(analysis_kernel, len(arrived)), out_shap...  38.1 us
    all_to_all x1, blocking collectives, shards(): lax.all_to_all(mine.reshape(homes, chunk, LANES), ('z', 'y'), 0, 0, tiled...  28.3 us
    all_to_all x1, blocking collectives, shards(): lax.all_to_all(jnp.broadcast_to(mine[None], (homes, chunk, LANES)), ('z',...  22.8 us
    ppermute x4, starting transfers between devices, other_core(): return lax.ppermute(part, 'core', swap)  14.7 us
    ppermute x3, starting transfers between devices, ship(): return lax.ppermute(part, ('core', 'x'), both_ways)  11.9 us
    ppermute x1, starting transfers between devices, shards(): mine = mine + lax.ppermute(other, 'core', swap)  8.79 us
    ppermute x3, waiting for transfers between devices, ship(): return lax.ppermute(part, ('core', 'x'), both_ways)  7.9 us
    pallas_call x1, Pallas kernels, forecast(): pl.pallas_call(forecast_kernel, out_shape=(jax.ShapeDtypeStruct((groups *...  5.11 us
  transfers between devices with their start and end apart: 10, of which 5 were waited for; matrix products, arithmetic and copies ran while one was open for 0% of the time, Pallas kernels for 0%

profile of v3, /device:TPU:1, one launch (start us, length us, event | category | flops | bytes accessed | tf_op | source)
XLA Modules:
  0.0 155.4 jit_solution(12828711442064840196)
XLA Ops:
  0.0 0.0 copy-start.9
  0.0 0.0 copy-start.4
  0.0 0.0 copy-start.5
  0.0 0.0 copy-start.3
  0.0 0.0 copy-start.1
  0.0 0.0 copy-start.2
  0.0 0.6 copy-done.9
  0.7 0.1 copy.12.table
  0.8 0.1 pad_add_fusion.1.place
  0.8 0.0 copy-done.4
  0.9 0.0 copy-done.5
  0.9 0.0 copy-done.3
  0.9 0.0 copy-done.1
  0.9 0.0 copy-done.2
  0.9 0.0 copy-start
  0.9 1.2 copy-done
  2.1 5.1 %shard_map.100 = (f32[24,80,128]{2,1,0:T(8,128)S(1)}, f32[12,80,128]{2,1,0:T(8,128)}, f32[12,80,128]{2,1,0:T(8,128)}, f32[1024,128]{1,0:T(8,128)S(1)}, f32[1024,128]{1,0:T(8,128)S(1)}) custom-call(s32[4]{0:T(128)S(1)} %pad_add_fusion.1.place, f32[4,2]{1,0:T(4,128)S(1)} %copy.12.table, f32[80,3,2,4,128]{4,3,2,1,0:T(4,128)S(1)} %copy-done, ...), custom_call_target="tpu_custom_call" | custom-call | tf_op jit(solution)/shard_map/pallas_call | solution.py:314
  7.2 8.8 %collective-permute-start = (f32[1024,128]{1,0:T(8,128)S(1)}, f32[1024,128]{1,0:T(8,128)S(1)}, u32[]{:S(2)}, u32[]{:S(2)}) collective-permute-start(f32[1024,128]{1,0:T(8,128)S(1)} %get-tuple-element.14), channel_id=1, source_target_pairs={{0,4},{4,0},{1,5},{5,1},{2,6},{6,2},{3,7},{7,3},{8,12},{12,8},{9,1... | collective-permute-start | bytes 1572872 | tf_op jit(solution)/shard_map/ppermute | solution.py:389
  16.0 1.5 collective-permute-done
  17.5 0.1 add.12
  17.6 28.3 %all_to_all.10 = f32[64,16,128]{2,1,0:T(8,128)S(1)} all-to-all(f32[64,16,128]{2,1,0:T(8,128)S(1)} %bitcast.8), channel_id=1, replica_groups=mesh['z'=8,'y'=8,'core'=2,'x'=4] {'z','y'}, dimensions={0} | all-to-all | bytes 1048576 | tf_op jit(solution)/shard_map/all_to_all | solution.py:390
  45.9 0.1 reduce_sum.9
  46.0 22.8 %all_to_all.11 = f32[64,16,128]{2,1,0:T(8,128)S(1)} all-to-all(f32[64,16,128]{2,1,0:T(8,128)S(1)} %broadcast_in_dim.2), channel_id=1, replica_groups=mesh['z'=8,'y'=8,'core'=2,'x'=4] {'z','y'}, dimensions={0} | all-to-all | bytes 1048576 | tf_op jit(solution)/shard_map/all_to_all | solution.py:392
  68.9 6.1 %collective-permute-start.1 = (f32[1024,128]{1,0:T(8,128)S(1)}, f32[1024,128]{1,0:T(8,128)S(1)}, u32[]{:S(2)}, u32[]{:S(2)}) collective-permute-start(f32[1024,128]{1,0:T(8,128)S(1)} %bitcast.5), channel_id=1, source_target_pairs={{0,4},{4,0},{1,5},{5,1},{2,6},{6,2},{3,7},{7,3},{8,12},{12,8},{9,1... | collective-permute-start | bytes 1572872 | tf_op jit(solution)/shard_map/ppermute | solution.py:405
  74.9 4.4 %collective-permute-start.2 = (f32[1024,128]{1,0:T(8,128)S(1)}, f32[1024,128]{1,0:T(8,128)S(1)}, u32[]{:S(2)}, u32[]{:S(2)}) collective-permute-start(f32[1024,128]{1,0:T(8,128)S(1)} %bitcast.6), channel_id=1, source_target_pairs={{0,1},{1,2},{2,3},{3,0},{5,4},{6,5},{7,6},{4,7},{8,9},{9,10},{10,1... | collective-permute-start | bytes 1572872 | tf_op jit(solution)/shard_map/ppermute | solution.py:402
  79.3 0.0 collective-permute-done.1.refs_1_
  79.3 2.5 %collective-permute-start.3 = (f32[1024,128]{1,0:T(8,128)S(1)}, f32[1024,128]{1,0:T(8,128)S(1)}, u32[]{:S(2)}, u32[]{:S(2)}) collective-permute-start(f32[1024,128]{1,0:T(8,128)S(1)} %collective-permute-done.1.refs_1_), channel_id=1, source_target_pairs={{0,1},{1,2},{2,3},{3,0},{5,4},{6,5},{7,6},{4,7},{8,9},{9,10},{10,1... | collective-permute-start | bytes 1572872 | tf_op jit(solution)/shard_map/ppermute | solution.py:402
  81.8 3.6 %collective-permute-done.2.refs_2_ = f32[1024,128]{1,0:T(8,128)S(1)} collective-permute-done((f32[1024,128]{1,0:T(8,128)S(1)}, f32[1024,128]{1,0:T(8,128)S(1)}, u32[]{:S(2)}, u32[]{:S(2)}) %collective-permute-start.2) | collective-permute-done | bytes 524320 | tf_op jit(solution)/shard_map/ppermute | solution.py:402
  85.4 5.0 %collective-permute-start.4 = (f32[1024,128]{1,0:T(8,128)S(1)}, f32[1024,128]{1,0:T(8,128)}, u32[]{:S(2)}, u32[]{:S(2)}) collective-permute-start(f32[1024,128]{1,0:T(8,128)S(1)} %collective-permute-done.2.refs_2_), channel_id=1, source_target_pairs={{0,1},{1,2},{2,3},{3,0},{5,4},{6,5},{7,6},{4,7},{8,9},{9,10},{10,1... | collective-permute-start | bytes 1572872 | tf_op jit(solution)/shard_map/ppermute | solution.py:402
  90.5 1.9 %collective-permute-start.5 = (f32[1024,128]{1,0:T(8,128)S(1)}, f32[1024,128]{1,0:T(8,128)}, u32[]{:S(2)}, u32[]{:S(2)}) collective-permute-start(f32[1024,128]{1,0:T(8,128)S(1)} %collective-permute-done.2.refs_2_), channel_id=1, source_target_pairs={{0,4},{4,0},{1,5},{5,1},{2,6},{6,2},{3,7},{7,3},{8,12},{12,8},{9,1... | collective-permute-start | bytes 1572872 | tf_op jit(solution)/shard_map/ppermute | solution.py:405
  92.4 0.0 collective-permute-done.3.refs_3_
  92.4 4.3 %collective-permute-done.4.refs_4_ = f32[1024,128]{1,0:T(8,128)} collective-permute-done((f32[1024,128]{1,0:T(8,128)S(1)}, f32[1024,128]{1,0:T(8,128)}, u32[]{:S(2)}, u32[]{:S(2)}) %collective-permute-start.4) | collective-permute-done | bytes 524320 | tf_op jit(solution)/shard_map/ppermute | solution.py:402
  96.7 4.8 %collective-permute-start.7 = (f32[1024,128]{1,0:T(8,128)}, f32[1024,128]{1,0:T(8,128)}, u32[]{:S(2)}, u32[]{:S(2)}) collective-permute-start(f32[1024,128]{1,0:T(8,128)} %collective-permute-done.4.refs_4_), channel_id=1, source_target_pairs={{0,4},{4,0},{1,5},{5,1},{2,6},{6,2},{3,7},{7,3},{8,12},{12,8},{9,1... | collective-permute-start | bytes 1572872 | tf_op jit(solution)/shard_map/ppermute | solution.py:405
  101.5 1.9 %collective-permute-start.6 = (f32[1024,128]{1,0:T(8,128)S(1)}, f32[1024,128]{1,0:T(8,128)}, u32[]{:S(2)}, u32[]{:S(2)}) collective-permute-start(f32[1024,128]{1,0:T(8,128)S(1)} %collective-permute-done.3.refs_3_), channel_id=1, source_target_pairs={{0,4},{4,0},{1,5},{5,1},{2,6},{6,2},{3,7},{7,3},{8,12},{12,8},{9,1... | collective-permute-start | bytes 1572872 | tf_op jit(solution)/shard_map/ppermute | solution.py:405
  103.4 3.4 %collective-permute-start.8 = (f32[12,80,128]{2,1,0:T(8,128)}, f32[12,80,128]{2,1,0:T(8,128)}, u32[]{:S(2)}, u32[]{:S(2)}) collective-permute-start(f32[12,80,128]{2,1,0:T(8,128)} %get-tuple-element.19), channel_id=1, source_target_pairs={{0,4},{4,8},{8,12},{12,16},{16,20},{20,24},{24,28},{28,32},{32,36}... | collective-permute-start | bytes 1474568 | tf_op jit(solution)/shard_map/ppermute | solution.py:416
  106.9 1.9 %collective-permute-start.9 = (f32[12,80,128]{2,1,0:T(8,128)}, f32[12,80,128]{2,1,0:T(8,128)}, u32[]{:S(2)}, u32[]{:S(2)}) collective-permute-start(f32[12,80,128]{2,1,0:T(8,128)} %get-tuple-element.20), channel_id=1, source_target_pairs={{4,0},{8,4},{12,8},{16,12},{20,16},{24,20},{28,24},{32,28},{36,32}... | collective-permute-start | bytes 1474568 | tf_op jit(solution)/shard_map/ppermute | solution.py:417
  108.8 0.0 copy-start.6
  108.8 0.7 copy-done.6
  109.5 0.0 copy-start.7
  109.5 0.7 copy-done.7
  110.2 0.0 copy-start.8
  110.2 0.7 copy-done.8
  111.0 0.1 stack.48.info
  111.1 0.1 pad_add_fusion.place
  111.1 0.0 collective-permute-done.5.refs_5_
  111.1 1.8 %collective-permute-done.8.refs_9_ = f32[12,80,128]{2,1,0:T(8,128)} collective-permute-done((f32[12,80,128]{2,1,0:T(8,128)}, f32[12,80,128]{2,1,0:T(8,128)}, u32[]{:S(2)}, u32[]{:S(2)}) %collective-permute-start.8) | collective-permute-done | bytes 491552 | tf_op jit(solution)/shard_map/ppermute | solution.py:416
  112.9 4.4 %collective-permute-done.9.refs_10_ = f32[12,80,128]{2,1,0:T(8,128)} collective-permute-done((f32[12,80,128]{2,1,0:T(8,128)}, f32[12,80,128]{2,1,0:T(8,128)}, u32[]{:S(2)}, u32[]{:S(2)}) %collective-permute-start.9) | collective-permute-done | bytes 491552 | tf_op jit(solution)/shard_map/ppermute | solution.py:417
  117.3 0.0 collective-permute-done.7.refs_7_
  117.4 0.0 collective-permute-done.6.refs_6_
  117.4 38.1 %shard_map.101 = f32[80,3,2,4,128]{4,3,2,1,0:T(4,128)} custom-call(s32[2]{0:T(128)S(1)} %pad_add_fusion.place, f32[4,2]{1,0:T(4,128)S(1)} %copy.12.table, f32[12,8,128]{2,1,0:T(8,128)S(1)} %stack.48.info, f32[1024,128]{1,0:T(8,128)S(1)} %bitcast.7, f32[1024,128]{1,0:T(8,128)S(1)} %collective-permute-done.1.refs_1_, ...), custom_call_target="tpu_custom_call" | custom-call | tf_op jit(solution)/shard_map/pallas_call | solution.py:341
  (11 shorter events, 0.1 us)
Async XLA Ops:
  0.0 0.7 copy-start.9
  0.0 0.8 copy-start.4
  0.0 0.8 copy-start.5
  0.0 0.8 copy-start.3
  0.0 0.8 copy-start.1
  0.0 0.8 copy-start.2
  0.9 1.2 copy-start
  7.2 10.3 %collective-permute-start = (f32[1024,128]{1,0:T(8,128)S(1)}, f32[1024,128]{1,0:T(8,128)S(1)}, u32[]{:S(2)}, u32[]{:S(2)}) collective-permute-start(f32[1024,128]{1,0:T(8,128)S(1)} %get-tuple-element.14), channel_id=1, source_target_pairs={{0,4},{4,0},{1,5},{5,1},{2,6},{6,2},{3,7},{7,3},{8,12},{12,8},{9,1... | collective-permute-start | bytes 1572872 | tf_op jit(solution)/shard_map/ppermute | solution.py:389
  68.9 10.5 %collective-permute-start.1 = (f32[1024,128]{1,0:T(8,128)S(1)}, f32[1024,128]{1,0:T(8,128)S(1)}, u32[]{:S(2)}, u32[]{:S(2)}) collective-permute-start(f32[1024,128]{1,0:T(8,128)S(1)} %bitcast.5), channel_id=1, source_target_pairs={{0,4},{4,0},{1,5},{5,1},{2,6},{6,2},{3,7},{7,3},{8,12},{12,8},{9,1... | collective-permute-start | bytes 1572872 | tf_op jit(solution)/shard_map/ppermute | solution.py:405
  74.9 10.5 %collective-permute-start.2 = (f32[1024,128]{1,0:T(8,128)S(1)}, f32[1024,128]{1,0:T(8,128)S(1)}, u32[]{:S(2)}, u32[]{:S(2)}) collective-permute-start(f32[1024,128]{1,0:T(8,128)S(1)} %bitcast.6), channel_id=1, source_target_pairs={{0,1},{1,2},{2,3},{3,0},{5,4},{6,5},{7,6},{4,7},{8,9},{9,10},{10,1... | collective-permute-start | bytes 1572872 | tf_op jit(solution)/shard_map/ppermute | solution.py:402
  79.3 13.0 %collective-permute-start.3 = (f32[1024,128]{1,0:T(8,128)S(1)}, f32[1024,128]{1,0:T(8,128)S(1)}, u32[]{:S(2)}, u32[]{:S(2)}) collective-permute-start(f32[1024,128]{1,0:T(8,128)S(1)} %collective-permute-done.1.refs_1_), channel_id=1, source_target_pairs={{0,1},{1,2},{2,3},{3,0},{5,4},{6,5},{7,6},{4,7},{8,9},{9,10},{10,1... | collective-permute-start | bytes 1572872 | tf_op jit(solution)/shard_map/ppermute | solution.py:402
  85.4 11.2 %collective-permute-start.4 = (f32[1024,128]{1,0:T(8,128)S(1)}, f32[1024,128]{1,0:T(8,128)}, u32[]{:S(2)}, u32[]{:S(2)}) collective-permute-start(f32[1024,128]{1,0:T(8,128)S(1)} %collective-permute-done.2.refs_2_), channel_id=1, source_target_pairs={{0,1},{1,2},{2,3},{3,0},{5,4},{6,5},{7,6},{4,7},{8,9},{9,10},{10,1... | collective-permute-start | bytes 1572872 | tf_op jit(solution)/shard_map/ppermute | solution.py:402
  90.5 20.7 %collective-permute-start.5 = (f32[1024,128]{1,0:T(8,128)S(1)}, f32[1024,128]{1,0:T(8,128)}, u32[]{:S(2)}, u32[]{:S(2)}) collective-permute-start(f32[1024,128]{1,0:T(8,128)S(1)} %collective-permute-done.2.refs_2_), channel_id=1, source_target_pairs={{0,4},{4,0},{1,5},{5,1},{2,6},{6,2},{3,7},{7,3},{8,12},{12,8},{9,1... | collective-permute-start | bytes 1572872 | tf_op jit(solution)/shard_map/ppermute | solution.py:405
  96.7 20.7 %collective-permute-start.7 = (f32[1024,128]{1,0:T(8,128)}, f32[1024,128]{1,0:T(8,128)}, u32[]{:S(2)}, u32[]{:S(2)}) collective-permute-start(f32[1024,128]{1,0:T(8,128)} %collective-permute-done.4.refs_4_), channel_id=1, source_target_pairs={{0,4},{4,0},{1,5},{5,1},{2,6},{6,2},{3,7},{7,3},{8,12},{12,8},{9,1... | collective-permute-start | bytes 1572872 | tf_op jit(solution)/shard_map/ppermute | solution.py:405
  101.5 15.8 %collective-permute-start.6 = (f32[1024,128]{1,0:T(8,128)S(1)}, f32[1024,128]{1,0:T(8,128)}, u32[]{:S(2)}, u32[]{:S(2)}) collective-permute-start(f32[1024,128]{1,0:T(8,128)S(1)} %collective-permute-done.3.refs_3_), channel_id=1, source_target_pairs={{0,4},{4,0},{1,5},{5,1},{2,6},{6,2},{3,7},{7,3},{8,12},{12,8},{9,1... | collective-permute-start | bytes 1572872 | tf_op jit(solution)/shard_map/ppermute | solution.py:405
  103.4 9.5 %collective-permute-start.8 = (f32[12,80,128]{2,1,0:T(8,128)}, f32[12,80,128]{2,1,0:T(8,128)}, u32[]{:S(2)}, u32[]{:S(2)}) collective-permute-start(f32[12,80,128]{2,1,0:T(8,128)} %get-tuple-element.19), channel_id=1, source_target_pairs={{0,4},{4,8},{8,12},{12,16},{16,20},{20,24},{24,28},{28,32},{32,36}... | collective-permute-start | bytes 1474568 | tf_op jit(solution)/shard_map/ppermute | solution.py:416
  106.9 10.5 %collective-permute-start.9 = (f32[12,80,128]{2,1,0:T(8,128)}, f32[12,80,128]{2,1,0:T(8,128)}, u32[]{:S(2)}, u32[]{:S(2)}) collective-permute-start(f32[12,80,128]{2,1,0:T(8,128)} %get-tuple-element.20), channel_id=1, source_target_pairs={{4,0},{8,4},{12,8},{16,12},{20,16},{24,20},{28,24},{32,28},{36,32}... | collective-permute-start | bytes 1474568 | tf_op jit(solution)/shard_map/ppermute | solution.py:417
  108.8 0.7 copy-start.6
  109.5 0.7 copy-start.7
  110.2 0.7 copy-start.8

commit v4 on v2

--- a/solution.py
+++ b/solution.py
@@ -137,7 +137,7 @@
 def analysis_kernel(count, place, table, info, *refs):
     arrived, rest = refs[:count], refs[count:]
     grid, from_left, from_right, out = rest[:4]
-    local, remote, edges, spread_rows, spread_cols, vertical, sems = rest[4:]
+    local, remote, edges, spread_rows, spread_cols, vertical, position, sems = rest[4:]
     all_levels, length, _ = remote.shape
     slabs, members, rows = grid.shape
     fields, levels, columns = out.shape[1], out.shape[2], out.shape[3]
@@ -147,13 +147,11 @@
     classes = table.shape[0]
     first = place[0].astype(jnp.float32)
     incoming = []
-    level, at = 0, 0
+    level = 0
     for ref in arrived:
-        size = ref.shape[0]
-        incoming.append((ref, remote.at[level, at : at + size]))
-        at += size
-        if at == length:
-            level, at = level + 1, 0
+        for at in range(0, ref.shape[0], length):
+            incoming.append((ref.at[at : at + length], remote.at[level]))
+            level += 1
     incoming += [(grid, local), (from_left, edges.at[0]), (from_right, edges.at[1])]
     incoming = [
         pltpu.make_async_copy(ref, target, sems.at[slabs + n])
@@ -170,27 +168,37 @@
             local[east] = local[east] + edges[1, g * 2 + k]
     inverse = 1.0 / total_cols
 
-    def update(x, weight):
+    def widen(x):
         high, low = halves(x)
-        covariance = jnp.dot(
-            spread_cols[...],
-            jnp.concatenate([high, high, low], axis=0),
+        return jnp.concatenate([high, high, low], axis=0)
+
+    def spread_out(turn, weighted):
+        change = jnp.dot(
+            spread_rows[turn],
+            jnp.concatenate(halves(weighted), axis=0),
             preferred_element_type=jnp.float32,
         )
-        change = jnp.dot(
-            spread_rows[...],
-            jnp.concatenate(halves(covariance * weight), axis=0),
-            preferred_element_type=jnp.float32,
-        )
-        return x + (change[:members] + change[members:])
-
-    def batch(b, carry):
-        mine = pl.ds(pl.multiple_of(b * members, 8), members)
-        facts = info[b]
-        priors = remote[0, mine, :]
-        for level in range(1, all_levels):
-            priors = priors + remote[level, mine, :]
-        priors = priors * (1.0 / all_levels)
+        return change[:members] + change[members:]
+
+    def covariance(turn, x):
+        return jnp.dot(spread_cols[turn], widen(x), preferred_element_type=jnp.float32)
+
+    def update(turn, x, weight):
+        return x + spread_out(turn, covariance(turn, x) * weight)
+
+    def rows_of(c):
+        return pl.ds(pl.multiple_of(c * members, 8), members)
+
+    def taper_to(turn, c):
+        there = info[c]
+        d_col = (there[0:1] - position[turn, 0]) * inverse
+        d_row = (there[1:2] - position[turn, 1]) * (1.0 / RADY)
+        radial = jnp.maximum(1.0 - d_col * d_col - d_row * d_row, 0.0)
+        return radial * radial
+
+    def analyse(turn, c, total):
+        facts = info[c]
+        priors = total * (1.0 / all_levels)
         average = jnp.sum(priors, axis=0, keepdims=True) * (1.0 / members)
         spread = priors - average
         variance = jnp.sum(spread * spread, axis=0, keepdims=True) / (members - 1) + EPSILON
@@ -201,21 +209,23 @@
         increments = shrink * (facts[3:4] - average) + (factor - 1.0) * spread
         regress = spread / ((members - 1) * variance)
         high, low = halves(increments)
-        spread_rows[:members, :LANES] = high
-        spread_rows[:members, LANES:] = high
-        spread_rows[members:, :LANES] = low
-        spread_rows[members:, LANES:] = jnp.zeros_like(low)
+        spread_rows[turn, :members, :LANES] = high
+        spread_rows[turn, :members, LANES:] = high
+        spread_rows[turn, members:, :LANES] = low
+        spread_rows[turn, members:, LANES:] = jnp.zeros_like(low)
         high = regress.astype(jnp.bfloat16).astype(jnp.float32)
         low = regress - high
         stacked = jnp.concatenate(
             [high, low, high, jnp.zeros((256 - 3 * members, LANES), jnp.float32)], axis=0
         )
-        spread_cols[...] = jnp.transpose(stacked)[:, : 3 * members].astype(jnp.bfloat16)
+        spread_cols[turn] = jnp.transpose(stacked)[:, : 3 * members].astype(jnp.bfloat16)
 
         def column_of(k):
             return jnp.transpose(jnp.broadcast_to(facts[k : k + 1], (LANES, LANES)))
 
-        obs_col, obs_row, obs_class = column_of(0), column_of(1), column_of(2)
+        position[turn, 0] = column_of(0)
+        position[turn, 1] = column_of(1)
+        obs_class = column_of(2)
         for level in range(all_levels + levels):
             if level < all_levels:
                 row = remote[level, batches * members : batches * members + 8, :]
@@ -227,65 +237,74 @@
             chosen = jnp.zeros((LANES, LANES), jnp.float32) + weights[classes - 1]
             for k in range(classes - 1):
                 chosen = jnp.where(obs_class == float(k), weights[k], chosen)
-            vertical[level] = chosen
-
-        def later_many(c0, many):
-            xs, ws, keep = [], [], []
-            for k in range(many):
-                c = c0 + k
-                theirs = pl.ds(pl.multiple_of(c * members, 8), members)
-                there = info[c]
-                d_col = (there[0:1] - obs_col) * inverse
-                d_row = (there[1:2] - obs_row) * (1.0 / RADY)
-                radial = jnp.maximum(1.0 - d_col * d_col - d_row * d_row, 0.0)
-                taper = radial * radial
-                for g in range(all_levels):
-                    xs.append(remote[g, theirs, :])
-                    ws.append(taper * vertical[g])
-                    keep.append((g, theirs))
-            x = update(jnp.concatenate(xs, axis=1), jnp.concatenate(ws, axis=1))
-            for n, (g, theirs) in enumerate(keep):
-                remote[g, theirs, :] = x[:, n * LANES : (n + 1) * LANES]
-
-        count = batches - 1 - b
-
-        for size in (1, 2):
-
-            @pl.when((count // size) % 2 == 1)
-            def _():
-                later_many(b + 1 + (count % size), size)
-
-        start = b + 1 + count % 4
-
-        def four(i, carry):
-            later_many(start + 4 * i, 4)
-            return carry
-
-        lax.fori_loop(0, count // 4, four, 0)
+            vertical[turn, level] = chosen
+
+    def batch(b, carry):
+        turn = b % 2
+        soon = jnp.minimum(b + 1, batches - 1)
+        xs = [remote[g, rows_of(soon), :] for g in range(all_levels)]
+        linked = covariance(turn, jnp.concatenate(xs, axis=1))
+        weighted = linked[:, :LANES] * vertical[turn, 0]
+        total = xs[0]
+        for g in range(1, all_levels):
+            weighted = weighted + linked[:, g * LANES : (g + 1) * LANES] * vertical[turn, g]
+            total = total + xs[g]
+        total = total + spread_out(turn, weighted * taper_to(turn, soon))
+
         lane = lax.broadcasted_iota(jnp.int32, (1, LANES), 1).astype(jnp.float32)
-        d_row = (lane - obs_row) * (1.0 / RADY)
+        d_row = (lane - position[turn, 1]) * (1.0 / RADY)
         across = 1.0 - d_row * d_row
-        along = (first - obs_col) * inverse
-        xs, ws = [], []
+        along = (first - position[turn, 0]) * inverse
+        ats, ws = [], []
         for k in range(columns):
             d_col = along + k * inverse
             radial = jnp.maximum(across - d_col * d_col, 0.0)
             taper = radial * radial
             for level in range(levels):
-                weight = taper * vertical[all_levels + level]
+                weight = taper * vertical[turn, all_levels + level]
                 for f in range(fields):
-                    xs.append((f * levels + level) * columns + k)
+                    ats.append((f * levels + level) * columns + k)
                     ws.append(weight)
-        step = 24
-        for n in range(0, len(xs), step):
-            x = update(
-                jnp.concatenate([local[at] for at in xs[n : n + step]], axis=1),
-                jnp.concatenate(ws[n : n + step], axis=1),
-            )
-            for i, at in enumerate(xs[n : n + step]):
-                local[at] = x[:, i * LANES : (i + 1) * LANES]
+        x = jnp.concatenate([local[at] for at in ats], axis=1)
+        x = update(turn, x, jnp.concatenate(ws, axis=1))
+        for i, at in enumerate(ats):
+            local[at] = x[:, i * LANES : (i + 1) * LANES]
+        analyse(1 - turn, soon, total)
+
+        def later_many(c0, many):
+            xs, ws, keep = [], [], []
+            for k in range(many):
+                theirs = rows_of(c0 + k)
+                taper = taper_to(turn, c0 + k)
+                for g in range(all_levels):
+                    xs.append(remote[g, theirs, :])
+                    ws.append(taper * vertical[turn, g])
+                    keep.append((g, theirs))
+            x = update(turn, jnp.concatenate(xs, axis=1), jnp.concatenate(ws, axis=1))
+            for n, (g, theirs) in enumerate(keep):
+                remote[g, theirs, :] = x[:, n * LANES : (n + 1) * LANES]
+
+        count = jnp.maximum(batches - 2 - b, 0)
+
+        for size in (1, 2):
+
+            @pl.when((count // size) % 2 == 1)
+            def _():
+                later_many(b + 2 + (count % size), size)
+
+        start = b + 2 + count % 4
+
+        def four(i, carry):
+            later_many(start + 4 * i, 4)
+            return carry
+
+        lax.fori_loop(0, count // 4, four, 0)
         return carry
 
+    total = remote[0, 0:members, :]
+    for level in range(1, all_levels):
+        total = total + remote[level, 0:members, :]
+    analyse(0, 0, total)
     lax.fori_loop(0, batches, batch, 0)
     outgoing = []
     for f in range(fields):
@@ -347,12 +366,13 @@
             pltpu.VMEM(grid.shape, jnp.float32),
             pltpu.VMEM((all_levels, length, LANES), jnp.float32),
             pltpu.VMEM((2,) + from_left.shape, jnp.float32),
-            pltpu.VMEM((2 * members, 2 * LANES), jnp.bfloat16),
-            pltpu.VMEM((LANES, 3 * members), jnp.bfloat16),
-            pltpu.VMEM((all_levels + levels, LANES, LANES), jnp.float32),
-            pltpu.SemaphoreType.DMA((grid.shape[0] + len(arrived) + 3,)),
+            pltpu.VMEM((2, 2 * members, 2 * LANES), jnp.bfloat16),
+            pltpu.VMEM((2, LANES, 3 * members), jnp.bfloat16),
+            pltpu.VMEM((2, all_levels + levels, LANES, LANES), jnp.float32),
+            pltpu.VMEM((2, 2, LANES, LANES), jnp.float32),
+            pltpu.SemaphoreType.DMA((grid.shape[0] + all_levels + 3,)),
         ],
-        compiler_params=pltpu.CompilerParams(vmem_limit_bytes=48 * 2**20),
+        compiler_params=pltpu.CompilerParams(vmem_limit_bytes=60 * 2**20),
     )(place, table, info, *arrived, grid, from_left, from_right)
 
 
@@ -394,20 +414,25 @@
     )
     mine = mine.reshape(length, LANES)
 
-    mine, to_left, to_right = lax.optimization_barrier((mine, to_left, to_right))
     ring = lax.axis_size("x")
     right = [(i, (i + 1) % ring) for i in range(ring)]
     left = [(j, i) for i, j in right]
+    up = [(i, i + 1) for i in range(tiles - 1)]
+    down = [(j, i) for i, j in up]
+    mine, to_left, to_right = lax.optimization_barrier((mine, to_left, to_right))
     before = lax.ppermute(mine, "x", right)
     after = lax.ppermute(mine, "x", left)
+    from_left = lax.ppermute(to_right, TILES, up)
+    from_right = lax.ppermute(to_left, TILES, down)
+    before, after, from_left, from_right = lax.optimization_barrier(
+        (before, after, from_left, from_right)
+    )
     across_a = lax.ppermute(after[: length // 2], "x", left)
     across_b = lax.ppermute(before[length // 2 :], "x", right)
-    parts = [mine, before, after, across_a, across_b]
-    arrived = parts + [lax.ppermute(part, "core", swap) for part in parts]
-    up = [(i, i + 1) for i in range(tiles - 1)]
-    down = [(j, i) for i, j in up]
-    from_left = lax.ppermute(to_right, TILES, up)
-    from_right = lax.ppermute(to_left, TILES, down)
+    near = jnp.concatenate([mine, before, after], axis=0)
+    across = jnp.concatenate([across_a, across_b], axis=0)
+    arrived = [near, across]
+    arrived += [lax.ppermute(part, "core", swap) for part in (near, across)]
 
     as_float = [v.astype(jnp.float32) for v in (obs_col, obs_row, obs_class)]
     blank = jnp.zeros_like(obs_value)

time: 148 us -> 154 us (1.041)
  waiting for transfers between devices: 1.54 us -> 17.8 us
  starting transfers between devices: 43.2 us -> 35.7 us
  Pallas kernels: 41.8 us -> 39 us
    ppermute x5 -> x2, starting transfers between devices: 12.2 us -> 5.63 us  [shards(): arrived += [lax.ppermute(part, 'core', swap) for part in (near, across)]]
    ppermute x1, waiting for transfers between devices: 0.01 us -> 4.39 us  [shards(): from_right = lax.ppermute(to_left, TILES, down)]
    ppermute x1, waiting for transfers between devices: 0.01 us -> 4.1 us  [shards(): across_b = lax.ppermute(before[length // 2:], 'x', right)]
    ppermute x1, waiting for transfers between devices: 0.01 us -> 3.92 us  [shards(): across_a = lax.ppermute(after[:length // 2], 'x', left)]
    ppermute x1, waiting for transfers between devices: 0.01 us -> 3.78 us  [shards(): from_left = lax.ppermute(to_right, TILES, up)]
    pallas_call x1, Pallas kernels: 37.6 us -> 34.8 us  [assimilate(): pl.pallas_call(functools.partial(analysis_kernel, len(arrived)), out_shap...]
    ppermute x1, starting transfers between devices: 4.85 us -> 3.18 us  [shards(): across_a = lax.ppermute(after[:length // 2], 'x', left)]
    unnamed x37 -> x40, local copies, waits for them, and re-layouts: 7.64 us -> 7.27 us
  transfers between devices with their start and end apart: 12 -> 9, of which waited for: 1 -> 6; matrix products, arithmetic and copies ran while one was open for 0% -> 1% of each run, Pallas kernels for 0% -> 0%
where the time goes in v4:
time: 154 us; the launch traced here: 153 us
  blocking collectives  51.2 us (33%)
  Pallas kernels  39 us (25%)
  starting transfers between devices  35.7 us (23%)
  waiting for transfers between devices  17.8 us (12%)
  local copies, waits for them, and re-layouts  8.12 us (5%)
    pallas_call x1, Pallas kernels, assimilate(): pl.pallas_call(functools.partial(analysis_kernel, len(arrived)), out_shap...  34.8 us
    all_to_all x1, blocking collectives, shards(): lax.all_to_all(mine.reshape(homes, chunk, LANES), ('z', 'y'), 0, 0, tiled...  28.3 us
    all_to_all x1, blocking collectives, shards(): lax.all_to_all(jnp.broadcast_to(mine[None], (homes, chunk, LANES)), ('z',...  22.8 us
    ppermute x1, starting transfers between devices, shards(): mine = mine + lax.ppermute(other, 'core', swap)  8.77 us
    ppermute x1, starting transfers between devices, shards(): from_left = lax.ppermute(to_right, TILES, up)  7.65 us
    unnamed x40, local copies, waits for them, and re-layouts  7.27 us
    ppermute x2, starting transfers between devices, shards(): arrived += [lax.ppermute(part, 'core', swap) for part in (near, across)]  5.63 us
    ppermute x1, waiting for transfers between devices, shards(): from_right = lax.ppermute(to_left, TILES, down)  4.39 us
  transfers between devices with their start and end apart: 9, of which 6 were waited for; matrix products, arithmetic and copies ran while one was open for 1% of the time, Pallas kernels for 0%

profile of v4, /device:TPU:1, one launch (start us, length us, event | category | flops | bytes accessed | tf_op | source)
XLA Modules:
  0.0 152.9 jit_solution(11328969268942764947)
XLA Ops:
  0.0 0.8 copy.12.table
  0.8 0.0 copy-start.6
  0.8 0.1 pad_add_fusion.1.place
  0.8 0.0 copy-start
  0.8 1.2 copy-done
  2.0 0.0 copy-start.2
  2.0 0.7 copy-done.2
  2.7 0.0 copy-start.4
  2.7 0.7 copy-done.4
  3.4 0.0 copy-start.7
  3.4 0.7 copy-done.7
  4.1 0.0 copy-start.8
  4.1 0.7 copy-done.8
  4.8 0.0 copy-start.9
  4.8 0.7 copy-done.9
  5.5 4.1 %shard_map.100 = (f32[24,80,128]{2,1,0:T(8,128)S(1)}, f32[12,80,128]{2,1,0:T(8,128)S(1)}, f32[12,80,128]{2,1,0:T(8,128)S(1)}, f32[1024,128]{1,0:T(8,128)S(1)}, f32[1024,128]{1,0:T(8,128)S(1)}) custom-call(s32[4]{0:T(128)S(1)} %pad_add_fusion.1.place, f32[4,2]{1,0:T(4,128)S(1)} %copy.12.table, f32[80,3,2,4,128]{4,3,2,1,0:T(4,128)S(1)} %copy-done, ...), custom_call_target="tpu_custom_call" | custom-call | tf_op jit(solution)/shard_map/pallas_call | solution.py:333
  9.6 0.0 copy-start.1
  9.7 0.9 copy-done.1
  10.6 8.8 %collective-permute-start = (f32[1024,128]{1,0:T(8,128)S(1)}, f32[1024,128]{1,0:T(8,128)S(1)}, u32[]{:S(2)}, u32[]{:S(2)}) collective-permute-start(f32[1024,128]{1,0:T(8,128)S(1)} %get-tuple-element.18), channel_id=1, source_target_pairs={{0,4},{4,0},{1,5},{5,1},{2,6},{6,2},{3,7},{7,3},{8,12},{12,8},{9,1... | collective-permute-start | bytes 1572872 | tf_op jit(solution)/shard_map/ppermute | solution.py:409
  19.4 1.5 collective-permute-done
  20.9 0.1 add.12
  20.9 28.3 %all_to_all.10 = f32[64,16,128]{2,1,0:T(8,128)S(1)} all-to-all(f32[64,16,128]{2,1,0:T(8,128)S(1)} %bitcast.5), channel_id=1, replica_groups=mesh['z'=8,'y'=8,'core'=2,'x'=4] {'z','y'}, dimensions={0} | all-to-all | bytes 1048576 | tf_op jit(solution)/shard_map/all_to_all | solution.py:410
  49.3 0.0 copy-done.6
  49.3 0.1 reduce_sum.9
  49.4 22.8 %all_to_all.11 = f32[64,16,128]{2,1,0:T(8,128)S(1)} all-to-all(f32[64,16,128]{2,1,0:T(8,128)S(1)} %broadcast_in_dim.2), channel_id=1, replica_groups=mesh['z'=8,'y'=8,'core'=2,'x'=4] {'z','y'}, dimensions={0} | all-to-all | bytes 1048576 | tf_op jit(solution)/shard_map/all_to_all | solution.py:412
  72.2 3.1 %collective-permute-start.1 = (f32[1024,128]{1,0:T(8,128)S(1)}, f32[1024,128]{1,0:T(8,128)S(1)}, u32[]{:S(2)}, u32[]{:S(2)}) collective-permute-start(f32[1024,128]{1,0:T(8,128)S(1)} %bitcast.6), channel_id=1, source_target_pairs={{0,1},{1,2},{2,3},{3,0},{4,5},{5,6},{6,7},{7,4},{8,9},{9,10},{10,1... | collective-permute-start | bytes 1572872 | tf_op jit(solution)/shard_map/ppermute | solution.py:423
  75.3 3.4 %collective-permute-start.2 = (f32[1024,128]{1,0:T(8,128)S(1)}, f32[1024,128]{1,0:T(8,128)S(1)}, u32[]{:S(2)}, u32[]{:S(2)}) collective-permute-start(f32[1024,128]{1,0:T(8,128)S(1)} %bitcast.7), channel_id=1, source_target_pairs={{1,0},{2,1},{3,2},{0,3},{5,4},{6,5},{7,6},{4,7},{9,8},{10,9},{11,1... | collective-permute-start | bytes 1572872 | tf_op jit(solution)/shard_map/ppermute | solution.py:424
  78.7 7.6 %collective-permute-start.3 = (f32[12,80,128]{2,1,0:T(8,128)S(1)}, f32[12,80,128]{2,1,0:T(8,128)S(1)}, u32[]{:S(2)}, u32[]{:S(2)}) collective-permute-start(f32[12,80,128]{2,1,0:T(8,128)S(1)} %get-tuple-element.22), channel_id=1, source_target_pairs={{0,4},{4,8},{8,12},{12,16},{16,20},{20,24},{24,28},{28,32},{32,36}... | collective-permute-start | bytes 1474568 | tf_op jit(solution)/shard_map/ppermute | solution.py:425
  86.4 1.9 %collective-permute-start.4 = (f32[12,80,128]{2,1,0:T(8,128)S(1)}, f32[12,80,128]{2,1,0:T(8,128)S(1)}, u32[]{:S(2)}, u32[]{:S(2)}) collective-permute-start(f32[12,80,128]{2,1,0:T(8,128)S(1)} %get-tuple-element.23), channel_id=1, source_target_pairs={{4,0},{8,4},{12,8},{16,12},{20,16},{24,20},{28,24},{32,28},{36,32}... | collective-permute-start | bytes 1474568 | tf_op jit(solution)/shard_map/ppermute | solution.py:426
  88.3 3.8 %collective-permute-done.3.refs_5_ = f32[12,80,128]{2,1,0:T(8,128)S(1)} collective-permute-done((f32[12,80,128]{2,1,0:T(8,128)S(1)}, f32[12,80,128]{2,1,0:T(8,128)S(1)}, u32[]{:S(2)}, u32[]{:S(2)}) %collective-permute-start.3) | collective-permute-done | bytes 491552 | tf_op jit(solution)/shard_map/ppermute | solution.py:425
  92.1 0.0 copy-start.13
  92.1 4.4 %collective-permute-done.4.refs_6_ = f32[12,80,128]{2,1,0:T(8,128)S(1)} collective-permute-done((f32[12,80,128]{2,1,0:T(8,128)S(1)}, f32[12,80,128]{2,1,0:T(8,128)S(1)}, u32[]{:S(2)}, u32[]{:S(2)}) %collective-permute-start.4) | collective-permute-done | bytes 491552 | tf_op jit(solution)/shard_map/ppermute | solution.py:426
  96.5 0.0 copy-start.14
  96.5 0.0 collective-permute-done.1
  96.5 0.0 collective-permute-done.2
  96.6 0.0 copy-start.3
  96.6 0.0 copy-start.5
  96.6 0.0 copy-start.17
  96.6 0.0 copy-start.15
  96.6 0.0 copy-start.16
  96.7 0.0 copy-start.10
  96.7 2.1 %collective-permute-start.7 = (f32[3072,128]{1,0:T(8,128)S(1)}, f32[3072,128]{1,0:T(8,128)}, u32[]{:S(2)}, u32[]{:S(2)}) collective-permute-start(f32[3072,128]{1,0:T(8,128)S(1)} %constant_dynamic-update-slice_fusion.refs_0_), channel_id=1, source_target_pairs={{0,4},{4,0},{1,5},{5,1},{2,6},{6,2},{3,7},{7,3},{8,12},{12,8},{9,1... | collective-permute-start | bytes 4718600 | tf_op jit(solution)/shard_map/ppermute | solution.py:435
  98.8 3.2 %collective-permute-start.5 = (f32[512,128]{1,0:T(8,128)S(1)}, f32[512,128]{1,0:T(8,128)S(1)}, u32[]{:S(2)}, u32[]{:S(2)}) collective-permute-start(f32[512,128]{1,0:T(8,128)S(1)} %slice.6), channel_id=1, source_target_pairs={{1,0},{2,1},{3,2},{0,3},{5,4},{6,5},{7,6},{4,7},{9,8},{10,9},{11,1... | collective-permute-start | bytes 786440 | tf_op jit(solution)/shard_map/ppermute | solution.py:430
  102.0 0.0 copy-done.13
  102.0 0.0 copy-done.14
  102.0 2.1 %collective-permute-start.6 = (f32[512,128]{1,0:T(8,128)S(1)}, f32[512,128]{1,0:T(8,128)S(1)}, u32[]{:S(2)}, u32[]{:S(2)}) collective-permute-start(f32[512,128]{1,0:T(8,128)S(1)} %slice.7), channel_id=1, source_target_pairs={{0,1},{1,2},{2,3},{3,0},{4,5},{5,6},{6,7},{7,4},{8,9},{9,10},{10,1... | collective-permute-start | bytes 786440 | tf_op jit(solution)/shard_map/ppermute | solution.py:431
  104.1 3.9 %collective-permute-done.5 = f32[512,128]{1,0:T(8,128)S(1)} collective-permute-done((f32[512,128]{1,0:T(8,128)S(1)}, f32[512,128]{1,0:T(8,128)S(1)}, u32[]{:S(2)}, u32[]{:S(2)}) %collective-permute-start.5) | collective-permute-done | bytes 262176 | tf_op jit(solution)/shard_map/ppermute | solution.py:430
  108.1 4.1 %collective-permute-done.6 = f32[512,128]{1,0:T(8,128)S(1)} collective-permute-done((f32[512,128]{1,0:T(8,128)S(1)}, f32[512,128]{1,0:T(8,128)S(1)}, u32[]{:S(2)}, u32[]{:S(2)}) %collective-permute-start.6) | collective-permute-done | bytes 262176 | tf_op jit(solution)/shard_map/ppermute | solution.py:431
  112.2 0.0 copy-start.11
  112.2 3.6 %collective-permute-start.8 = (f32[1024,128]{1,0:T(8,128)S(1)}, f32[1024,128]{1,0:T(8,128)S(1)}, u32[]{:S(2)}, u32[]{:S(2)}) collective-permute-start(f32[1024,128]{1,0:T(8,128)S(1)} %constant_dynamic-update-slice_fusion.3.refs_1_), channel_id=1, source_target_pairs={{0,4},{4,0},{1,5},{5,1},{2,6},{6,2},{3,7},{7,3},{8,12},{12,8},{9,1... | collective-permute-start | bytes 1572872 | tf_op jit(solution)/shard_map/ppermute | solution.py:435
  115.8 0.0 copy-done.3
  115.8 0.0 copy-done.5
  115.9 0.0 copy-done.17
  115.9 0.0 copy-done.15
  115.9 0.0 copy-done.16
  116.0 0.7 stack.48.info
  116.7 0.6 pad_add_fusion.place
  117.2 0.1 collective-permute-done.8.refs_3_
  117.3 0.0 copy-start.12
  117.3 0.0 collective-permute-done.7.refs_2_
  117.3 0.0 copy-done.10
  117.3 0.0 copy-done.11
  117.3 0.8 copy-done.12
  118.1 34.8 %shard_map.101 = f32[80,3,2,4,128]{4,3,2,1,0:T(4,128)} custom-call(s32[2]{0:T(128)} %pad_add_fusion.place, f32[4,2]{1,0:T(4,128)} %copy-done.6, f32[12,8,128]{2,1,0:T(8,128)} %stack.48.info, f32[3072,128]{1,0:T(8,128)} %copy-done.10, f32[1024,128]{1,0:T(8,128)} %copy-done.11, f32[3072,128]{1,0:T(8,128)} %collective-permute-done.7.refs_2_, ...), custom_call_target="tpu_custom_call" | custom-call | tf_op jit(solution)/shard_map/pallas_call | solution.py:360
  (18 shorter events, 0.3 us)
Async XLA Ops:
  0.8 48.5 %copy-start.6 = (f32[4,2]{1,0:T(4,128)}, f32[4,2]{1,0:T(4,128)S(1)}, u32[]{:S(2)}) copy-start(f32[4,2]{1,0:T(4,128)S(1)} %copy.12.table) | copy-start | bytes 100
  0.8 1.2 copy-start
  2.0 0.7 copy-start.2
  2.7 0.7 copy-start.4
  3.4 0.7 copy-start.7
  4.1 0.7 copy-start.8
  4.8 0.7 copy-start.9
  9.6 0.9 copy-start.1
  10.6 10.3 %collective-permute-start = (f32[1024,128]{1,0:T(8,128)S(1)}, f32[1024,128]{1,0:T(8,128)S(1)}, u32[]{:S(2)}, u32[]{:S(2)}) collective-permute-start(f32[1024,128]{1,0:T(8,128)S(1)} %get-tuple-element.18), channel_id=1, source_target_pairs={{0,4},{4,0},{1,5},{5,1},{2,6},{6,2},{3,7},{7,3},{8,12},{12,8},{9,1... | collective-permute-start | bytes 1572872 | tf_op jit(solution)/shard_map/ppermute | solution.py:409
  72.2 24.3 %collective-permute-start.1 = (f32[1024,128]{1,0:T(8,128)S(1)}, f32[1024,128]{1,0:T(8,128)S(1)}, u32[]{:S(2)}, u32[]{:S(2)}) collective-permute-start(f32[1024,128]{1,0:T(8,128)S(1)} %bitcast.6), channel_id=1, source_target_pairs={{0,1},{1,2},{2,3},{3,0},{4,5},{5,6},{6,7},{7,4},{8,9},{9,10},{10,1... | collective-permute-start | bytes 1572872 | tf_op jit(solution)/shard_map/ppermute | solution.py:423
  75.3 21.2 %collective-permute-start.2 = (f32[1024,128]{1,0:T(8,128)S(1)}, f32[1024,128]{1,0:T(8,128)S(1)}, u32[]{:S(2)}, u32[]{:S(2)}) collective-permute-start(f32[1024,128]{1,0:T(8,128)S(1)} %bitcast.7), channel_id=1, source_target_pairs={{1,0},{2,1},{3,2},{0,3},{5,4},{6,5},{7,6},{4,7},{9,8},{10,9},{11,1... | collective-permute-start | bytes 1572872 | tf_op jit(solution)/shard_map/ppermute | solution.py:424
  78.7 13.4 %collective-permute-start.3 = (f32[12,80,128]{2,1,0:T(8,128)S(1)}, f32[12,80,128]{2,1,0:T(8,128)S(1)}, u32[]{:S(2)}, u32[]{:S(2)}) collective-permute-start(f32[12,80,128]{2,1,0:T(8,128)S(1)} %get-tuple-element.22), channel_id=1, source_target_pairs={{0,4},{4,8},{8,12},{12,16},{16,20},{20,24},{24,28},{28,32},{32,36}... | collective-permute-start | bytes 1474568 | tf_op jit(solution)/shard_map/ppermute | solution.py:425
  86.4 10.1 %collective-permute-start.4 = (f32[12,80,128]{2,1,0:T(8,128)S(1)}, f32[12,80,128]{2,1,0:T(8,128)S(1)}, u32[]{:S(2)}, u32[]{:S(2)}) collective-permute-start(f32[12,80,128]{2,1,0:T(8,128)S(1)} %get-tuple-element.23), channel_id=1, source_target_pairs={{4,0},{8,4},{12,8},{16,12},{20,16},{24,20},{28,24},{32,28},{36,32}... | collective-permute-start | bytes 1474568 | tf_op jit(solution)/shard_map/ppermute | solution.py:426
  92.1 9.9 %copy-start.13 = (f32[12,80,128]{2,1,0:T(8,128)}, f32[12,80,128]{2,1,0:T(8,128)S(1)}, u32[]{:S(2)}) copy-start(f32[12,80,128]{2,1,0:T(8,128)S(1)} %collective-permute-done.3.refs_5_) | copy-start | bytes 1474564
  96.5 5.5 %copy-start.14 = (f32[12,80,128]{2,1,0:T(8,128)}, f32[12,80,128]{2,1,0:T(8,128)S(1)}, u32[]{:S(2)}) copy-start(f32[12,80,128]{2,1,0:T(8,128)S(1)} %collective-permute-done.4.refs_6_) | copy-start | bytes 1474564
  96.6 19.2 %copy-start.3 = (s32[12,128]{1,0:T(8,128)S(1)}, s32[12,128]{1,0:T(8,128)}, u32[]{:S(2)}) copy-start(s32[12,128]{1,0:T(8,128)} %cols.1) | copy-start | bytes 18436
  96.6 19.2 %copy-start.5 = (s32[12,128]{1,0:T(8,128)S(1)}, s32[12,128]{1,0:T(8,128)}, u32[]{:S(2)}) copy-start(s32[12,128]{1,0:T(8,128)} %rws.1) | copy-start | bytes 18436
  96.6 19.3 %copy-start.17 = (s32[12,128]{1,0:T(8,128)S(1)}, s32[12,128]{1,0:T(8,128)}, u32[]{:S(2)}) copy-start(s32[12,128]{1,0:T(8,128)} %param.16) | copy-start | bytes 18436
  96.6 19.3 %copy-start.15 = (f32[12,128]{1,0:T(8,128)S(1)}, f32[12,128]{1,0:T(8,128)}, u32[]{:S(2)}) copy-start(f32[12,128]{1,0:T(8,128)} %param.17) | copy-start | bytes 18436
  96.6 19.3 %copy-start.16 = (f32[12,128]{1,0:T(8,128)S(1)}, f32[12,128]{1,0:T(8,128)}, u32[]{:S(2)}) copy-start(f32[12,128]{1,0:T(8,128)} %param.18) | copy-start | bytes 18436
  96.7 20.6 %copy-start.10 = (f32[3072,128]{1,0:T(8,128)}, f32[3072,128]{1,0:T(8,128)S(1)}, u32[]{:S(2)}) copy-start(f32[3072,128]{1,0:T(8,128)S(1)} %constant_dynamic-update-slice_fusion.refs_0_) | copy-start | bytes 4718596
  96.7 20.6 %collective-permute-start.7 = (f32[3072,128]{1,0:T(8,128)S(1)}, f32[3072,128]{1,0:T(8,128)}, u32[]{:S(2)}, u32[]{:S(2)}) collective-permute-start(f32[3072,128]{1,0:T(8,128)S(1)} %constant_dynamic-update-slice_fusion.refs_0_), channel_id=1, source_target_pairs={{0,4},{4,0},{1,5},{5,1},{2,6},{6,2},{3,7},{7,3},{8,12},{12,8},{9,1... | collective-permute-start | bytes 4718600 | tf_op jit(solution)/shard_map/ppermute | solution.py:435
  98.8 9.3 %collective-permute-start.5 = (f32[512,128]{1,0:T(8,128)S(1)}, f32[512,128]{1,0:T(8,128)S(1)}, u32[]{:S(2)}, u32[]{:S(2)}) collective-permute-start(f32[512,128]{1,0:T(8,128)S(1)} %slice.6), channel_id=1, source_target_pairs={{1,0},{2,1},{3,2},{0,3},{5,4},{6,5},{7,6},{4,7},{9,8},{10,9},{11,1... | collective-permute-start | bytes 786440 | tf_op jit(solution)/shard_map/ppermute | solution.py:430
  102.0 10.2 %collective-permute-start.6 = (f32[512,128]{1,0:T(8,128)S(1)}, f32[512,128]{1,0:T(8,128)S(1)}, u32[]{:S(2)}, u32[]{:S(2)}) collective-permute-start(f32[512,128]{1,0:T(8,128)S(1)} %slice.7), channel_id=1, source_target_pairs={{0,1},{1,2},{2,3},{3,0},{4,5},{5,6},{6,7},{7,4},{8,9},{9,10},{10,1... | collective-permute-start | bytes 786440 | tf_op jit(solution)/shard_map/ppermute | solution.py:431
  112.2 5.1 %copy-start.11 = (f32[1024,128]{1,0:T(8,128)}, f32[1024,128]{1,0:T(8,128)S(1)}, u32[]{:S(2)}) copy-start(f32[1024,128]{1,0:T(8,128)S(1)} %constant_dynamic-update-slice_fusion.3.refs_1_) | copy-start | bytes 1572868
  112.2 5.1 %collective-permute-start.8 = (f32[1024,128]{1,0:T(8,128)S(1)}, f32[1024,128]{1,0:T(8,128)S(1)}, u32[]{:S(2)}, u32[]{:S(2)}) collective-permute-start(f32[1024,128]{1,0:T(8,128)S(1)} %constant_dynamic-update-slice_fusion.3.refs_1_), channel_id=1, source_target_pairs={{0,4},{4,0},{1,5},{5,1},{2,6},{6,2},{3,7},{7,3},{8,12},{12,8},{9,1... | collective-permute-start | bytes 1572872 | tf_op jit(solution)/shard_map/ppermute | solution.py:435
  117.3 0.8 copy-start.12

commit v5 on v4

--- a/solution.py
+++ b/solution.py
@@ -147,11 +147,15 @@
     classes = table.shape[0]
     first = place[0].astype(jnp.float32)
     incoming = []
-    level = 0
-    for ref in arrived:
-        for at in range(0, ref.shape[0], length):
-            incoming.append((ref.at[at : at + length], remote.at[level]))
-            level += 1
+    around = place[2]
+    ring = all_levels // 2
+    for n, ref in enumerate(arrived):
+        for part in range(ring):
+            level = part
+            if n < 2:
+                level = lax.rem(around + (0, ring - 1, 1, 2)[part], ring)
+            rows_in = slice(0, ref.shape[1]) if n >= 2 else slice(length - ref.shape[1], length)
+            incoming.append((ref.at[part], remote.at[(n % 2) * ring + level, rows_in]))
     incoming += [(grid, local), (from_left, edges.at[0]), (from_right, edges.at[1])]
     incoming = [
         pltpu.make_async_copy(ref, target, sems.at[slabs + n])
@@ -356,7 +360,7 @@
     smem = pl.BlockSpec(memory_space=pltpu.SMEM)
     vmem = pl.BlockSpec(memory_space=pltpu.VMEM)
     anywhere = pl.BlockSpec(memory_space=pl.ANY)
-    all_levels = sum(part.shape[0] for part in arrived) // length
+    all_levels = 2 * arrived[0].shape[0]
     return pl.pallas_call(
         functools.partial(analysis_kernel, len(arrived)),
         out_shape=jax.ShapeDtypeStruct(shape, jnp.float32),
@@ -370,9 +374,9 @@
             pltpu.VMEM((2, LANES, 3 * members), jnp.bfloat16),
             pltpu.VMEM((2, all_levels + levels, LANES, LANES), jnp.float32),
             pltpu.VMEM((2, 2, LANES, LANES), jnp.float32),
-            pltpu.SemaphoreType.DMA((grid.shape[0] + all_levels + 3,)),
+            pltpu.SemaphoreType.DMA((grid.shape[0] + 2 * all_levels + 3,)),
         ],
-        compiler_params=pltpu.CompilerParams(vmem_limit_bytes=60 * 2**20),
+        compiler_params=pltpu.CompilerParams(vmem_limit_bytes=28 * 2**20),
     )(place, table, info, *arrived, grid, from_left, from_right)
 
 
@@ -419,27 +423,33 @@
     left = [(j, i) for i, j in right]
     up = [(i, i + 1) for i in range(tiles - 1)]
     down = [(j, i) for i, j in up]
+    cut = 640
+    used = batches * members + 8
+    middle = (used - cut) // 16 * 8
     mine, to_left, to_right = lax.optimization_barrier((mine, to_left, to_right))
-    before = lax.ppermute(mine, "x", right)
-    after = lax.ppermute(mine, "x", left)
+    first_rows = lax.all_gather(mine[:cut], "x")
+    last_rows = mine[cut:used]
+    before = lax.ppermute(last_rows, "x", right)
+    after = lax.ppermute(last_rows, "x", left)
     from_left = lax.ppermute(to_right, TILES, up)
     from_right = lax.ppermute(to_left, TILES, down)
-    before, after, from_left, from_right = lax.optimization_barrier(
-        (before, after, from_left, from_right)
+    across_a = lax.ppermute(after[:middle], "x", left)
+    across_b = lax.ppermute(before[middle:], "x", right)
+    last_rows = jnp.concatenate([last_rows, before, after, across_a, across_b], axis=0)
+    last_rows = last_rows.reshape(ring, used - cut, LANES)
+    last_swapped = lax.ppermute(last_rows, "core", swap)
+    first_rows, last_rows, from_left, from_right = lax.optimization_barrier(
+        (first_rows, last_rows, from_left, from_right)
     )
-    across_a = lax.ppermute(after[: length // 2], "x", left)
-    across_b = lax.ppermute(before[length // 2 :], "x", right)
-    near = jnp.concatenate([mine, before, after], axis=0)
-    across = jnp.concatenate([across_a, across_b], axis=0)
-    arrived = [near, across]
-    arrived += [lax.ppermute(part, "core", swap) for part in (near, across)]
+    arrived = [last_rows, last_swapped]
+    arrived += [first_rows, lax.ppermute(first_rows, "core", swap)]
 
     as_float = [v.astype(jnp.float32) for v in (obs_col, obs_row, obs_class)]
     blank = jnp.zeros_like(obs_value)
     info = jnp.stack([*as_float, obs_value, obs_error, blank, blank, blank], axis=1)
-    where = jnp.stack([first, jnp.int32(tiles * columns)]).astype(jnp.int32)
+    where = jnp.stack([first, jnp.int32(tiles * columns), lax.axis_index("x")]).astype(jnp.int32)
     return assimilate(
-        where, vertical_table, info, arrived, grid, from_left, from_right, state.shape, length
+        where, vertical_table, info, arrived, grid, from_left, from_right, state.shape, used
     )
 
 

time: 154 us -> 161 us (1.045)
  between operations: 0.36 us -> 13.7 us
  waiting for transfers between devices: 17.8 us -> 7.81 us
  local copies, waits for them, and re-layouts: 8.12 us -> 12.5 us
    ppermute x1, waiting for transfers between devices: 4.39 us -> 0.01 us  [shards(): from_right = lax.ppermute(to_left, TILES, down)]
    ppermute x1, waiting for transfers between devices: 3.78 us -> 0.01 us  [shards(): from_left = lax.ppermute(to_right, TILES, up)]
    ppermute x6, waiting for transfers between devices: 8.11 us -> 6.27 us  [the longest x1 5.01 us: shards(): across_b = lax.ppermute(before[middle:], 'x', right)]
    slice x2 -> x4, local copies, waits for them, and re-layouts: 0.04 us -> 1.72 us  [the longest x1 0.94 us: shards(): last_rows = mine[cut:used]]
    unnamed x40 -> x34, local copies, waits for them, and re-layouts: 7.27 us -> 8.69 us
  transfers between devices with their start and end apart: 9 -> 10, of which waited for: 6 -> 3; matrix products, arithmetic and copies ran while one was open for 1% -> 2% of each run, Pallas kernels for 0% -> 0%
where the time goes in v5:
time: 161 us; the launch traced here: 160 us
  blocking collectives  51.7 us (32%)
  Pallas kernels  38.1 us (24%)
  starting transfers between devices  35.7 us (22%)
  between operations  13.7 us (9%)
  local copies, waits for them, and re-layouts  12.5 us (8%)
  waiting for transfers between devices  7.81 us (5%)
    pallas_call x1, Pallas kernels, assimilate(): pl.pallas_call(functools.partial(analysis_kernel, len(arrived)), out_shap...  34.6 us
    all_to_all x1, blocking collectives, shards(): lax.all_to_all(mine.reshape(homes, chunk, LANES), ('z', 'y'), 0, 0, tiled...  28.9 us
    all_to_all x1, blocking collectives, shards(): lax.all_to_all(jnp.broadcast_to(mine[None], (homes, chunk, LANES)), ('z',...  22.8 us
    ppermute x1, starting transfers between devices, shards(): mine = mine + lax.ppermute(other, 'core', swap)  8.79 us
    unnamed x34, local copies, waits for them, and re-layouts  8.69 us
    ppermute x1, starting transfers between devices, shards(): from_left = lax.ppermute(to_right, TILES, up)  7.37 us
    ppermute x1, waiting for transfers between devices, shards(): across_b = lax.ppermute(before[middle:], 'x', right)  5.01 us
    ppermute x1, starting transfers between devices, shards(): across_a = lax.ppermute(after[:middle], 'x', left)  4.85 us
  transfers between devices with their start and end apart: 10, of which 3 were waited for; matrix products, arithmetic and copies ran while one was open for 2% of the time, Pallas kernels for 0%

profile of v5, /device:TPU:1, one launch (start us, length us, event | category | flops | bytes accessed | tf_op | source)
XLA Modules:
  0.0 159.8 jit_solution(12623673921964055553)
XLA Ops:
  6.5 0.0 all-gather.3.cloned.1.call-start
  6.5 0.8 copy.12.table
  7.3 0.1 pad_add_fusion.1.place
  7.4 1.2 copy-done.1
  8.6 0.0 copy-start.4
  8.6 0.7 copy-done.4
  9.3 0.0 copy-start.6
  9.3 0.7 copy-done.6
  10.0 0.0 copy-start.8
  10.0 0.7 copy-done.8
  10.7 0.0 copy-start.9
  10.7 0.7 copy-done.9
  11.4 0.0 copy-start.10
  11.4 0.7 copy-done.10
  12.0 3.6 %shard_map.100 = (f32[24,80,128]{2,1,0:T(8,128)S(1)}, f32[12,80,128]{2,1,0:T(8,128)S(1)}, f32[12,80,128]{2,1,0:T(8,128)S(1)}, f32[1024,128]{1,0:T(8,128)S(1)}, f32[1024,128]{1,0:T(8,128)S(1)}) custom-call(s32[4]{0:T(128)S(1)} %pad_add_fusion.1.place, f32[4,2]{1,0:T(4,128)S(1)} %copy.12.table, f32[80,3,2,4,128]{4,3,2,1,0:T(4,128)S(1)} %copy-done.1, ...), custom_call_target="tpu_custom_call" | custom-call | tf_op jit(solution)/shard_map/pallas_call | solution.py:337
  15.6 8.8 %collective-permute-start = (f32[1024,128]{1,0:T(8,128)S(1)}, f32[1024,128]{1,0:T(8,128)S(1)}, u32[]{:S(2)}, u32[]{:S(2)}) collective-permute-start(f32[1024,128]{1,0:T(8,128)S(1)} %get-tuple-element.18), channel_id=1, source_target_pairs={{0,4},{4,0},{1,5},{5,1},{2,6},{6,2},{3,7},{7,3},{8,12},{12,8},{9,1... | collective-permute-start | bytes 1572872 | tf_op jit(solution)/shard_map/ppermute | solution.py:413
  24.4 1.5 collective-permute-done
  25.9 0.1 add.12
  26.0 28.9 %all_to_all.10 = f32[64,16,128]{2,1,0:T(8,128)S(1)} all-to-all(f32[64,16,128]{2,1,0:T(8,128)S(1)} %bitcast.12), channel_id=1, replica_groups=mesh['z'=8,'y'=8,'core'=2,'x'=4] {'z','y'}, dimensions={0} | all-to-all | bytes 1048576 | tf_op jit(solution)/shard_map/all_to_all | solution.py:414
  54.9 0.1 reduce_sum.9
  55.0 22.8 %all_to_all.11 = f32[64,16,128]{2,1,0:T(8,128)S(1)} all-to-all(f32[64,16,128]{2,1,0:T(8,128)S(1)} %broadcast_in_dim.2), channel_id=1, replica_groups=mesh['z'=8,'y'=8,'core'=2,'x'=4] {'z','y'}, dimensions={0} | all-to-all | bytes 1048576 | tf_op jit(solution)/shard_map/all_to_all | solution.py:416
  77.8 0.0 copy-start.11
  77.8 0.0 copy-start.5
  77.8 0.0 copy-start.7
  77.8 0.0 copy-start.12
  77.8 0.0 copy-start.13
  77.9 0.0 copy-start.14
  77.9 0.8 slice.12
  78.6 0.1 copy-done.11
  78.7 0.0 all-gather.3.cloned.1.call-update
  78.8 0.9 fusion
  79.7 4.4 %collective-permute-start.2 = (f32[328,128]{1,0:T(8,128)S(1)}, f32[328,128]{1,0:T(8,128)S(1)}, u32[]{:S(2)}, u32[]{:S(2)}) collective-permute-start(f32[328,128]{1,0:T(8,128)S(1)} %get-tuple-element.29), channel_id=1, source_target_pairs={{1,0},{2,1},{3,2},{0,3},{5,4},{6,5},{7,6},{4,7},{9,8},{10,9},{11,1... | collective-permute-start | bytes 503816 | tf_op jit(solution)/shard_map/ppermute | solution.py:433
  84.1 1.9 %collective-permute-start.1 = (f32[328,128]{1,0:T(8,128)S(1)}, f32[328,128]{1,0:T(8,128)S(1)}, u32[]{:S(2)}, u32[]{:S(2)}) collective-permute-start(f32[328,128]{1,0:T(8,128)S(1)} %get-tuple-element.29), channel_id=1, source_target_pairs={{0,1},{1,2},{2,3},{3,0},{4,5},{5,6},{6,7},{7,4},{8,9},{9,10},{10,1... | collective-permute-start | bytes 503816 | tf_op jit(solution)/shard_map/ppermute | solution.py:432
  86.0 7.4 %collective-permute-start.5 = (f32[12,80,128]{2,1,0:T(8,128)S(1)}, f32[12,80,128]{2,1,0:T(8,128)S(1)}, u32[]{:S(2)}, u32[]{:S(2)}) collective-permute-start(f32[12,80,128]{2,1,0:T(8,128)S(1)} %get-tuple-element.22), channel_id=1, source_target_pairs={{0,4},{4,8},{8,12},{12,16},{16,20},{20,24},{24,28},{28,32},{32,36}... | collective-permute-start | bytes 1474568 | tf_op jit(solution)/shard_map/ppermute | solution.py:434
  93.4 1.9 %collective-permute-start.6 = (f32[12,80,128]{2,1,0:T(8,128)S(1)}, f32[12,80,128]{2,1,0:T(8,128)S(1)}, u32[]{:S(2)}, u32[]{:S(2)}) collective-permute-start(f32[12,80,128]{2,1,0:T(8,128)S(1)} %get-tuple-element.23), channel_id=1, source_target_pairs={{4,0},{8,4},{12,8},{16,12},{20,16},{24,20},{28,24},{32,28},{36,32}... | collective-permute-start | bytes 1474568 | tf_op jit(solution)/shard_map/ppermute | solution.py:435
  95.3 0.0 collective-permute-done.2
  95.4 4.9 %collective-permute-start.3 = (f32[160,128]{1,0:T(8,128)S(1)}, f32[160,128]{1,0:T(8,128)S(1)}, u32[]{:S(2)}, u32[]{:S(2)}) collective-permute-start(f32[160,128]{1,0:T(8,128)S(1)} %slice.16), channel_id=1, source_target_pairs={{1,0},{2,1},{3,2},{0,3},{5,4},{6,5},{7,6},{4,7},{9,8},{10,9},{11,1... | collective-permute-start | bytes 245768 | tf_op jit(solution)/shard_map/ppermute | solution.py:436
  100.2 0.0 collective-permute-done.1
  100.3 1.9 %collective-permute-start.4 = (f32[168,128]{1,0:T(8,128)S(1)}, f32[168,128]{1,0:T(8,128)S(1)}, u32[]{:S(2)}, u32[]{:S(2)}) collective-permute-start(f32[168,128]{1,0:T(8,128)S(1)} %slice.17), channel_id=1, source_target_pairs={{0,1},{1,2},{2,3},{3,0},{4,5},{5,6},{6,7},{7,4},{8,9},{9,10},{10,1... | collective-permute-start | bytes 258056 | tf_op jit(solution)/shard_map/ppermute | solution.py:437
  102.2 1.2 collective-permute-done.3
  103.5 5.0 %collective-permute-done.4 = f32[168,128]{1,0:T(8,128)S(1)} collective-permute-done((f32[168,128]{1,0:T(8,128)S(1)}, f32[168,128]{1,0:T(8,128)S(1)}, u32[]{:S(2)}, u32[]{:S(2)}) %collective-permute-start.4) | collective-permute-done | bytes 86048 | tf_op jit(solution)/shard_map/ppermute | solution.py:437
  108.5 0.0 collective-permute-done.5.refs_5_
  108.5 0.0 collective-permute-done.6.refs_6_
  108.5 0.0 copy-start.2
  108.5 0.8 copy-done.2
  109.3 0.0 all-gather.3.cloned.1.call-done
  109.3 2.6 %collective-permute-start.8 = (f32[4,640,128]{2,1,0:T(8,128)}, f32[4,640,128]{2,1,0:T(8,128)S(1)}, u32[]{:S(2)}, u32[]{:S(2)}) collective-permute-start(f32[4,640,128]{2,1,0:T(8,128)} %bitcast.8), channel_id=1, source_target_pairs={{0,4},{4,0},{1,5},{5,1},{2,6},{6,2},{3,7},{7,3},{8,12},{12,8},{9,1... | collective-permute-start | bytes 3932168 | tf_op jit(solution)/shard_map/ppermute | solution.py:445
  111.9 1.9 %collective-permute-start.7 = (f32[4,328,128]{2,1,0:T(8,128)S(1)}, f32[4,328,128]{2,1,0:T(8,128)}, u32[]{:S(2)}, u32[]{:S(2)}) collective-permute-start(f32[4,328,128]{2,1,0:T(8,128)S(1)} %bitcast.10), channel_id=1, source_target_pairs={{0,4},{4,0},{1,5},{5,1},{2,6},{6,2},{3,7},{7,3},{8,12},{12,8},{9,1... | collective-permute-start | bytes 2015240 | tf_op jit(solution)/shard_map/ppermute | solution.py:440
  113.8 0.0 copy-done.5
  113.9 0.0 copy-done.7
  113.9 0.0 copy-done.12
  113.9 0.0 copy-done.13
  113.9 0.0 copy-done.14
  114.0 0.6 stack.47
  114.6 0.6 stack_broadcast_in_dim.3
  115.2 0.8 stack.52.info
  115.9 0.1 pad_add_fusion.place
  116.0 0.0 collective-permute-done.7.refs_1_
  116.0 0.0 collective-permute-done.8.refs_3_
  116.1 0.0 copy-start
  116.1 1.3 copy-done
  117.4 0.0 copy-start.3
  117.4 1.0 copy-done.3
  118.4 34.6 %shard_map.101 = f32[80,3,2,4,128]{4,3,2,1,0:T(4,128)} custom-call(s32[3]{0:T(128)S(1)} %pad_add_fusion.place, f32[4,2]{1,0:T(4,128)S(1)} %copy.12.table, f32[12,8,128]{2,1,0:T(8,128)S(1)} %stack.52.info, f32[4,328,128]{2,1,0:T(8,128)S(1)} %bitcast.11, f32[4,328,128]{2,1,0:T(8,128)} %collective-permute-done.7.refs_1_, f32[4,640,128]{2,1,0:T(8,128)S(1)} %bitcast.9, ...), custom_call_target="tpu_custom_call" | custom-call | tf_op jit(solution)/shard_map/pallas_call | solution.py:364
  (16 shorter events, 0.1 us)
Async XLA Ops:
  6.5 102.7 %all-gather.3.cloned.1.call-start = ((), (), s32[]{:S(2)}) async-start(), calls=%async_computation.2 | async-start | bytes 1638400 | tf_op jit(solution)/shard_map/all_gather | solution.py:430
  7.4 1.2 copy-start.1
  8.6 0.7 copy-start.4
  9.3 0.7 copy-start.6
  10.0 0.7 copy-start.8
  10.7 0.7 copy-start.9
  11.4 0.7 copy-start.10
  15.6 10.3 %collective-permute-start = (f32[1024,128]{1,0:T(8,128)S(1)}, f32[1024,128]{1,0:T(8,128)S(1)}, u32[]{:S(2)}, u32[]{:S(2)}) collective-permute-start(f32[1024,128]{1,0:T(8,128)S(1)} %get-tuple-element.18), channel_id=1, source_target_pairs={{0,4},{4,0},{1,5},{5,1},{2,6},{6,2},{3,7},{7,3},{8,12},{12,8},{9,1... | collective-permute-start | bytes 1572872 | tf_op jit(solution)/shard_map/ppermute | solution.py:413
  77.8 0.9 copy-start.11
  77.8 36.0 %copy-start.5 = (s32[12,128]{1,0:T(8,128)S(1)}, s32[12,128]{1,0:T(8,128)}, u32[]{:S(2)}) copy-start(s32[12,128]{1,0:T(8,128)} %cols.1) | copy-start | bytes 18436
  77.8 36.0 %copy-start.7 = (s32[12,128]{1,0:T(8,128)S(1)}, s32[12,128]{1,0:T(8,128)}, u32[]{:S(2)}) copy-start(s32[12,128]{1,0:T(8,128)} %rws.1) | copy-start | bytes 18436
  77.8 36.0 %copy-start.12 = (f32[12,128]{1,0:T(8,128)S(1)}, f32[12,128]{1,0:T(8,128)}, u32[]{:S(2)}) copy-start(f32[12,128]{1,0:T(8,128)} %param.17) | copy-start | bytes 18436
  77.8 36.1 %copy-start.13 = (f32[12,128]{1,0:T(8,128)S(1)}, f32[12,128]{1,0:T(8,128)}, u32[]{:S(2)}) copy-start(f32[12,128]{1,0:T(8,128)} %param.18) | copy-start | bytes 18436
  77.9 36.1 %copy-start.14 = (s32[12,128]{1,0:T(8,128)S(1)}, s32[12,128]{1,0:T(8,128)}, u32[]{:S(2)}) copy-start(s32[12,128]{1,0:T(8,128)} %param.16) | copy-start | bytes 18436
  79.7 15.6 %collective-permute-start.2 = (f32[328,128]{1,0:T(8,128)S(1)}, f32[328,128]{1,0:T(8,128)S(1)}, u32[]{:S(2)}, u32[]{:S(2)}) collective-permute-start(f32[328,128]{1,0:T(8,128)S(1)} %get-tuple-element.29), channel_id=1, source_target_pairs={{1,0},{2,1},{3,2},{0,3},{5,4},{6,5},{7,6},{4,7},{9,8},{10,9},{11,1... | collective-permute-start | bytes 503816 | tf_op jit(solution)/shard_map/ppermute | solution.py:433
  84.1 16.1 %collective-permute-start.1 = (f32[328,128]{1,0:T(8,128)S(1)}, f32[328,128]{1,0:T(8,128)S(1)}, u32[]{:S(2)}, u32[]{:S(2)}) collective-permute-start(f32[328,128]{1,0:T(8,128)S(1)} %get-tuple-element.29), channel_id=1, source_target_pairs={{0,1},{1,2},{2,3},{3,0},{4,5},{5,6},{6,7},{7,4},{8,9},{9,10},{10,1... | collective-permute-start | bytes 503816 | tf_op jit(solution)/shard_map/ppermute | solution.py:432
  86.0 22.4 %collective-permute-start.5 = (f32[12,80,128]{2,1,0:T(8,128)S(1)}, f32[12,80,128]{2,1,0:T(8,128)S(1)}, u32[]{:S(2)}, u32[]{:S(2)}) collective-permute-start(f32[12,80,128]{2,1,0:T(8,128)S(1)} %get-tuple-element.22), channel_id=1, source_target_pairs={{0,4},{4,8},{8,12},{12,16},{16,20},{20,24},{24,28},{28,32},{32,36}... | collective-permute-start | bytes 1474568 | tf_op jit(solution)/shard_map/ppermute | solution.py:434
  93.4 15.1 %collective-permute-start.6 = (f32[12,80,128]{2,1,0:T(8,128)S(1)}, f32[12,80,128]{2,1,0:T(8,128)S(1)}, u32[]{:S(2)}, u32[]{:S(2)}) collective-permute-start(f32[12,80,128]{2,1,0:T(8,128)S(1)} %get-tuple-element.23), channel_id=1, source_target_pairs={{4,0},{8,4},{12,8},{16,12},{20,16},{24,20},{28,24},{32,28},{36,32}... | collective-permute-start | bytes 1474568 | tf_op jit(solution)/shard_map/ppermute | solution.py:435
  95.4 8.1 %collective-permute-start.3 = (f32[160,128]{1,0:T(8,128)S(1)}, f32[160,128]{1,0:T(8,128)S(1)}, u32[]{:S(2)}, u32[]{:S(2)}) collective-permute-start(f32[160,128]{1,0:T(8,128)S(1)} %slice.16), channel_id=1, source_target_pairs={{1,0},{2,1},{3,2},{0,3},{5,4},{6,5},{7,6},{4,7},{9,8},{10,9},{11,1... | collective-permute-start | bytes 245768 | tf_op jit(solution)/shard_map/ppermute | solution.py:436
  100.3 8.2 %collective-permute-start.4 = (f32[168,128]{1,0:T(8,128)S(1)}, f32[168,128]{1,0:T(8,128)S(1)}, u32[]{:S(2)}, u32[]{:S(2)}) collective-permute-start(f32[168,128]{1,0:T(8,128)S(1)} %slice.17), channel_id=1, source_target_pairs={{0,1},{1,2},{2,3},{3,0},{4,5},{5,6},{6,7},{7,4},{8,9},{9,10},{10,1... | collective-permute-start | bytes 258056 | tf_op jit(solution)/shard_map/ppermute | solution.py:437
  108.5 0.8 copy-start.2
  109.3 6.8 %collective-permute-start.8 = (f32[4,640,128]{2,1,0:T(8,128)}, f32[4,640,128]{2,1,0:T(8,128)S(1)}, u32[]{:S(2)}, u32[]{:S(2)}) collective-permute-start(f32[4,640,128]{2,1,0:T(8,128)} %bitcast.8), channel_id=1, source_target_pairs={{0,4},{4,0},{1,5},{5,1},{2,6},{6,2},{3,7},{7,3},{8,12},{12,8},{9,1... | collective-permute-start | bytes 3932168 | tf_op jit(solution)/shard_map/ppermute | solution.py:445
  111.9 4.1 %collective-permute-start.7 = (f32[4,328,128]{2,1,0:T(8,128)S(1)}, f32[4,328,128]{2,1,0:T(8,128)}, u32[]{:S(2)}, u32[]{:S(2)}) collective-permute-start(f32[4,328,128]{2,1,0:T(8,128)S(1)} %bitcast.10), channel_id=1, source_target_pairs={{0,4},{4,0},{1,5},{5,1},{2,6},{6,2},{3,7},{7,3},{8,12},{12,8},{9,1... | collective-permute-start | bytes 2015240 | tf_op jit(solution)/shard_map/ppermute | solution.py:440
  116.1 1.3 copy-start
  117.4 1.0 copy-start.3
Sparse Core Ops, SparseCore 0:
  78.9 28.7 all-gather.2

commit v6 on v5

--- a/solution.py
+++ b/solution.py
@@ -15,8 +15,9 @@
 
 
 def forecast_kernel(
-    place, table, state, east, north, cols, rws, flds, grid, to_left, to_right, mine, other,
-    plain, ahead, seen, sems
+    place, table, state, east_in, north_in, cols_in, rws_in, flds_in,
+    grid, to_left, to_right, mine, other,
+    whole, east, north, cols, rws, flds, plain, ahead, seen, sems,
 ):
     members, fields, levels, columns, rows = state.shape
     reach = 2
@@ -24,13 +25,23 @@
     span = columns + 2 * reach
     groups = fields * levels
     first, core, origin, total_cols = place[0], place[1], place[2], place[3]
+    small = ((east_in, east), (north_in, north), (cols_in, cols), (rws_in, rws), (flds_in, flds))
+    slots = groups * columns
+    fetches = [
+        pltpu.make_async_copy(source, target, sems.at[slots + n])
+        for n, (source, target) in enumerate(((state, whole),) + small)
+    ]
+    for fetch in fetches:
+        fetch.start()
+    for fetch in fetches:
+        fetch.wait()
     copies = []
     for g in range(groups):
         for k in range(columns):
             slot = g * columns + k
             copies.append(
                 pltpu.make_async_copy(
-                    state.at[:, g // levels, g % levels, k, :], plain.at[slot], sems.at[slot]
+                    whole.at[:, g // levels, g % levels, k, :], plain.at[slot], sems.at[slot]
                 )
             )
     for copy in copies:
@@ -93,8 +104,8 @@
         )
     vt = jnp.zeros((8, LANES), jnp.float32)
     spot = lax.broadcasted_iota(jnp.int32, (8, LANES), 1)
-    for k in range(table.shape[0]):
-        own_weight = jnp.where(core == 0, table[k, 0], table[k, 1])
+    for k in range(table.shape[1]):
+        own_weight = jnp.where(core == 0, table[0, k], table[1, k])
         vt = jnp.where(spot == k, own_weight, vt)
     mine[batches * members : batches * members + 8, :] = jnp.where(origin == 1, vt, 0.0)
 
@@ -134,7 +145,8 @@
     return high, low
 
 
-def analysis_kernel(count, place, table, info, *refs):
+def analysis_kernel(count, place, table, *refs):
+    info, refs = refs[:5], refs[5:]
     arrived, rest = refs[:count], refs[count:]
     grid, from_left, from_right, out = rest[:4]
     local, remote, edges, spread_rows, spread_cols, vertical, position, sems = rest[4:]
@@ -142,9 +154,9 @@
     slabs, members, rows = grid.shape
     fields, levels, columns = out.shape[1], out.shape[2], out.shape[3]
     groups = fields * levels
-    batches = info.shape[0]
+    batches = info[0].shape[0]
     total_cols = place[1].astype(jnp.float32)
-    classes = table.shape[0]
+    classes = table.shape[1]
     first = place[0].astype(jnp.float32)
     incoming = []
     around = place[2]
@@ -193,24 +205,25 @@
     def rows_of(c):
         return pl.ds(pl.multiple_of(c * members, 8), members)
 
+    def fact(k, c):
+        return info[k][pl.ds(c, 1), :].astype(jnp.float32)
+
     def taper_to(turn, c):
-        there = info[c]
-        d_col = (there[0:1] - position[turn, 0]) * inverse
-        d_row = (there[1:2] - position[turn, 1]) * (1.0 / RADY)
+        d_col = (fact(0, c) - position[turn, 0]) * inverse
+        d_row = (fact(1, c) - position[turn, 1]) * (1.0 / RADY)
         radial = jnp.maximum(1.0 - d_col * d_col - d_row * d_row, 0.0)
         return radial * radial
 
     def analyse(turn, c, total):
-        facts = info[c]
         priors = total * (1.0 / all_levels)
         average = jnp.sum(priors, axis=0, keepdims=True) * (1.0 / members)
         spread = priors - average
         variance = jnp.sum(spread * spread, axis=0, keepdims=True) / (members - 1) + EPSILON
-        error = facts[4:5]
+        error = fact(4, c)
         ratio = 1.0 / (variance + error)
         shrink = variance * ratio
         factor = jnp.sqrt(error * ratio)
-        increments = shrink * (facts[3:4] - average) + (factor - 1.0) * spread
+        increments = shrink * (fact(3, c) - average) + (factor - 1.0) * spread
         regress = spread / ((members - 1) * variance)
         high, low = halves(increments)
         spread_rows[turn, :members, :LANES] = high
@@ -225,7 +238,7 @@
         spread_cols[turn] = jnp.transpose(stacked)[:, : 3 * members].astype(jnp.bfloat16)
 
         def column_of(k):
-            return jnp.transpose(jnp.broadcast_to(facts[k : k + 1], (LANES, LANES)))
+            return jnp.transpose(jnp.broadcast_to(fact(k, c), (LANES, LANES)))
 
         position[turn, 0] = column_of(0)
         position[turn, 1] = column_of(1)
@@ -237,7 +250,7 @@
                     jnp.broadcast_to(row[0:1, k : k + 1], (LANES, LANES)) for k in range(classes)
                 ]
             else:
-                weights = [table[k, level - all_levels] for k in range(classes)]
+                weights = [table[level - all_levels, k] for k in range(classes)]
             chosen = jnp.zeros((LANES, LANES), jnp.float32) + weights[classes - 1]
             for k in range(classes - 1):
                 chosen = jnp.where(obs_class == float(k), weights[k], chosen)
@@ -343,15 +356,16 @@
             picks,
             picks,
         ),
-        in_specs=[smem, smem, anywhere] + [vmem] * 5,
+        in_specs=[smem, smem] + [anywhere] * 6,
         out_specs=(vmem,) * 5,
-        scratch_shapes=[
+        scratch_shapes=[pltpu.VMEM(v.shape, v.dtype) for v in (state, east, north, cols, rws, flds)]
+        + [
             pltpu.VMEM((groups * columns, members, rows), jnp.float32),
             pltpu.VMEM((groups * (columns + 4), members, rows), jnp.float32),
             pltpu.SMEM((cols.shape[0],), jnp.int32),
-            pltpu.SemaphoreType.DMA((groups * columns,)),
+            pltpu.SemaphoreType.DMA((groups * columns + 6,)),
         ],
-        compiler_params=pltpu.CompilerParams(vmem_limit_bytes=40 * 2**20),
+        compiler_params=pltpu.CompilerParams(vmem_limit_bytes=60 * 2**20),
     )(place, table, state, east, north, cols, rws, flds)
 
 
@@ -364,7 +378,7 @@
     return pl.pallas_call(
         functools.partial(analysis_kernel, len(arrived)),
         out_shape=jax.ShapeDtypeStruct(shape, jnp.float32),
-        in_specs=[smem, smem, vmem] + [anywhere] * (len(arrived) + 3),
+        in_specs=[smem, smem] + [vmem] * len(info) + [anywhere] * (len(arrived) + 3),
         out_specs=anywhere,
         scratch_shapes=[
             pltpu.VMEM(grid.shape, jnp.float32),
@@ -376,8 +390,8 @@
             pltpu.VMEM((2, 2, LANES, LANES), jnp.float32),
             pltpu.SemaphoreType.DMA((grid.shape[0] + 2 * all_levels + 3,)),
         ],
-        compiler_params=pltpu.CompilerParams(vmem_limit_bytes=28 * 2**20),
-    )(place, table, info, *arrived, grid, from_left, from_right)
+        compiler_params=pltpu.CompilerParams(vmem_limit_bytes=60 * 2**20),
+    )(place, table, *info, *arrived, grid, from_left, from_right)
 
 
 def shards(
@@ -402,10 +416,11 @@
     chunk = -(-(batches * members + 8) // (8 * homes)) * 8
     length = chunk * homes
 
+    table = vertical_table.T
     origin = (tile // 2 == 0).astype(jnp.int32)
     place = jnp.stack([first, core, origin, jnp.int32(tiles * columns)]).astype(jnp.int32)
     grid, to_left, to_right, mine, other = forecast(
-        place, vertical_table, state, eastward_current, northward_current, obs_col, obs_row,
+        place, table, state, eastward_current, northward_current, obs_col, obs_row,
         obs_field, length,
     )
 
@@ -444,12 +459,10 @@
     arrived = [last_rows, last_swapped]
     arrived += [first_rows, lax.ppermute(first_rows, "core", swap)]
 
-    as_float = [v.astype(jnp.float32) for v in (obs_col, obs_row, obs_class)]
-    blank = jnp.zeros_like(obs_value)
-    info = jnp.stack([*as_float, obs_value, obs_error, blank, blank, blank], axis=1)
+    facts = [obs_col, obs_row, obs_class, obs_value, obs_error]
     where = jnp.stack([first, jnp.int32(tiles * columns), lax.axis_index("x")]).astype(jnp.int32)
     return assimilate(
-        where, vertical_table, info, arrived, grid, from_left, from_right, state.shape, used
+        where, table, facts, arrived, grid, from_left, from_right, state.shape, used
     )
 
 

time: 161 us -> 158 us (0.981)
  local copies, waits for them, and re-layouts: 12.5 us -> 2.93 us
  Pallas kernels: 38.1 us -> 41.5 us
  other arithmetic: 0.3 us -> 2.4 us
  waiting for transfers between devices: 7.81 us -> 9.56 us
    unnamed x34 -> x13, local copies, waits for them, and re-layouts: 8.69 us -> 2.1 us
    pallas_call x1, Pallas kernels: 3.57 us -> 6.58 us  [forecast(): pl.pallas_call(forecast_kernel, out_shape=(jax.ShapeDtypeStruct((groups *...]
    another operation x8 -> x0, local copies, waits for them, and re-layouts: 2 us -> none  [shards(): jnp.stack([*as_float, obs_value, obs_error, blank, blank, blank], axis=1)]
  transfers between devices with their start and end apart: 10 -> 10, of which waited for: 3 -> 4; matrix products, arithmetic and copies ran while one was open for 2% -> 0% of each run, Pallas kernels for 0% -> 0%
where the time goes in v6:
time: 158 us; the launch traced here: 157 us
  blocking collectives  51.7 us (33%)
  Pallas kernels  41.5 us (26%)
  starting transfers between devices  35.5 us (22%)
  between operations  13.6 us (9%)
  waiting for transfers between devices  9.56 us (6%)
  local copies, waits for them, and re-layouts  2.93 us (2%)
  other arithmetic  2.4 us (2%)
    pallas_call x1, Pallas kernels, assimilate(): pl.pallas_call(functools.partial(analysis_kernel, len(arrived)), out_shap...  35 us
    all_to_all x1, blocking collectives, shards(): lax.all_to_all(mine.reshape(homes, chunk, LANES), ('z', 'y'), 0, 0, tiled...  28.9 us
    all_to_all x1, blocking collectives, shards(): lax.all_to_all(jnp.broadcast_to(mine[None], (homes, chunk, LANES)), ('z',...  22.8 us
    ppermute x1, starting transfers between devices, shards(): mine = mine + lax.ppermute(other, 'core', swap)  8.79 us
    ppermute x1, starting transfers between devices, shards(): from_left = lax.ppermute(to_right, TILES, up)  7.37 us
    pallas_call x1, Pallas kernels, forecast(): pl.pallas_call(forecast_kernel, out_shape=(jax.ShapeDtypeStruct((groups *...  6.58 us
    ppermute x1, waiting for transfers between devices, shards(): across_b = lax.ppermute(before[middle:], 'x', right)  5.65 us
    ppermute x1, starting transfers between devices, shards(): across_a = lax.ppermute(after[:middle], 'x', left)  4.85 us
  transfers between devices with their start and end apart: 10, of which 4 were waited for; matrix products, arithmetic and copies ran while one was open for 0% of the time, Pallas kernels for 0%

profile of v6, /device:TPU:1, one launch (start us, length us, event | category | flops | bytes accessed | tf_op | source)
XLA Modules:
  0.0 157.3 jit_solution(2413216952961712409)
XLA Ops:
  6.5 0.0 all-gather.3.cloned.1.call-start
  6.5 0.6 pad_add_fusion.1.place
  7.1 6.6 %shard_map.100 = (f32[24,80,128]{2,1,0:T(8,128)}, f32[12,80,128]{2,1,0:T(8,128)}, f32[12,80,128]{2,1,0:T(8,128)}, f32[1024,128]{1,0:T(8,128)}, f32[1024,128]{1,0:T(8,128)}) custom-call(s32[4]{0:T(128)} %pad_add_fusion.1.place, f32[2,4]{1,0:T(2,128)} %bitcast.16, f32[80,3,2,4,128]{4,3,2,1,0:T(4,128)} %state.1, f32[2,128]{1,0:T(2,128)} %east_in.1, ...), custom_call_target="tpu_custom_call" | custom-call | tf_op jit(solution)/shard_map/pallas_call | solution.py:350
  13.7 8.8 %collective-permute-start = (f32[1024,128]{1,0:T(8,128)}, f32[1024,128]{1,0:T(8,128)S(1)}, u32[]{:S(2)}, u32[]{:S(2)}) collective-permute-start(f32[1024,128]{1,0:T(8,128)} %get-tuple-element.18), channel_id=1, source_target_pairs={{0,4},{4,0},{1,5},{5,1},{2,6},{6,2},{3,7},{7,3},{8,12},{12,8},{9,1... | collective-permute-start | bytes 1572872 | tf_op jit(solution)/shard_map/ppermute | solution.py:428
  22.5 1.7 %collective-permute-done = f32[1024,128]{1,0:T(8,128)S(1)} collective-permute-done((f32[1024,128]{1,0:T(8,128)}, f32[1024,128]{1,0:T(8,128)S(1)}, u32[]{:S(2)}, u32[]{:S(2)}) %collective-permute-start) | collective-permute-done | bytes 524320 | tf_op jit(solution)/shard_map/ppermute | solution.py:428
  24.2 1.1 add.12
  25.3 28.9 %all_to_all.10 = f32[64,16,128]{2,1,0:T(8,128)S(1)} all-to-all(f32[64,16,128]{2,1,0:T(8,128)S(1)} %bitcast.9), channel_id=1, replica_groups=mesh['z'=8,'y'=8,'core'=2,'x'=4] {'z','y'}, dimensions={0} | all-to-all | bytes 1048576 | tf_op jit(solution)/shard_map/all_to_all | solution.py:429
  54.2 0.1 reduce_sum.9
  54.3 22.8 %all_to_all.11 = f32[64,16,128]{2,1,0:T(8,128)S(1)} all-to-all(f32[64,16,128]{2,1,0:T(8,128)S(1)} %broadcast_in_dim.2), channel_id=1, replica_groups=mesh['z'=8,'y'=8,'core'=2,'x'=4] {'z','y'}, dimensions={0} | all-to-all | bytes 1048576 | tf_op jit(solution)/shard_map/all_to_all | solution.py:431
  77.2 0.7 slice.12
  77.9 0.0 all-gather.3.cloned.1.call-update
  78.0 4.4 %collective-permute-start.2 = (f32[328,128]{1,0:T(8,128)S(1)}, f32[328,128]{1,0:T(8,128)S(1)}, u32[]{:S(2)}, u32[]{:S(2)}) collective-permute-start(f32[328,128]{1,0:T(8,128)S(1)} %get-tuple-element.29), channel_id=1, source_target_pairs={{1,0},{2,1},{3,2},{0,3},{5,4},{6,5},{7,6},{4,7},{9,8},{10,9},{11,1... | collective-permute-start | bytes 503816 | tf_op jit(solution)/shard_map/ppermute | solution.py:448
  82.4 1.9 %collective-permute-start.1 = (f32[328,128]{1,0:T(8,128)S(1)}, f32[328,128]{1,0:T(8,128)S(1)}, u32[]{:S(2)}, u32[]{:S(2)}) collective-permute-start(f32[328,128]{1,0:T(8,128)S(1)} %get-tuple-element.29), channel_id=1, source_target_pairs={{0,1},{1,2},{2,3},{3,0},{4,5},{5,6},{6,7},{7,4},{8,9},{9,10},{10,1... | collective-permute-start | bytes 503816 | tf_op jit(solution)/shard_map/ppermute | solution.py:447
  84.3 7.4 %collective-permute-start.5 = (f32[12,80,128]{2,1,0:T(8,128)}, f32[12,80,128]{2,1,0:T(8,128)S(1)}, u32[]{:S(2)}, u32[]{:S(2)}) collective-permute-start(f32[12,80,128]{2,1,0:T(8,128)} %get-tuple-element.22), channel_id=1, source_target_pairs={{0,4},{4,8},{8,12},{12,16},{16,20},{20,24},{24,28},{28,32},{32,36}... | collective-permute-start | bytes 1474568 | tf_op jit(solution)/shard_map/ppermute | solution.py:449
  91.7 1.9 %collective-permute-start.6 = (f32[12,80,128]{2,1,0:T(8,128)}, f32[12,80,128]{2,1,0:T(8,128)S(1)}, u32[]{:S(2)}, u32[]{:S(2)}) collective-permute-start(f32[12,80,128]{2,1,0:T(8,128)} %get-tuple-element.23), channel_id=1, source_target_pairs={{4,0},{8,4},{12,8},{16,12},{20,16},{24,20},{28,24},{32,28},{36,32}... | collective-permute-start | bytes 1474568 | tf_op jit(solution)/shard_map/ppermute | solution.py:450
  93.6 0.0 collective-permute-done.2
  93.6 4.9 %collective-permute-start.3 = (f32[160,128]{1,0:T(8,128)S(1)}, f32[160,128]{1,0:T(8,128)S(1)}, u32[]{:S(2)}, u32[]{:S(2)}) collective-permute-start(f32[160,128]{1,0:T(8,128)S(1)} %slice.16), channel_id=1, source_target_pairs={{1,0},{2,1},{3,2},{0,3},{5,4},{6,5},{7,6},{4,7},{9,8},{10,9},{11,1... | collective-permute-start | bytes 245768 | tf_op jit(solution)/shard_map/ppermute | solution.py:451
  98.5 0.0 collective-permute-done.1
  98.5 1.9 %collective-permute-start.4 = (f32[168,128]{1,0:T(8,128)S(1)}, f32[168,128]{1,0:T(8,128)S(1)}, u32[]{:S(2)}, u32[]{:S(2)}) collective-permute-start(f32[168,128]{1,0:T(8,128)S(1)} %slice.17), channel_id=1, source_target_pairs={{0,1},{1,2},{2,3},{3,0},{4,5},{5,6},{6,7},{7,4},{8,9},{9,10},{10,1... | collective-permute-start | bytes 258056 | tf_op jit(solution)/shard_map/ppermute | solution.py:452
  100.5 1.1 collective-permute-done.3
  101.6 5.6 %collective-permute-done.4 = f32[168,128]{1,0:T(8,128)S(1)} collective-permute-done((f32[168,128]{1,0:T(8,128)S(1)}, f32[168,128]{1,0:T(8,128)S(1)}, u32[]{:S(2)}, u32[]{:S(2)}) %collective-permute-start.4) | collective-permute-done | bytes 86048 | tf_op jit(solution)/shard_map/ppermute | solution.py:452
  107.2 0.0 copy-start.1
  107.2 0.0 collective-permute-done.5.refs_10_
  107.2 0.0 copy-start.3
  107.3 0.0 collective-permute-done.6.refs_11_
  107.3 0.0 copy-start.4
  107.3 0.0 all-gather.3.cloned.1.call-done
  107.3 0.8 copy-done.4
  108.1 1.9 %collective-permute-start.8 = (f32[4,640,128]{2,1,0:T(8,128)}, f32[4,640,128]{2,1,0:T(8,128)S(1)}, u32[]{:S(2)}, u32[]{:S(2)}) collective-permute-start(f32[4,640,128]{2,1,0:T(8,128)} %bitcast.12), channel_id=1, source_target_pairs={{0,4},{4,0},{1,5},{5,1},{2,6},{6,2},{3,7},{7,3},{8,12},{12,8},{9,1... | collective-permute-start | bytes 3932168 | tf_op jit(solution)/shard_map/ppermute | solution.py:460
  110.0 2.4 %collective-permute-start.7 = (f32[4,328,128]{2,1,0:T(8,128)S(1)}, f32[4,328,128]{2,1,0:T(8,128)S(1)}, u32[]{:S(2)}, u32[]{:S(2)}) collective-permute-start(f32[4,328,128]{2,1,0:T(8,128)S(1)} %bitcast.14), channel_id=1, source_target_pairs={{0,4},{4,0},{1,5},{5,1},{2,6},{6,2},{3,7},{7,3},{8,12},{12,8},{9,1... | collective-permute-start | bytes 2015240 | tf_op jit(solution)/shard_map/ppermute | solution.py:455
  112.4 0.7 pad_add_fusion.place
  113.1 1.1 collective-permute-done.7.refs_6_
  114.2 0.0 copy-start.2
  114.2 0.0 collective-permute-done.8.refs_8_
  114.2 0.0 copy-start
  114.2 0.0 copy-done.1
  114.2 0.0 copy-done.3
  114.2 0.8 copy-done.2
  115.0 0.4 copy-done
  115.4 35.0 %shard_map.101 = f32[80,3,2,4,128]{4,3,2,1,0:T(4,128)} custom-call(s32[3]{0:T(128)} %pad_add_fusion.place, f32[2,4]{1,0:T(2,128)} %bitcast.17, s32[12,128]{1,0:T(8,128)} %refs_0_.1, s32[12,128]{1,0:T(8,128)} %refs_1_.1, s32[12,128]{1,0:T(8,128)} %refs_2_.1, f32[12,128]{1,0:T(8,128)} %refs_3_.1, f32[12,128]{1,0:T(8,128)} %refs_4_.1, f32[4,328,128]{2,1,0:T(8,128)} %bitcast.15, ...), custom_call_target="tpu_custom_call" | custom-call | tf_op jit(solution)/shard_map/pallas_call | solution.py:378
  (8 shorter events, 0.1 us)
Async XLA Ops:
  6.5 100.8 %all-gather.3.cloned.1.call-start = ((), (), s32[]{:S(2)}) async-start(), calls=%async_computation.2 | async-start | bytes 1638400 | tf_op jit(solution)/shard_map/all_gather | solution.py:445
  13.7 10.5 %collective-permute-start = (f32[1024,128]{1,0:T(8,128)}, f32[1024,128]{1,0:T(8,128)S(1)}, u32[]{:S(2)}, u32[]{:S(2)}) collective-permute-start(f32[1024,128]{1,0:T(8,128)} %get-tuple-element.18), channel_id=1, source_target_pairs={{0,4},{4,0},{1,5},{5,1},{2,6},{6,2},{3,7},{7,3},{8,12},{12,8},{9,1... | collective-permute-start | bytes 1572872 | tf_op jit(solution)/shard_map/ppermute | solution.py:428
  78.0 15.6 %collective-permute-start.2 = (f32[328,128]{1,0:T(8,128)S(1)}, f32[328,128]{1,0:T(8,128)S(1)}, u32[]{:S(2)}, u32[]{:S(2)}) collective-permute-start(f32[328,128]{1,0:T(8,128)S(1)} %get-tuple-element.29), channel_id=1, source_target_pairs={{1,0},{2,1},{3,2},{0,3},{5,4},{6,5},{7,6},{4,7},{9,8},{10,9},{11,1... | collective-permute-start | bytes 503816 | tf_op jit(solution)/shard_map/ppermute | solution.py:448
  82.4 16.1 %collective-permute-start.1 = (f32[328,128]{1,0:T(8,128)S(1)}, f32[328,128]{1,0:T(8,128)S(1)}, u32[]{:S(2)}, u32[]{:S(2)}) collective-permute-start(f32[328,128]{1,0:T(8,128)S(1)} %get-tuple-element.29), channel_id=1, source_target_pairs={{0,1},{1,2},{2,3},{3,0},{4,5},{5,6},{6,7},{7,4},{8,9},{9,10},{10,1... | collective-permute-start | bytes 503816 | tf_op jit(solution)/shard_map/ppermute | solution.py:447
  84.3 22.9 %collective-permute-start.5 = (f32[12,80,128]{2,1,0:T(8,128)}, f32[12,80,128]{2,1,0:T(8,128)S(1)}, u32[]{:S(2)}, u32[]{:S(2)}) collective-permute-start(f32[12,80,128]{2,1,0:T(8,128)} %get-tuple-element.22), channel_id=1, source_target_pairs={{0,4},{4,8},{8,12},{12,16},{16,20},{20,24},{24,28},{28,32},{32,36}... | collective-permute-start | bytes 1474568 | tf_op jit(solution)/shard_map/ppermute | solution.py:449
  91.7 15.6 %collective-permute-start.6 = (f32[12,80,128]{2,1,0:T(8,128)}, f32[12,80,128]{2,1,0:T(8,128)S(1)}, u32[]{:S(2)}, u32[]{:S(2)}) collective-permute-start(f32[12,80,128]{2,1,0:T(8,128)} %get-tuple-element.23), channel_id=1, source_target_pairs={{4,0},{8,4},{12,8},{16,12},{20,16},{24,20},{28,24},{32,28},{36,32}... | collective-permute-start | bytes 1474568 | tf_op jit(solution)/shard_map/ppermute | solution.py:450
  93.6 7.9 %collective-permute-start.3 = (f32[160,128]{1,0:T(8,128)S(1)}, f32[160,128]{1,0:T(8,128)S(1)}, u32[]{:S(2)}, u32[]{:S(2)}) collective-permute-start(f32[160,128]{1,0:T(8,128)S(1)} %slice.16), channel_id=1, source_target_pairs={{1,0},{2,1},{3,2},{0,3},{5,4},{6,5},{7,6},{4,7},{9,8},{10,9},{11,1... | collective-permute-start | bytes 245768 | tf_op jit(solution)/shard_map/ppermute | solution.py:451
  98.5 8.7 %collective-permute-start.4 = (f32[168,128]{1,0:T(8,128)S(1)}, f32[168,128]{1,0:T(8,128)S(1)}, u32[]{:S(2)}, u32[]{:S(2)}) collective-permute-start(f32[168,128]{1,0:T(8,128)S(1)} %slice.17), channel_id=1, source_target_pairs={{0,1},{1,2},{2,3},{3,0},{4,5},{5,6},{6,7},{7,4},{8,9},{9,10},{10,1... | collective-permute-start | bytes 258056 | tf_op jit(solution)/shard_map/ppermute | solution.py:452
  107.2 6.9 %copy-start.1 = (f32[1312,128]{1,0:T(8,128)}, f32[1312,128]{1,0:T(8,128)S(1)}, u32[]{:S(2)}) copy-start(f32[1312,128]{1,0:T(8,128)S(1)} %constant_dynamic-update-slice_fusion) | copy-start | bytes 2015236
  107.2 6.9 %copy-start.3 = (f32[12,80,128]{2,1,0:T(8,128)}, f32[12,80,128]{2,1,0:T(8,128)S(1)}, u32[]{:S(2)}) copy-start(f32[12,80,128]{2,1,0:T(8,128)S(1)} %collective-permute-done.5.refs_10_) | copy-start | bytes 1474564
  107.3 0.8 copy-start.4
  108.1 6.1 %collective-permute-start.8 = (f32[4,640,128]{2,1,0:T(8,128)}, f32[4,640,128]{2,1,0:T(8,128)S(1)}, u32[]{:S(2)}, u32[]{:S(2)}) collective-permute-start(f32[4,640,128]{2,1,0:T(8,128)} %bitcast.12), channel_id=1, source_target_pairs={{0,4},{4,0},{1,5},{5,1},{2,6},{6,2},{3,7},{7,3},{8,12},{12,8},{9,1... | collective-permute-start | bytes 3932168 | tf_op jit(solution)/shard_map/ppermute | solution.py:460
  110.0 4.1 %collective-permute-start.7 = (f32[4,328,128]{2,1,0:T(8,128)S(1)}, f32[4,328,128]{2,1,0:T(8,128)S(1)}, u32[]{:S(2)}, u32[]{:S(2)}) collective-permute-start(f32[4,328,128]{2,1,0:T(8,128)S(1)} %bitcast.14), channel_id=1, source_target_pairs={{0,4},{4,0},{1,5},{5,1},{2,6},{6,2},{3,7},{7,3},{8,12},{12,8},{9,1... | collective-permute-start | bytes 2015240 | tf_op jit(solution)/shard_map/ppermute | solution.py:455
  114.2 0.9 copy-start.2
  114.2 1.3 copy-start
Sparse Core Ops, SparseCore 0:
  78.1 28.5 all-gather.2

commit v7 on v6

--- a/solution.py
+++ b/solution.py
@@ -15,9 +15,8 @@
 
 
 def forecast_kernel(
-    place, table, state, east_in, north_in, cols_in, rws_in, flds_in,
-    grid, to_left, to_right, mine, other,
-    whole, east, north, cols, rws, flds, plain, ahead, seen, sems,
+    place, table, state, east, north, cols, rws, flds, grid, to_left, to_right, mine, other,
+    plain, ahead, seen, sems
 ):
     members, fields, levels, columns, rows = state.shape
     reach = 2
@@ -25,23 +24,13 @@
     span = columns + 2 * reach
     groups = fields * levels
     first, core, origin, total_cols = place[0], place[1], place[2], place[3]
-    small = ((east_in, east), (north_in, north), (cols_in, cols), (rws_in, rws), (flds_in, flds))
-    slots = groups * columns
-    fetches = [
-        pltpu.make_async_copy(source, target, sems.at[slots + n])
-        for n, (source, target) in enumerate(((state, whole),) + small)
-    ]
-    for fetch in fetches:
-        fetch.start()
-    for fetch in fetches:
-        fetch.wait()
     copies = []
     for g in range(groups):
         for k in range(columns):
             slot = g * columns + k
             copies.append(
                 pltpu.make_async_copy(
-                    whole.at[:, g // levels, g % levels, k, :], plain.at[slot], sems.at[slot]
+                    state.at[:, g // levels, g % levels, k, :], plain.at[slot], sems.at[slot]
                 )
             )
     for copy in copies:
@@ -159,15 +148,13 @@
     classes = table.shape[1]
     first = place[0].astype(jnp.float32)
     incoming = []
-    around = place[2]
-    ring = all_levels // 2
-    for n, ref in enumerate(arrived):
-        for part in range(ring):
-            level = part
-            if n < 2:
-                level = lax.rem(around + (0, ring - 1, 1, 2)[part], ring)
-            rows_in = slice(0, ref.shape[1]) if n >= 2 else slice(length - ref.shape[1], length)
-            incoming.append((ref.at[part], remote.at[(n % 2) * ring + level, rows_in]))
+    level, at = 0, 0
+    for ref in arrived:
+        size = ref.shape[0]
+        incoming.append((ref, remote.at[level, at : at + size]))
+        at += size
+        if at == length:
+            level, at = level + 1, 0
     incoming += [(grid, local), (from_left, edges.at[0]), (from_right, edges.at[1])]
     incoming = [
         pltpu.make_async_copy(ref, target, sems.at[slabs + n])
@@ -356,16 +343,15 @@
             picks,
             picks,
         ),
-        in_specs=[smem, smem] + [anywhere] * 6,
+        in_specs=[smem, smem, anywhere] + [vmem] * 5,
         out_specs=(vmem,) * 5,
-        scratch_shapes=[pltpu.VMEM(v.shape, v.dtype) for v in (state, east, north, cols, rws, flds)]
-        + [
+        scratch_shapes=[
             pltpu.VMEM((groups * columns, members, rows), jnp.float32),
             pltpu.VMEM((groups * (columns + 4), members, rows), jnp.float32),
             pltpu.SMEM((cols.shape[0],), jnp.int32),
-            pltpu.SemaphoreType.DMA((groups * columns + 6,)),
+            pltpu.SemaphoreType.DMA((groups * columns,)),
         ],
-        compiler_params=pltpu.CompilerParams(vmem_limit_bytes=60 * 2**20),
+        compiler_params=pltpu.CompilerParams(vmem_limit_bytes=40 * 2**20),
     )(place, table, state, east, north, cols, rws, flds)
 
 
@@ -374,7 +360,7 @@
     smem = pl.BlockSpec(memory_space=pltpu.SMEM)
     vmem = pl.BlockSpec(memory_space=pltpu.VMEM)
     anywhere = pl.BlockSpec(memory_space=pl.ANY)
-    all_levels = 2 * arrived[0].shape[0]
+    all_levels = sum(part.shape[0] for part in arrived) // length
     return pl.pallas_call(
         functools.partial(analysis_kernel, len(arrived)),
         out_shape=jax.ShapeDtypeStruct(shape, jnp.float32),
@@ -388,7 +374,7 @@
             pltpu.VMEM((2, LANES, 3 * members), jnp.bfloat16),
             pltpu.VMEM((2, all_levels + levels, LANES, LANES), jnp.float32),
             pltpu.VMEM((2, 2, LANES, LANES), jnp.float32),
-            pltpu.SemaphoreType.DMA((grid.shape[0] + 2 * all_levels + 3,)),
+            pltpu.SemaphoreType.DMA((grid.shape[0] + len(arrived) + 3,)),
         ],
         compiler_params=pltpu.CompilerParams(vmem_limit_bytes=60 * 2**20),
     )(place, table, *info, *arrived, grid, from_left, from_right)
@@ -438,29 +424,20 @@
     left = [(j, i) for i, j in right]
     up = [(i, i + 1) for i in range(tiles - 1)]
     down = [(j, i) for i, j in up]
-    cut = 640
     used = batches * members + 8
-    middle = (used - cut) // 16 * 8
-    mine, to_left, to_right = lax.optimization_barrier((mine, to_left, to_right))
-    first_rows = lax.all_gather(mine[:cut], "x")
-    last_rows = mine[cut:used]
-    before = lax.ppermute(last_rows, "x", right)
-    after = lax.ppermute(last_rows, "x", left)
+    middle = used // 16 * 8
+    mine, to_left, to_right = lax.optimization_barrier((mine[:used], to_left, to_right))
+    before = lax.ppermute(mine, "x", right)
+    after = lax.ppermute(mine, "x", left)
     from_left = lax.ppermute(to_right, TILES, up)
     from_right = lax.ppermute(to_left, TILES, down)
     across_a = lax.ppermute(after[:middle], "x", left)
     across_b = lax.ppermute(before[middle:], "x", right)
-    last_rows = jnp.concatenate([last_rows, before, after, across_a, across_b], axis=0)
-    last_rows = last_rows.reshape(ring, used - cut, LANES)
-    last_swapped = lax.ppermute(last_rows, "core", swap)
-    first_rows, last_rows, from_left, from_right = lax.optimization_barrier(
-        (first_rows, last_rows, from_left, from_right)
-    )
-    arrived = [last_rows, last_swapped]
-    arrived += [first_rows, lax.ppermute(first_rows, "core", swap)]
+    parts = [mine, before, after, across_a, across_b]
+    arrived = parts + [lax.ppermute(part, "core", swap) for part in parts]
 
     facts = [obs_col, obs_row, obs_class, obs_value, obs_error]
-    where = jnp.stack([first, jnp.int32(tiles * columns), lax.axis_index("x")]).astype(jnp.int32)
+    where = jnp.stack([first, jnp.int32(tiles * columns)]).astype(jnp.int32)
     return assimilate(
         where, table, facts, arrived, grid, from_left, from_right, state.shape, used
     )

time: 158 us -> 146 us (0.924)
  between operations: 13.6 us -> 0.35 us
  starting transfers between devices: 35.5 us -> 43.4 us
  waiting for transfers between devices: 9.56 us -> 5.19 us
  Pallas kernels: 41.5 us -> 38.9 us
  other arithmetic: 2.4 us -> 0.78 us
    ppermute x4 -> x7, starting transfers between devices: 10.6 us -> 18.6 us  [the longest x5 12.1 us: shards(): arrived = parts + [lax.ppermute(part, 'core', swap) for part in parts]]
    ppermute x1, waiting for transfers between devices: 5.65 us -> 0.01 us  [shards(): across_b = lax.ppermute(before[middle:], 'x', right)]
    pallas_call x1, Pallas kernels: 6.58 us -> 4.12 us  [forecast(): pl.pallas_call(forecast_kernel, out_shape=(jax.ShapeDtypeStruct((groups *...]
    ppermute x1, waiting for transfers between devices: 1.07 us -> 3.12 us  [shards(): across_a = lax.ppermute(after[:middle], 'x', left)]
    unnamed x13 -> x40, local copies, waits for them, and re-layouts: 2.1 us -> 3.94 us
  transfers between devices with their start and end apart: 10 -> 12, of which waited for: 4 -> 3; matrix products, arithmetic and copies ran while one was open for 0% -> 0% of each run, Pallas kernels for 0% -> 0%
where the time goes in v7:
time: 146 us; the launch traced here: 144 us
  blocking collectives  51.2 us (35%)
  starting transfers between devices  43.4 us (30%)
  Pallas kernels  38.9 us (27%)
  waiting for transfers between devices  5.19 us (4%)
  local copies, waits for them, and re-layouts  4.05 us (3%)
    pallas_call x1, Pallas kernels, assimilate(): pl.pallas_call(functools.partial(analysis_kernel, len(arrived)), out_shap...  34.8 us
    all_to_all x1, blocking collectives, shards(): lax.all_to_all(mine.reshape(homes, chunk, LANES), ('z', 'y'), 0, 0, tiled...  28.3 us
    all_to_all x1, blocking collectives, shards(): lax.all_to_all(jnp.broadcast_to(mine[None], (homes, chunk, LANES)), ('z',...  22.8 us
    ppermute x5, starting transfers between devices, shards(): arrived = parts + [lax.ppermute(part, 'core', swap) for part in parts]  12.1 us
    ppermute x1, starting transfers between devices, shards(): mine = mine + lax.ppermute(other, 'core', swap)  8.75 us
    ppermute x1, starting transfers between devices, shards(): from_left = lax.ppermute(to_right, TILES, up)  7.65 us
    ppermute x1, starting transfers between devices, shards(): across_a = lax.ppermute(after[:middle], 'x', left)  4.58 us
    pallas_call x1, Pallas kernels, forecast(): pl.pallas_call(forecast_kernel, out_shape=(jax.ShapeDtypeStruct((groups *...  4.12 us
  transfers between devices with their start and end apart: 12, of which 3 were waited for; matrix products, arithmetic and copies ran while one was open for 0% of the time, Pallas kernels for 0%

profile of v7, /device:TPU:1, one launch (start us, length us, event | category | flops | bytes accessed | tf_op | source)
XLA Modules:
  0.0 143.9 jit_solution(11157782754184482771)
XLA Ops:
  0.0 0.0 copy-start.6
  0.0 0.0 copy-start.3
  0.0 0.0 copy-start.2
  0.0 0.1 pad_add_fusion.1.place
  0.1 0.6 copy-done.6
  0.7 0.0 copy-done.7
  0.7 0.0 copy-done.4
  0.7 0.0 copy-done.3
  0.7 0.0 copy-done.2
  0.8 0.0 copy-done.5
  0.8 1.2 copy-done.1
  2.0 4.1 %shard_map.100 = (f32[24,80,128]{2,1,0:T(8,128)S(1)}, f32[12,80,128]{2,1,0:T(8,128)S(1)}, f32[12,80,128]{2,1,0:T(8,128)S(1)}, f32[1024,128]{1,0:T(8,128)S(1)}, f32[1024,128]{1,0:T(8,128)S(1)}) custom-call(s32[4]{0:T(128)S(1)} %pad_add_fusion.1.place, f32[2,4]{1,0:T(2,128)S(1)} %bitcast.7, f32[80,3,2,4,128]{4,3,2,1,0:T(4,128)S(1)} %copy-done.1, ...), custom_call_target="tpu_custom_call" | custom-call | tf_op jit(solution)/shard_map/pallas_call | solution.py:337
  6.1 0.0 copy-start
  6.1 1.0 copy-done
  7.1 8.8 %collective-permute-start = (f32[1024,128]{1,0:T(8,128)S(1)}, f32[1024,128]{1,0:T(8,128)S(1)}, u32[]{:S(2)}, u32[]{:S(2)}) collective-permute-start(f32[1024,128]{1,0:T(8,128)S(1)} %get-tuple-element.14), channel_id=1, source_target_pairs={{0,4},{4,0},{1,5},{5,1},{2,6},{6,2},{3,7},{7,3},{8,12},{12,8},{9,1... | collective-permute-start | bytes 1572872 | tf_op jit(solution)/shard_map/ppermute | solution.py:414
  15.9 1.5 %collective-permute-done = f32[1024,128]{1,0:T(8,128)S(1)} collective-permute-done((f32[1024,128]{1,0:T(8,128)S(1)}, f32[1024,128]{1,0:T(8,128)S(1)}, u32[]{:S(2)}, u32[]{:S(2)}) %collective-permute-start) | collective-permute-done | bytes 524320 | tf_op jit(solution)/shard_map/ppermute | solution.py:414
  17.4 0.1 add.12
  17.5 28.3 %all_to_all.10 = f32[64,16,128]{2,1,0:T(8,128)S(1)} all-to-all(f32[64,16,128]{2,1,0:T(8,128)S(1)} %bitcast.8), channel_id=1, replica_groups=mesh['z'=8,'y'=8,'core'=2,'x'=4] {'z','y'}, dimensions={0} | all-to-all | bytes 1048576 | tf_op jit(solution)/shard_map/all_to_all | solution.py:415
  45.8 0.1 reduce_sum.9
  45.9 22.8 %all_to_all.11 = f32[64,16,128]{2,1,0:T(8,128)S(1)} all-to-all(f32[64,16,128]{2,1,0:T(8,128)S(1)} %broadcast_in_dim.2), channel_id=1, replica_groups=mesh['z'=8,'y'=8,'core'=2,'x'=4] {'z','y'}, dimensions={0} | all-to-all | bytes 1048576 | tf_op jit(solution)/shard_map/all_to_all | solution.py:417
  68.8 0.0 copy-start.8
  68.8 3.1 %collective-permute-start.1 = (f32[968,128]{1,0:T(8,128)S(1)}, f32[968,128]{1,0:T(8,128)S(1)}, u32[]{:S(2)}, u32[]{:S(2)}) collective-permute-start(f32[968,128]{1,0:T(8,128)S(1)} %slice.12.refs_5_), channel_id=1, source_target_pairs={{0,1},{1,2},{2,3},{3,0},{4,5},{5,6},{6,7},{7,4},{8,9},{9,10},{10,1... | collective-permute-start | bytes 1486856 | tf_op jit(solution)/shard_map/ppermute | solution.py:430
  71.9 3.4 %collective-permute-start.2 = (f32[968,128]{1,0:T(8,128)S(1)}, f32[968,128]{1,0:T(8,128)S(1)}, u32[]{:S(2)}, u32[]{:S(2)}) collective-permute-start(f32[968,128]{1,0:T(8,128)S(1)} %slice.12.refs_5_), channel_id=1, source_target_pairs={{1,0},{2,1},{3,2},{0,3},{5,4},{6,5},{7,6},{4,7},{9,8},{10,9},{11,1... | collective-permute-start | bytes 1486856 | tf_op jit(solution)/shard_map/ppermute | solution.py:431
  75.3 7.6 %collective-permute-start.10 = (f32[12,80,128]{2,1,0:T(8,128)S(1)}, f32[12,80,128]{2,1,0:T(8,128)S(1)}, u32[]{:S(2)}, u32[]{:S(2)}) collective-permute-start(f32[12,80,128]{2,1,0:T(8,128)S(1)} %get-tuple-element.19), channel_id=1, source_target_pairs={{0,4},{4,8},{8,12},{12,16},{16,20},{20,24},{24,28},{28,32},{32,36}... | collective-permute-start | bytes 1474568 | tf_op jit(solution)/shard_map/ppermute | solution.py:432
  83.0 1.9 %collective-permute-start.11 = (f32[12,80,128]{2,1,0:T(8,128)S(1)}, f32[12,80,128]{2,1,0:T(8,128)S(1)}, u32[]{:S(2)}, u32[]{:S(2)}) collective-permute-start(f32[12,80,128]{2,1,0:T(8,128)S(1)} %get-tuple-element.20), channel_id=1, source_target_pairs={{4,0},{8,4},{12,8},{16,12},{20,16},{24,20},{28,24},{32,28},{36,32}... | collective-permute-start | bytes 1474568 | tf_op jit(solution)/shard_map/ppermute | solution.py:433
  84.9 0.0 collective-permute-done.1.refs_6_
  84.9 0.0 copy-start.9
  84.9 1.9 %collective-permute-start.4 = (f32[488,128]{1,0:T(8,128)S(1)}, f32[488,128]{1,0:T(8,128)S(1)}, u32[]{:S(2)}, u32[]{:S(2)}) collective-permute-start(f32[488,128]{1,0:T(8,128)S(1)} %slice.14), channel_id=1, source_target_pairs={{0,1},{1,2},{2,3},{3,0},{4,5},{5,6},{6,7},{7,4},{8,9},{9,10},{10,1... | collective-permute-start | bytes 749576 | tf_op jit(solution)/shard_map/ppermute | solution.py:435
  86.9 2.9 %collective-permute-start.5 = (f32[968,128]{1,0:T(8,128)S(1)}, f32[968,128]{1,0:T(8,128)S(1)}, u32[]{:S(2)}, u32[]{:S(2)}) collective-permute-start(f32[968,128]{1,0:T(8,128)S(1)} %slice.12.refs_5_), channel_id=1, source_target_pairs={{0,4},{4,0},{1,5},{5,1},{2,6},{6,2},{3,7},{7,3},{8,12},{12,8},{9,1... | collective-permute-start | bytes 1486856 | tf_op jit(solution)/shard_map/ppermute | solution.py:437
  89.8 0.0 collective-permute-done.2.refs_7_
  89.8 0.0 copy-start.10
  89.8 1.9 %collective-permute-start.7 = (f32[968,128]{1,0:T(8,128)S(1)}, f32[968,128]{1,0:T(8,128)S(1)}, u32[]{:S(2)}, u32[]{:S(2)}) collective-permute-start(f32[968,128]{1,0:T(8,128)S(1)} %collective-permute-done.2.refs_7_), channel_id=1, source_target_pairs={{0,4},{4,0},{1,5},{5,1},{2,6},{6,2},{3,7},{7,3},{8,12},{12,8},{9,1... | collective-permute-start | bytes 1486856 | tf_op jit(solution)/shard_map/ppermute | solution.py:437
  91.7 0.0 collective-permute-done.10.refs_16_
  91.7 0.0 copy-start.14
  91.7 2.4 %collective-permute-start.6 = (f32[968,128]{1,0:T(8,128)S(1)}, f32[968,128]{1,0:T(8,128)S(1)}, u32[]{:S(2)}, u32[]{:S(2)}) collective-permute-start(f32[968,128]{1,0:T(8,128)S(1)} %collective-permute-done.1.refs_6_), channel_id=1, source_target_pairs={{0,4},{4,0},{1,5},{5,1},{2,6},{6,2},{3,7},{7,3},{8,12},{12,8},{9,1... | collective-permute-start | bytes 1486856 | tf_op jit(solution)/shard_map/ppermute | solution.py:437
  94.2 0.0 copy-done.8
  94.2 0.0 collective-permute-done.11.refs_17_
  94.2 0.0 copy-start.15
  94.2 4.6 %collective-permute-start.3 = (f32[480,128]{1,0:T(8,128)S(1)}, f32[480,128]{1,0:T(8,128)S(1)}, u32[]{:S(2)}, u32[]{:S(2)}) collective-permute-start(f32[480,128]{1,0:T(8,128)S(1)} %slice.13), channel_id=1, source_target_pairs={{1,0},{2,1},{3,2},{0,3},{5,4},{6,5},{7,6},{4,7},{9,8},{10,9},{11,1... | collective-permute-start | bytes 737288 | tf_op jit(solution)/shard_map/ppermute | solution.py:434
  98.8 0.0 collective-permute-done.4.refs_9_
  98.8 0.0 copy-start.16
  98.8 2.2 %collective-permute-start.9 = (f32[488,128]{1,0:T(8,128)S(1)}, f32[488,128]{1,0:T(8,128)S(1)}, u32[]{:S(2)}, u32[]{:S(2)}) collective-permute-start(f32[488,128]{1,0:T(8,128)S(1)} %collective-permute-done.4.refs_9_), channel_id=1, source_target_pairs={{0,4},{4,0},{1,5},{5,1},{2,6},{6,2},{3,7},{7,3},{8,12},{12,8},{9,1... | collective-permute-start | bytes 749576 | tf_op jit(solution)/shard_map/ppermute | solution.py:437
  101.0 3.1 %collective-permute-done.3.refs_8_ = f32[480,128]{1,0:T(8,128)S(1)} collective-permute-done((f32[480,128]{1,0:T(8,128)S(1)}, f32[480,128]{1,0:T(8,128)S(1)}, u32[]{:S(2)}, u32[]{:S(2)}) %collective-permute-start.3) | collective-permute-done | bytes 245792 | tf_op jit(solution)/shard_map/ppermute | solution.py:434
  104.2 2.7 %collective-permute-start.8 = (f32[480,128]{1,0:T(8,128)S(1)}, f32[480,128]{1,0:T(8,128)S(1)}, u32[]{:S(2)}, u32[]{:S(2)}) collective-permute-start(f32[480,128]{1,0:T(8,128)S(1)} %collective-permute-done.3.refs_8_), channel_id=1, source_target_pairs={{0,4},{4,0},{1,5},{5,1},{2,6},{6,2},{3,7},{7,3},{8,12},{12,8},{9,1... | collective-permute-start | bytes 737288 | tf_op jit(solution)/shard_map/ppermute | solution.py:437
  106.9 0.6 pad_add_fusion.place
  107.4 0.0 copy-done.9
  107.4 0.0 collective-permute-done.5.refs_10_
  107.4 0.5 collective-permute-done.8.refs_13_
  108.0 0.0 collective-permute-done.7.refs_12_
  108.0 0.0 collective-permute-done.6.refs_11_
  108.0 0.0 copy-done.14
  108.0 0.0 copy-start.13
  108.0 0.0 collective-permute-done.9.refs_14_
  108.0 0.0 copy-done.15
  108.0 0.0 copy-done.16
  108.0 0.0 copy-start.17
  108.0 0.0 copy-done.10
  108.1 0.0 copy-done.18
  108.1 0.2 copy-done.11
  108.2 0.4 copy-done.19
  108.7 0.2 copy-done.12
  108.9 0.2 copy-done.13
  109.0 0.1 copy-done.17
  109.1 34.8 %shard_map.101 = f32[80,3,2,4,128]{4,3,2,1,0:T(4,128)} custom-call(s32[2]{0:T(128)} %pad_add_fusion.place, f32[2,4]{1,0:T(2,128)} %bitcast.6, s32[12,128]{1,0:T(8,128)} %refs_0_.1, s32[12,128]{1,0:T(8,128)} %refs_1_.1, s32[12,128]{1,0:T(8,128)} %refs_2_.1, f32[12,128]{1,0:T(8,128)} %refs_3_.1, f32[12,128]{1,0:T(8,128)} %refs_4_.1, f32[968,128]{1,0:T(8,128)} %copy-done.8, ...), custom_call_target="tpu_custom_call" | custom-call | tf_op jit(solution)/shard_map/pallas_call | solution.py:364
  (12 shorter events, 0.1 us)
Async XLA Ops:
  0.0 0.7 copy-start.6
  0.0 0.7 copy-start.7
  0.0 0.7 copy-start.4
  0.0 0.7 copy-start.3
  0.0 0.7 copy-start.2
  0.1 0.7 copy-start.5
  0.8 1.2 copy-start.1
  6.1 1.0 copy-start
  7.1 10.3 %collective-permute-start = (f32[1024,128]{1,0:T(8,128)S(1)}, f32[1024,128]{1,0:T(8,128)S(1)}, u32[]{:S(2)}, u32[]{:S(2)}) collective-permute-start(f32[1024,128]{1,0:T(8,128)S(1)} %get-tuple-element.14), channel_id=1, source_target_pairs={{0,4},{4,0},{1,5},{5,1},{2,6},{6,2},{3,7},{7,3},{8,12},{12,8},{9,1... | collective-permute-start | bytes 1572872 | tf_op jit(solution)/shard_map/ppermute | solution.py:414
  68.8 25.4 %copy-start.8 = (f32[968,128]{1,0:T(8,128)}, f32[968,128]{1,0:T(8,128)S(1)}, u32[]{:S(2)}) copy-start(f32[968,128]{1,0:T(8,128)S(1)} %slice.12.refs_5_) | copy-start | bytes 1486852
  68.8 16.1 %collective-permute-start.1 = (f32[968,128]{1,0:T(8,128)S(1)}, f32[968,128]{1,0:T(8,128)S(1)}, u32[]{:S(2)}, u32[]{:S(2)}) collective-permute-start(f32[968,128]{1,0:T(8,128)S(1)} %slice.12.refs_5_), channel_id=1, source_target_pairs={{0,1},{1,2},{2,3},{3,0},{4,5},{5,6},{6,7},{7,4},{8,9},{9,10},{10,1... | collective-permute-start | bytes 1486856 | tf_op jit(solution)/shard_map/ppermute | solution.py:430
  71.9 17.8 %collective-permute-start.2 = (f32[968,128]{1,0:T(8,128)S(1)}, f32[968,128]{1,0:T(8,128)S(1)}, u32[]{:S(2)}, u32[]{:S(2)}) collective-permute-start(f32[968,128]{1,0:T(8,128)S(1)} %slice.12.refs_5_), channel_id=1, source_target_pairs={{1,0},{2,1},{3,2},{0,3},{5,4},{6,5},{7,6},{4,7},{9,8},{10,9},{11,1... | collective-permute-start | bytes 1486856 | tf_op jit(solution)/shard_map/ppermute | solution.py:431
  75.3 16.4 %collective-permute-start.10 = (f32[12,80,128]{2,1,0:T(8,128)S(1)}, f32[12,80,128]{2,1,0:T(8,128)S(1)}, u32[]{:S(2)}, u32[]{:S(2)}) collective-permute-start(f32[12,80,128]{2,1,0:T(8,128)S(1)} %get-tuple-element.19), channel_id=1, source_target_pairs={{0,4},{4,8},{8,12},{12,16},{16,20},{20,24},{24,28},{28,32},{32,36}... | collective-permute-start | bytes 1474568 | tf_op jit(solution)/shard_map/ppermute | solution.py:432
  83.0 11.2 %collective-permute-start.11 = (f32[12,80,128]{2,1,0:T(8,128)S(1)}, f32[12,80,128]{2,1,0:T(8,128)S(1)}, u32[]{:S(2)}, u32[]{:S(2)}) collective-permute-start(f32[12,80,128]{2,1,0:T(8,128)S(1)} %get-tuple-element.20), channel_id=1, source_target_pairs={{4,0},{8,4},{12,8},{16,12},{20,16},{24,20},{28,24},{32,28},{36,32}... | collective-permute-start | bytes 1474568 | tf_op jit(solution)/shard_map/ppermute | solution.py:433
  84.9 22.5 %copy-start.9 = (f32[968,128]{1,0:T(8,128)}, f32[968,128]{1,0:T(8,128)S(1)}, u32[]{:S(2)}) copy-start(f32[968,128]{1,0:T(8,128)S(1)} %collective-permute-done.1.refs_6_) | copy-start | bytes 1486852
  84.9 13.9 %collective-permute-start.4 = (f32[488,128]{1,0:T(8,128)S(1)}, f32[488,128]{1,0:T(8,128)S(1)}, u32[]{:S(2)}, u32[]{:S(2)}) collective-permute-start(f32[488,128]{1,0:T(8,128)S(1)} %slice.14), channel_id=1, source_target_pairs={{0,1},{1,2},{2,3},{3,0},{4,5},{5,6},{6,7},{7,4},{8,9},{9,10},{10,1... | collective-permute-start | bytes 749576 | tf_op jit(solution)/shard_map/ppermute | solution.py:435
  86.9 20.6 %collective-permute-start.5 = (f32[968,128]{1,0:T(8,128)S(1)}, f32[968,128]{1,0:T(8,128)S(1)}, u32[]{:S(2)}, u32[]{:S(2)}) collective-permute-start(f32[968,128]{1,0:T(8,128)S(1)} %slice.12.refs_5_), channel_id=1, source_target_pairs={{0,4},{4,0},{1,5},{5,1},{2,6},{6,2},{3,7},{7,3},{8,12},{12,8},{9,1... | collective-permute-start | bytes 1486856 | tf_op jit(solution)/shard_map/ppermute | solution.py:437
  89.8 18.3 %copy-start.10 = (f32[968,128]{1,0:T(8,128)}, f32[968,128]{1,0:T(8,128)S(1)}, u32[]{:S(2)}) copy-start(f32[968,128]{1,0:T(8,128)S(1)} %collective-permute-done.2.refs_7_) | copy-start | bytes 1486852
  89.8 18.2 %collective-permute-start.7 = (f32[968,128]{1,0:T(8,128)S(1)}, f32[968,128]{1,0:T(8,128)S(1)}, u32[]{:S(2)}, u32[]{:S(2)}) collective-permute-start(f32[968,128]{1,0:T(8,128)S(1)} %collective-permute-done.2.refs_7_), channel_id=1, source_target_pairs={{0,4},{4,0},{1,5},{5,1},{2,6},{6,2},{3,7},{7,3},{8,12},{12,8},{9,1... | collective-permute-start | bytes 1486856 | tf_op jit(solution)/shard_map/ppermute | solution.py:437
  91.7 16.3 %copy-start.14 = (f32[12,80,128]{2,1,0:T(8,128)}, f32[12,80,128]{2,1,0:T(8,128)S(1)}, u32[]{:S(2)}) copy-start(f32[12,80,128]{2,1,0:T(8,128)S(1)} %collective-permute-done.10.refs_16_) | copy-start | bytes 1474564
  91.7 16.2 %collective-permute-start.6 = (f32[968,128]{1,0:T(8,128)S(1)}, f32[968,128]{1,0:T(8,128)S(1)}, u32[]{:S(2)}, u32[]{:S(2)}) collective-permute-start(f32[968,128]{1,0:T(8,128)S(1)} %collective-permute-done.1.refs_6_), channel_id=1, source_target_pairs={{0,4},{4,0},{1,5},{5,1},{2,6},{6,2},{3,7},{7,3},{8,12},{12,8},{9,1... | collective-permute-start | bytes 1486856 | tf_op jit(solution)/shard_map/ppermute | solution.py:437
  94.2 13.8 %copy-start.15 = (f32[12,80,128]{2,1,0:T(8,128)}, f32[12,80,128]{2,1,0:T(8,128)S(1)}, u32[]{:S(2)}) copy-start(f32[12,80,128]{2,1,0:T(8,128)S(1)} %collective-permute-done.11.refs_17_) | copy-start | bytes 1474564
  94.2 9.9 %collective-permute-start.3 = (f32[480,128]{1,0:T(8,128)S(1)}, f32[480,128]{1,0:T(8,128)S(1)}, u32[]{:S(2)}, u32[]{:S(2)}) collective-permute-start(f32[480,128]{1,0:T(8,128)S(1)} %slice.13), channel_id=1, source_target_pairs={{1,0},{2,1},{3,2},{0,3},{5,4},{6,5},{7,6},{4,7},{9,8},{10,9},{11,1... | collective-permute-start | bytes 737288 | tf_op jit(solution)/shard_map/ppermute | solution.py:434
  98.8 9.2 %copy-start.16 = (f32[488,128]{1,0:T(8,128)}, f32[488,128]{1,0:T(8,128)S(1)}, u32[]{:S(2)}) copy-start(f32[488,128]{1,0:T(8,128)S(1)} %collective-permute-done.4.refs_9_) | copy-start | bytes 749572
  98.8 9.2 %collective-permute-start.9 = (f32[488,128]{1,0:T(8,128)S(1)}, f32[488,128]{1,0:T(8,128)S(1)}, u32[]{:S(2)}, u32[]{:S(2)}) collective-permute-start(f32[488,128]{1,0:T(8,128)S(1)} %collective-permute-done.4.refs_9_), channel_id=1, source_target_pairs={{0,4},{4,0},{1,5},{5,1},{2,6},{6,2},{3,7},{7,3},{8,12},{12,8},{9,1... | collective-permute-start | bytes 749576 | tf_op jit(solution)/shard_map/ppermute | solution.py:437
  104.2 3.9 %copy-start.18 = (f32[480,128]{1,0:T(8,128)}, f32[480,128]{1,0:T(8,128)S(1)}, u32[]{:S(2)}) copy-start(f32[480,128]{1,0:T(8,128)S(1)} %collective-permute-done.3.refs_8_) | copy-start | bytes 737284
  104.2 3.8 %collective-permute-start.8 = (f32[480,128]{1,0:T(8,128)S(1)}, f32[480,128]{1,0:T(8,128)S(1)}, u32[]{:S(2)}, u32[]{:S(2)}) collective-permute-start(f32[480,128]{1,0:T(8,128)S(1)} %collective-permute-done.3.refs_8_), channel_id=1, source_target_pairs={{0,4},{4,0},{1,5},{5,1},{2,6},{6,2},{3,7},{7,3},{8,12},{12,8},{9,1... | collective-permute-start | bytes 737288 | tf_op jit(solution)/shard_map/ppermute | solution.py:437
  107.4 0.8 copy-start.11
  108.0 0.7 copy-start.19
  108.0 0.9 copy-start.12
  108.0 1.0 copy-start.13
  108.0 1.1 copy-start.17

commit v8 on v7

--- a/solution.py
+++ b/solution.py
@@ -433,6 +433,7 @@
     from_right = lax.ppermute(to_left, TILES, down)
     across_a = lax.ppermute(after[:middle], "x", left)
     across_b = lax.ppermute(before[middle:], "x", right)
+    mine, before, after, across_a = lax.optimization_barrier((mine, before, after, across_a))
     parts = [mine, before, after, across_a, across_b]
     arrived = parts + [lax.ppermute(part, "core", swap) for part in parts]
 

time: 146 us -> 146 us (level); the launches traced: 144 us -> 145 us
    ppermute x1, waiting for transfers between devices: 3.12 us -> 0.01 us  [shards(): across_a = lax.ppermute(after[:middle], 'x', left)]
    ppermute x1, starting transfers between devices: 1.92 us -> 4.83 us  [shards(): from_right = lax.ppermute(to_left, TILES, down)]
    ppermute x1, waiting for transfers between devices: 0.01 us -> 2.6 us  [shards(): across_b = lax.ppermute(before[middle:], 'x', right)]
    ppermute x5, starting transfers between devices: 12.1 us -> 10.6 us  [shards(): arrived = parts + [lax.ppermute(part, 'core', swap) for part in parts]]
where the time goes in v8:
time: 146 us; the launch traced here: 145 us
  blocking collectives  52.3 us (36%)
  starting transfers between devices  44.6 us (31%)
  Pallas kernels  38.3 us (26%)
  waiting for transfers between devices  4.93 us (3%)
  local copies, waits for them, and re-layouts  4.19 us (3%)
    pallas_call x1, Pallas kernels, assimilate(): pl.pallas_call(functools.partial(analysis_kernel, len(arrived)), out_shap...  34.8 us
    all_to_all x1, blocking collectives, shards(): lax.all_to_all(mine.reshape(homes, chunk, LANES), ('z', 'y'), 0, 0, tiled...  29.5 us
    all_to_all x1, blocking collectives, shards(): lax.all_to_all(jnp.broadcast_to(mine[None], (homes, chunk, LANES)), ('z',...  22.8 us
    ppermute x5, starting transfers between devices, shards(): arrived = parts + [lax.ppermute(part, 'core', swap) for part in parts]  10.6 us
    ppermute x1, starting transfers between devices, shards(): mine = mine + lax.ppermute(other, 'core', swap)  8.75 us
    ppermute x1, starting transfers between devices, shards(): from_left = lax.ppermute(to_right, TILES, up)  7.37 us
    ppermute x1, starting transfers between devices, shards(): across_a = lax.ppermute(after[:middle], 'x', left)  4.85 us
    ppermute x1, starting transfers between devices, shards(): from_right = lax.ppermute(to_left, TILES, down)  4.83 us
  transfers between devices with their start and end apart: 12, of which 3 were waited for; matrix products, arithmetic and copies ran while one was open for 0% of the time, Pallas kernels for 0%

profile of v8, /device:TPU:1, one launch (start us, length us, event | category | flops | bytes accessed | tf_op | source)
XLA Modules:
  0.0 145.5 jit_solution(8821724469335193484)
XLA Ops:
  0.0 0.0 copy-start.3
  0.0 0.0 copy-start.2
  0.0 0.1 pad_add_fusion.1.place
  0.1 0.6 copy-done.6
  0.7 0.0 copy-done.7
  0.7 0.0 copy-done.4
  0.7 0.0 copy-done.3
  0.7 0.0 copy-done.2
  0.8 0.0 copy-done.5
  0.8 1.2 copy-done.1
  2.0 3.5 %shard_map.100 = (f32[24,80,128]{2,1,0:T(8,128)S(1)}, f32[12,80,128]{2,1,0:T(8,128)S(1)}, f32[12,80,128]{2,1,0:T(8,128)S(1)}, f32[1024,128]{1,0:T(8,128)S(1)}, f32[1024,128]{1,0:T(8,128)S(1)}) custom-call(s32[4]{0:T(128)S(1)} %pad_add_fusion.1.place, f32[2,4]{1,0:T(2,128)S(1)} %bitcast.7, f32[80,3,2,4,128]{4,3,2,1,0:T(4,128)S(1)} %copy-done.1, ...), custom_call_target="tpu_custom_call" | custom-call | tf_op jit(solution)/shard_map/pallas_call | solution.py:337
  5.6 0.0 copy-start
  5.6 1.0 copy-done
  6.5 8.8 %collective-permute-start = (f32[1024,128]{1,0:T(8,128)S(1)}, f32[1024,128]{1,0:T(8,128)S(1)}, u32[]{:S(2)}, u32[]{:S(2)}) collective-permute-start(f32[1024,128]{1,0:T(8,128)S(1)} %get-tuple-element.18), channel_id=1, source_target_pairs={{0,4},{4,0},{1,5},{5,1},{2,6},{6,2},{3,7},{7,3},{8,12},{12,8},{9,1... | collective-permute-start | bytes 1572872 | tf_op jit(solution)/shard_map/ppermute | solution.py:414
  15.3 1.5 %collective-permute-done = f32[1024,128]{1,0:T(8,128)S(1)} collective-permute-done((f32[1024,128]{1,0:T(8,128)S(1)}, f32[1024,128]{1,0:T(8,128)S(1)}, u32[]{:S(2)}, u32[]{:S(2)}) %collective-permute-start) | collective-permute-done | bytes 524320 | tf_op jit(solution)/shard_map/ppermute | solution.py:414
  16.8 0.1 add.12
  16.9 29.5 %all_to_all.10 = f32[64,16,128]{2,1,0:T(8,128)S(1)} all-to-all(f32[64,16,128]{2,1,0:T(8,128)S(1)} %bitcast.8), channel_id=1, replica_groups=mesh['z'=8,'y'=8,'core'=2,'x'=4] {'z','y'}, dimensions={0} | all-to-all | bytes 1048576 | tf_op jit(solution)/shard_map/all_to_all | solution.py:415
  46.4 0.1 reduce_sum.9
  46.5 22.8 %all_to_all.11 = f32[64,16,128]{2,1,0:T(8,128)S(1)} all-to-all(f32[64,16,128]{2,1,0:T(8,128)S(1)} %broadcast_in_dim.2), channel_id=1, replica_groups=mesh['z'=8,'y'=8,'core'=2,'x'=4] {'z','y'}, dimensions={0} | all-to-all | bytes 1048576 | tf_op jit(solution)/shard_map/all_to_all | solution.py:417
  69.3 0.0 copy-start.8
  69.4 4.4 %collective-permute-start.2 = (f32[968,128]{1,0:T(8,128)S(1)}, f32[968,128]{1,0:T(8,128)S(1)}, u32[]{:S(2)}, u32[]{:S(2)}) collective-permute-start(f32[968,128]{1,0:T(8,128)S(1)} %slice.12.refs_5_), channel_id=1, source_target_pairs={{1,0},{2,1},{3,2},{0,3},{5,4},{6,5},{7,6},{4,7},{9,8},{10,9},{11,1... | collective-permute-start | bytes 1486856 | tf_op jit(solution)/shard_map/ppermute | solution.py:431
  73.7 1.9 %collective-permute-start.1 = (f32[968,128]{1,0:T(8,128)S(1)}, f32[968,128]{1,0:T(8,128)S(1)}, u32[]{:S(2)}, u32[]{:S(2)}) collective-permute-start(f32[968,128]{1,0:T(8,128)S(1)} %slice.12.refs_5_), channel_id=1, source_target_pairs={{0,1},{1,2},{2,3},{3,0},{4,5},{5,6},{6,7},{7,4},{8,9},{9,10},{10,1... | collective-permute-start | bytes 1486856 | tf_op jit(solution)/shard_map/ppermute | solution.py:430
  75.7 7.4 %collective-permute-start.10 = (f32[12,80,128]{2,1,0:T(8,128)S(1)}, f32[12,80,128]{2,1,0:T(8,128)S(1)}, u32[]{:S(2)}, u32[]{:S(2)}) collective-permute-start(f32[12,80,128]{2,1,0:T(8,128)S(1)} %get-tuple-element.27), channel_id=1, source_target_pairs={{0,4},{4,8},{8,12},{12,16},{16,20},{20,24},{24,28},{28,32},{32,36}... | collective-permute-start | bytes 1474568 | tf_op jit(solution)/shard_map/ppermute | solution.py:432
  83.1 0.0 collective-permute-done.2.refs_7_
  83.1 0.0 copy-start.10
  83.1 4.9 %collective-permute-start.3 = (f32[480,128]{1,0:T(8,128)S(1)}, f32[480,128]{1,0:T(8,128)S(1)}, u32[]{:S(2)}, u32[]{:S(2)}) collective-permute-start(f32[480,128]{1,0:T(8,128)S(1)} %slice.13), channel_id=1, source_target_pairs={{1,0},{2,1},{3,2},{0,3},{5,4},{6,5},{7,6},{4,7},{9,8},{10,9},{11,1... | collective-permute-start | bytes 737288 | tf_op jit(solution)/shard_map/ppermute | solution.py:434
  88.0 4.8 %collective-permute-start.11 = (f32[12,80,128]{2,1,0:T(8,128)S(1)}, f32[12,80,128]{2,1,0:T(8,128)S(1)}, u32[]{:S(2)}, u32[]{:S(2)}) collective-permute-start(f32[12,80,128]{2,1,0:T(8,128)S(1)} %get-tuple-element.28), channel_id=1, source_target_pairs={{4,0},{8,4},{12,8},{16,12},{20,16},{24,20},{28,24},{32,28},{36,32}... | collective-permute-start | bytes 1474568 | tf_op jit(solution)/shard_map/ppermute | solution.py:433
  92.8 0.0 collective-permute-done.1.refs_6_
  92.8 0.0 copy-start.9
  92.8 1.9 %collective-permute-start.4 = (f32[488,128]{1,0:T(8,128)S(1)}, f32[488,128]{1,0:T(8,128)S(1)}, u32[]{:S(2)}, u32[]{:S(2)}) collective-permute-start(f32[488,128]{1,0:T(8,128)S(1)} %slice.14), channel_id=1, source_target_pairs={{0,1},{1,2},{2,3},{3,0},{4,5},{5,6},{6,7},{7,4},{8,9},{9,10},{10,1... | collective-permute-start | bytes 749576 | tf_op jit(solution)/shard_map/ppermute | solution.py:435
  94.8 0.0 collective-permute-done.3.refs_8_
  94.8 0.0 copy-done.8
  94.8 0.0 copy-start.18
  94.8 1.9 %collective-permute-start.5 = (f32[968,128]{1,0:T(8,128)S(1)}, f32[968,128]{1,0:T(8,128)S(1)}, u32[]{:S(2)}, u32[]{:S(2)}) collective-permute-start(f32[968,128]{1,0:T(8,128)S(1)} %slice.12.refs_5_), channel_id=1, source_target_pairs={{0,4},{4,0},{1,5},{5,1},{2,6},{6,2},{3,7},{7,3},{8,12},{12,8},{9,1... | collective-permute-start | bytes 1486856 | tf_op jit(solution)/shard_map/ppermute | solution.py:438
  96.7 2.4 %collective-permute-start.6 = (f32[968,128]{1,0:T(8,128)S(1)}, f32[968,128]{1,0:T(8,128)S(1)}, u32[]{:S(2)}, u32[]{:S(2)}) collective-permute-start(f32[968,128]{1,0:T(8,128)S(1)} %collective-permute-done.1.refs_6_), channel_id=1, source_target_pairs={{0,4},{4,0},{1,5},{5,1},{2,6},{6,2},{3,7},{7,3},{8,12},{12,8},{9,1... | collective-permute-start | bytes 1486856 | tf_op jit(solution)/shard_map/ppermute | solution.py:438
  99.1 0.0 collective-permute-done.10.refs_16_
  99.2 0.0 copy-start.14
  99.2 1.9 %collective-permute-start.7 = (f32[968,128]{1,0:T(8,128)S(1)}, f32[968,128]{1,0:T(8,128)S(1)}, u32[]{:S(2)}, u32[]{:S(2)}) collective-permute-start(f32[968,128]{1,0:T(8,128)S(1)} %collective-permute-done.2.refs_7_), channel_id=1, source_target_pairs={{0,4},{4,0},{1,5},{5,1},{2,6},{6,2},{3,7},{7,3},{8,12},{12,8},{9,1... | collective-permute-start | bytes 1486856 | tf_op jit(solution)/shard_map/ppermute | solution.py:438
  101.1 2.6 %collective-permute-done.4.refs_9_ = f32[488,128]{1,0:T(8,128)S(1)} collective-permute-done((f32[488,128]{1,0:T(8,128)S(1)}, f32[488,128]{1,0:T(8,128)S(1)}, u32[]{:S(2)}, u32[]{:S(2)}) %collective-permute-start.4) | collective-permute-done | bytes 249888 | tf_op jit(solution)/shard_map/ppermute | solution.py:435
  103.7 2.3 %collective-permute-start.9 = (f32[488,128]{1,0:T(8,128)S(1)}, f32[488,128]{1,0:T(8,128)S(1)}, u32[]{:S(2)}, u32[]{:S(2)}) collective-permute-start(f32[488,128]{1,0:T(8,128)S(1)} %collective-permute-done.4.refs_9_), channel_id=1, source_target_pairs={{0,4},{4,0},{1,5},{5,1},{2,6},{6,2},{3,7},{7,3},{8,12},{12,8},{9,1... | collective-permute-start | bytes 749576 | tf_op jit(solution)/shard_map/ppermute | solution.py:438
  106.0 0.0 collective-permute-done.11.refs_17_
  106.0 0.0 copy-start.15
  106.0 2.0 %collective-permute-start.8 = (f32[480,128]{1,0:T(8,128)S(1)}, f32[480,128]{1,0:T(8,128)S(1)}, u32[]{:S(2)}, u32[]{:S(2)}) collective-permute-start(f32[480,128]{1,0:T(8,128)S(1)} %collective-permute-done.3.refs_8_), channel_id=1, source_target_pairs={{0,4},{4,0},{1,5},{5,1},{2,6},{6,2},{3,7},{7,3},{8,12},{12,8},{9,1... | collective-permute-start | bytes 737288 | tf_op jit(solution)/shard_map/ppermute | solution.py:438
  108.0 0.6 pad_add_fusion.place
  108.6 0.8 collective-permute-done.8.refs_13_
  109.4 0.0 collective-permute-done.9.refs_14_
  109.4 0.0 collective-permute-done.5.refs_10_
  109.4 0.0 copy-start.11
  109.4 0.0 collective-permute-done.6.refs_11_
  109.5 0.0 copy-start.12
  109.5 0.0 collective-permute-done.7.refs_12_
  109.5 0.0 copy-done.18
  109.5 0.0 copy-done.14
  109.5 0.0 copy-done.16
  109.5 0.0 copy-done.15
  109.5 0.0 copy-start.13
  109.5 0.0 copy-done.10
  109.5 0.0 copy-done.9
  109.5 0.6 copy-done.19
  110.1 0.1 copy-done.17
  110.2 0.1 copy-done.11
  110.4 0.2 copy-done.12
  110.5 0.2 copy-done.13
  110.7 34.8 %shard_map.101 = f32[80,3,2,4,128]{4,3,2,1,0:T(4,128)} custom-call(s32[2]{0:T(128)} %pad_add_fusion.place, f32[2,4]{1,0:T(2,128)} %bitcast.6, s32[12,128]{1,0:T(8,128)} %refs_0_.1, s32[12,128]{1,0:T(8,128)} %refs_1_.1, s32[12,128]{1,0:T(8,128)} %refs_2_.1, f32[12,128]{1,0:T(8,128)} %refs_3_.1, f32[12,128]{1,0:T(8,128)} %refs_4_.1, f32[968,128]{1,0:T(8,128)} %copy-done.8, ...), custom_call_target="tpu_custom_call" | custom-call | tf_op jit(solution)/shard_map/pallas_call | solution.py:364
  (12 shorter events, 0.1 us)
Async XLA Ops:
  0.0 0.7 copy-start.6
  0.0 0.7 copy-start.7
  0.0 0.7 copy-start.4
  0.0 0.7 copy-start.3
  0.0 0.7 copy-start.2
  0.1 0.7 copy-start.5
  0.8 1.2 copy-start.1
  5.6 1.0 copy-start
  6.5 10.3 %collective-permute-start = (f32[1024,128]{1,0:T(8,128)S(1)}, f32[1024,128]{1,0:T(8,128)S(1)}, u32[]{:S(2)}, u32[]{:S(2)}) collective-permute-start(f32[1024,128]{1,0:T(8,128)S(1)} %get-tuple-element.18), channel_id=1, source_target_pairs={{0,4},{4,0},{1,5},{5,1},{2,6},{6,2},{3,7},{7,3},{8,12},{12,8},{9,1... | collective-permute-start | bytes 1572872 | tf_op jit(solution)/shard_map/ppermute | solution.py:414
  69.3 25.4 %copy-start.8 = (f32[968,128]{1,0:T(8,128)}, f32[968,128]{1,0:T(8,128)S(1)}, u32[]{:S(2)}) copy-start(f32[968,128]{1,0:T(8,128)S(1)} %slice.12.refs_5_) | copy-start | bytes 1486852
  69.4 13.7 %collective-permute-start.2 = (f32[968,128]{1,0:T(8,128)S(1)}, f32[968,128]{1,0:T(8,128)S(1)}, u32[]{:S(2)}, u32[]{:S(2)}) collective-permute-start(f32[968,128]{1,0:T(8,128)S(1)} %slice.12.refs_5_), channel_id=1, source_target_pairs={{1,0},{2,1},{3,2},{0,3},{5,4},{6,5},{7,6},{4,7},{9,8},{10,9},{11,1... | collective-permute-start | bytes 1486856 | tf_op jit(solution)/shard_map/ppermute | solution.py:431
  73.7 19.1 %collective-permute-start.1 = (f32[968,128]{1,0:T(8,128)S(1)}, f32[968,128]{1,0:T(8,128)S(1)}, u32[]{:S(2)}, u32[]{:S(2)}) collective-permute-start(f32[968,128]{1,0:T(8,128)S(1)} %slice.12.refs_5_), channel_id=1, source_target_pairs={{0,1},{1,2},{2,3},{3,0},{4,5},{5,6},{6,7},{7,4},{8,9},{9,10},{10,1... | collective-permute-start | bytes 1486856 | tf_op jit(solution)/shard_map/ppermute | solution.py:430
  75.7 23.5 %collective-permute-start.10 = (f32[12,80,128]{2,1,0:T(8,128)S(1)}, f32[12,80,128]{2,1,0:T(8,128)S(1)}, u32[]{:S(2)}, u32[]{:S(2)}) collective-permute-start(f32[12,80,128]{2,1,0:T(8,128)S(1)} %get-tuple-element.27), channel_id=1, source_target_pairs={{0,4},{4,8},{8,12},{12,16},{16,20},{20,24},{24,28},{28,32},{32,36}... | collective-permute-start | bytes 1474568 | tf_op jit(solution)/shard_map/ppermute | solution.py:432
  83.1 26.5 %copy-start.10 = (f32[968,128]{1,0:T(8,128)}, f32[968,128]{1,0:T(8,128)S(1)}, u32[]{:S(2)}) copy-start(f32[968,128]{1,0:T(8,128)S(1)} %collective-permute-done.2.refs_7_) | copy-start | bytes 1486852
  83.1 11.7 %collective-permute-start.3 = (f32[480,128]{1,0:T(8,128)S(1)}, f32[480,128]{1,0:T(8,128)S(1)}, u32[]{:S(2)}, u32[]{:S(2)}) collective-permute-start(f32[480,128]{1,0:T(8,128)S(1)} %slice.13), channel_id=1, source_target_pairs={{1,0},{2,1},{3,2},{0,3},{5,4},{6,5},{7,6},{4,7},{9,8},{10,9},{11,1... | collective-permute-start | bytes 737288 | tf_op jit(solution)/shard_map/ppermute | solution.py:434
  88.0 18.0 %collective-permute-start.11 = (f32[12,80,128]{2,1,0:T(8,128)S(1)}, f32[12,80,128]{2,1,0:T(8,128)S(1)}, u32[]{:S(2)}, u32[]{:S(2)}) collective-permute-start(f32[12,80,128]{2,1,0:T(8,128)S(1)} %get-tuple-element.28), channel_id=1, source_target_pairs={{4,0},{8,4},{12,8},{16,12},{20,16},{24,20},{28,24},{32,28},{36,32}... | collective-permute-start | bytes 1474568 | tf_op jit(solution)/shard_map/ppermute | solution.py:433
  92.8 16.7 %copy-start.9 = (f32[968,128]{1,0:T(8,128)}, f32[968,128]{1,0:T(8,128)S(1)}, u32[]{:S(2)}) copy-start(f32[968,128]{1,0:T(8,128)S(1)} %collective-permute-done.1.refs_6_) | copy-start | bytes 1486852
  92.8 10.9 %collective-permute-start.4 = (f32[488,128]{1,0:T(8,128)S(1)}, f32[488,128]{1,0:T(8,128)S(1)}, u32[]{:S(2)}, u32[]{:S(2)}) collective-permute-start(f32[488,128]{1,0:T(8,128)S(1)} %slice.14), channel_id=1, source_target_pairs={{0,1},{1,2},{2,3},{3,0},{4,5},{5,6},{6,7},{7,4},{8,9},{9,10},{10,1... | collective-permute-start | bytes 749576 | tf_op jit(solution)/shard_map/ppermute | solution.py:435
  94.8 14.7 %copy-start.18 = (f32[480,128]{1,0:T(8,128)}, f32[480,128]{1,0:T(8,128)S(1)}, u32[]{:S(2)}) copy-start(f32[480,128]{1,0:T(8,128)S(1)} %collective-permute-done.3.refs_8_) | copy-start | bytes 737284
  94.8 14.6 %collective-permute-start.5 = (f32[968,128]{1,0:T(8,128)S(1)}, f32[968,128]{1,0:T(8,128)S(1)}, u32[]{:S(2)}, u32[]{:S(2)}) collective-permute-start(f32[968,128]{1,0:T(8,128)S(1)} %slice.12.refs_5_), channel_id=1, source_target_pairs={{0,4},{4,0},{1,5},{5,1},{2,6},{6,2},{3,7},{7,3},{8,12},{12,8},{9,1... | collective-permute-start | bytes 1486856 | tf_op jit(solution)/shard_map/ppermute | solution.py:438
  96.7 12.7 %collective-permute-start.6 = (f32[968,128]{1,0:T(8,128)S(1)}, f32[968,128]{1,0:T(8,128)S(1)}, u32[]{:S(2)}, u32[]{:S(2)}) collective-permute-start(f32[968,128]{1,0:T(8,128)S(1)} %collective-permute-done.1.refs_6_), channel_id=1, source_target_pairs={{0,4},{4,0},{1,5},{5,1},{2,6},{6,2},{3,7},{7,3},{8,12},{12,8},{9,1... | collective-permute-start | bytes 1486856 | tf_op jit(solution)/shard_map/ppermute | solution.py:438
  99.2 10.3 %copy-start.14 = (f32[12,80,128]{2,1,0:T(8,128)}, f32[12,80,128]{2,1,0:T(8,128)S(1)}, u32[]{:S(2)}) copy-start(f32[12,80,128]{2,1,0:T(8,128)S(1)} %collective-permute-done.10.refs_16_) | copy-start | bytes 1474564
  99.2 10.3 %collective-permute-start.7 = (f32[968,128]{1,0:T(8,128)S(1)}, f32[968,128]{1,0:T(8,128)S(1)}, u32[]{:S(2)}, u32[]{:S(2)}) collective-permute-start(f32[968,128]{1,0:T(8,128)S(1)} %collective-permute-done.2.refs_7_), channel_id=1, source_target_pairs={{0,4},{4,0},{1,5},{5,1},{2,6},{6,2},{3,7},{7,3},{8,12},{12,8},{9,1... | collective-permute-start | bytes 1486856 | tf_op jit(solution)/shard_map/ppermute | solution.py:438
  103.7 5.8 %copy-start.16 = (f32[488,128]{1,0:T(8,128)}, f32[488,128]{1,0:T(8,128)S(1)}, u32[]{:S(2)}) copy-start(f32[488,128]{1,0:T(8,128)S(1)} %collective-permute-done.4.refs_9_) | copy-start | bytes 749572
  103.7 5.7 %collective-permute-start.9 = (f32[488,128]{1,0:T(8,128)S(1)}, f32[488,128]{1,0:T(8,128)S(1)}, u32[]{:S(2)}, u32[]{:S(2)}) collective-permute-start(f32[488,128]{1,0:T(8,128)S(1)} %collective-permute-done.4.refs_9_), channel_id=1, source_target_pairs={{0,4},{4,0},{1,5},{5,1},{2,6},{6,2},{3,7},{7,3},{8,12},{12,8},{9,1... | collective-permute-start | bytes 749576 | tf_op jit(solution)/shard_map/ppermute | solution.py:438
  106.0 3.5 %copy-start.15 = (f32[12,80,128]{2,1,0:T(8,128)}, f32[12,80,128]{2,1,0:T(8,128)S(1)}, u32[]{:S(2)}) copy-start(f32[12,80,128]{2,1,0:T(8,128)S(1)} %collective-permute-done.11.refs_17_) | copy-start | bytes 1474564
  106.0 3.4 %collective-permute-start.8 = (f32[480,128]{1,0:T(8,128)S(1)}, f32[480,128]{1,0:T(8,128)S(1)}, u32[]{:S(2)}, u32[]{:S(2)}) collective-permute-start(f32[480,128]{1,0:T(8,128)S(1)} %collective-permute-done.3.refs_8_), channel_id=1, source_target_pairs={{0,4},{4,0},{1,5},{5,1},{2,6},{6,2},{3,7},{7,3},{8,12},{12,8},{9,1... | collective-permute-start | bytes 737288 | tf_op jit(solution)/shard_map/ppermute | solution.py:438
  109.4 0.7 copy-start.19
  109.4 0.8 copy-start.17
  109.4 0.9 copy-start.11
  109.5 1.1 copy-start.12
  109.5 1.2 copy-start.13
